TPU v7x, 512 devices: a whole 4x4x16 slice. The times are simulated.
512 devices in a mesh: frame: 16 (over z), chan: 32 (over x, y, core).
Axes of the slice: x: 4, y: 4, z: 16, core: 2. Of those that a mesh axis runs over, the one named last changes fastest.
Arguments:
- features: bfloat16 [38912, 3072], P('frame', 'chan'), may hold values from -6 to 6
- w_value: bfloat16 [3072, 2048], P(None, 'chan'), may hold values from -0.109375 to 0.109375
- w_out: bfloat16 [2048, 3072], P(None, 'chan'), may hold values from -0.125 to 0.125
- maps: bfloat16 [16, 16, 4, 128, 128], P(None, 'frame'), may hold values from 0.0009994507 to 0.099609375
- lists: int32 [16, 16, 4], replicated, may hold values from 0 to 303, as said below
Outputs:
- mixed: bfloat16 [2048, 3072], P('frame', 'chan')
Inputs may be any that keep to these rules, and one draw needn't show every extreme that they name: `lists`: the 4 blocks of one list lie on 4 different indices of frame: their numbers integer-divided by 19 differ.
All inputs are finite; a program needn't handle non-finite values.
Results may differ from a plain program's by a relative error of at most 0.0057.
Values may be sent and summed in bfloat16 or wider, within the bound.
No kernel may reach another device: no remote copies, remote signals or barrier semaphores. Data moves between devices by JAX's collectives and lax.ppermute only.
A program may use at most 64 MiB of HBM per device.

v0:
```python
import jax
import jax.numpy as jnp
from jax import lax
from jax.sharding import PartitionSpec as P

HEADS = 16
HEAD_DIM = 128
BLK = 128


def body(features, w_value, w_out, maps, lists):
    width = w_value.shape[1]
    kv_rows = features.shape[0]
    values = jnp.dot(
        lax.all_gather(features, "chan", axis=1, tiled=True),
        w_value,
        preferred_element_type=jnp.float32,
    ).astype(jnp.bfloat16)
    chan_pos = lax.axis_index("chan")
    frame_pos = lax.axis_index("frame")
    frames = lax.axis_size("frame")
    blocks_dev = kv_rows // BLK
    span = max(1, width // HEAD_DIM)
    head_first = chan_pos * width // HEAD_DIM
    head_ids = head_first + jnp.arange(span, dtype=jnp.int32)
    head_safe = jnp.minimum(head_ids, HEADS - 1)
    chan_heads = (chan_pos * width + jnp.arange(width, dtype=jnp.int32)) // HEAD_DIM
    chan_mask = (chan_heads[None, :] == head_ids[:, None]).astype(jnp.float32)
    my_lists = jnp.take(lists, head_safe, axis=0)
    local_hit = my_lists // blocks_dev == frame_pos
    local_index = jnp.sum(jnp.where(local_hit, my_lists - frame_pos * blocks_dev, 0), axis=2)
    present = jnp.any(local_hit, axis=2)
    value_blocks = values.reshape(blocks_dev, BLK, width)
    outgoing = jnp.take(value_blocks, local_index, axis=0)
    outgoing = jnp.where(present[:, :, None, None], outgoing, jnp.zeros((), jnp.bfloat16))
    incoming = lax.all_to_all(
        outgoing[:, :, None], "frame", split_axis=1, concat_axis=2, tiled=True
    )
    query_blocks = maps.shape[1]
    mine = lax.dynamic_slice_in_dim(my_lists, frame_pos * query_blocks, query_blocks, 1)
    source = mine // blocks_dev
    picker = (source[..., None] == jnp.arange(frames, dtype=jnp.int32)).astype(jnp.bfloat16)
    chosen = jnp.einsum(
        "tqsf,tqfjc->tqsjc", picker, incoming, preferred_element_type=jnp.float32
    ).astype(jnp.bfloat16)
    map_heads = jnp.take(maps, head_safe, axis=0)
    partial_value = jnp.einsum(
        "tqsij,tqsjc->tqic", map_heads, chosen, preferred_element_type=jnp.float32
    )
    attn = jnp.sum(partial_value * chan_mask[:, None, None, :], axis=0).astype(jnp.bfloat16)
    attn = attn.reshape(query_blocks * BLK, width)
    mixed = jnp.dot(
        lax.all_gather(attn, "chan", axis=1, tiled=True), w_out, preferred_element_type=jnp.float32
    )
    return mixed.astype(jnp.bfloat16)


def solution(mesh):
    in_specs = (
        P("frame", "chan"),
        P(None, "chan"),
        P(None, "chan"),
        P(None, "frame", None, None, None),
        P(),
    )
    out_specs = P("frame", "chan")
    return jax.shard_map(body, mesh=mesh, in_specs=in_specs, out_specs=out_specs, check_vma=False)
```

profile of v0, /device:TPU:1, one launch (start us, length us, event | category | flops | bytes accessed | tf_op | source)
XLA Modules:
  0.0 173.8 jit_solution(13110492918595674894)
XLA Ops:
  6.5 0.0 copy-start
  6.5 0.0 copy-start.1
  6.5 0.0 all-gather.2.cloned.1.call-start
  6.5 0.7 all-gather.2.cloned.1.call-update
  7.3 0.7 fusion.21
  8.1 91.9 %all-gather.2.cloned.1.call-done = bf16[2432,3072]{0,1:T(8,128)(2,1)} async-done(((bf16[2432,96]{0,1:T(8,128)(2,1)}), bf16[2432,3072]{0,1:T(8,128)(2,1)}) %all-gather.2.cloned.1.call-update) | async-done | bytes 14942224 | tf_op jit(solution)/shard_map/all_gather | solution.py:15
  100.0 0.0 copy-done
  100.0 7.8 %fusion = bf16[8,19,8,128]{3,2,1,0:T(8,128)(2,1)S(1)} fusion(bf16[3072,64]{0,1:T(8,128)(2,1)S(1)} %copy-done, bf16[2432,3072]{0,1:T(8,128)(2,1)} %all-gather.2.cloned.1.call-done), kind=kOutput, calls=%fused_computation.2 | convolution fusion | flops 956456960 | bytes 15646720 | tf_op jit(solution)/shard_map/dot_general | solution.py:14
  107.8 0.1 copy.19
  107.9 0.6 gather_fusion
  108.5 0.8 fusion.5
  109.3 12.0 %all-to-all-start = ((bf16[1,16,1,128,64]{3,4,2,0,1:T(8,128)(2,1)}), bf16[1,16,1,128,64]{3,4,2,0,1:T(8,128)(2,1)S(1)}, u32[]{:S(2)}, u32[]{:S(2)}) async-start(bf16[1,16,1,128,64]{3,4,2,0,1:T(8,128)(2,1)} %fusion.5), calls=%async_computation | async-start | bytes 524288 | tf_op jit(solution)/shard_map/all_to_all | solution.py:36
  121.3 0.2 fusion.11
  121.5 13.9 %all-to-all-done = bf16[1,16,1,128,64]{3,4,2,0,1:T(8,128)(2,1)S(1)} async-done(((bf16[1,16,1,128,64]{3,4,2,0,1:T(8,128)(2,1)}), bf16[1,16,1,128,64]{3,4,2,0,1:T(8,128)(2,1)S(1)}, u32[]{:S(2)}, u32[]{:S(2)}) %all-to-all-start) | async-done | bytes 262176 | tf_op jit(solution)/shard_map/all_to_all | solution.py:36
  135.5 0.3 convolution_convert_fusion.1
  135.7 1.1 fusion.2
  136.8 29.3 %all_gather.7 = bf16[128,2048]{0,1:T(8,128)(2,1)S(1)} all-gather(bf16[128,64]{0,1:T(8,128)(2,1)S(1)} %fusion.2), channel_id=1, replica_groups=mesh['frame'=16,'chan'=32] {'chan'}, dimensions={1}, use_global_device_ids=true | all-gather | bytes 540672 | tf_op jit(solution)/shard_map/all_gather | solution.py:53
  166.1 0.0 copy-done.1
  166.1 0.9 convolution_convert_fusion.2
  (5 shorter events, 0.1 us)
Async XLA Ops:
  6.5 93.4 %copy-start = (bf16[3072,64]{0,1:T(8,128)(2,1)S(1)}, bf16[3072,64]{0,1:T(8,128)(2,1)}, u32[]{:S(2)}) copy-start(bf16[3072,64]{0,1:T(8,128)(2,1)} %param.6) | copy-start | bytes 1179652
  6.5 159.6 %copy-start.1 = (bf16[2048,96]{0,1:T(8,128)(2,1)S(1)}, bf16[2048,96]{0,1:T(8,128)(2,1)}, u32[]{:S(2)}) copy-start(bf16[2048,96]{0,1:T(8,128)(2,1)} %param.7) | copy-start | bytes 1179652
  6.5 93.4 %all-gather.2.cloned.1.call-start = ((), (), s32[]{:S(2)}) async-start(), calls=%async_computation.1 | async-start | bytes 15409152 | tf_op jit(solution)/shard_map/all_gather | solution.py:15
  109.3 26.1 %all-to-all-start = ((bf16[1,16,1,128,64]{3,4,2,0,1:T(8,128)(2,1)}), bf16[1,16,1,128,64]{3,4,2,0,1:T(8,128)(2,1)S(1)}, u32[]{:S(2)}, u32[]{:S(2)}) async-start(bf16[1,16,1,128,64]{3,4,2,0,1:T(8,128)(2,1)} %fusion.5), calls=%async_computation | async-start | bytes 524288 | tf_op jit(solution)/shard_map/all_to_all | solution.py:36
Sparse Core Ops, SparseCore 0:
  10.5 89.4 all-gather.1
where the time goes:
time: 174 us
  waiting for transfers between devices  107 us (61%)
  blocking collectives  29.3 us (17%)
  between operations  13.5 us (8%)
  starting transfers between devices  12 us (7%)
  matrix products  10.1 us (6%)
  other arithmetic  1.77 us (1%)
    all_gather x1, waiting for transfers between devices, body(): lax.all_gather(features, 'chan', axis=1, tiled=True)  91.9 us
    all_gather x1, blocking collectives, body(): lax.all_gather(attn, 'chan', axis=1, tiled=True)  29.3 us
    all_to_all x1, waiting for transfers between devices, body(): lax.all_to_all(outgoing[:, :, None], 'frame', split_axis=1, concat_axis=2...  13.9 us
    all_to_all x1, starting transfers between devices, body(): lax.all_to_all(outgoing[:, :, None], 'frame', split_axis=1, concat_axis=2...  12 us
    dot_general x1, matrix products, body(): jnp.dot(lax.all_gather(features, 'chan', axis=1, tiled=True), w_value, pr...  7.84 us
  transfers between devices with their start and end apart: 2, of which 2 were waited for; matrix products, arithmetic and copies ran while one was open for 1% of the time, Pallas kernels for 0%

commit v1 on v0

v1 whole, which is shorter than its diff:
```python
import jax
import jax.numpy as jnp
from jax import lax
from jax.experimental import pallas as pl
from jax.experimental.pallas import tpu as pltpu
from jax.sharding import Mesh, PartitionSpec as P

BLK = 128
NX = 4
NY = 4
BF = jnp.bfloat16
F32 = jnp.float32


def shift(n, k):
    return [(i, (i + k) % n) for i in range(n)]


def project(idx, pos, w0, w1, w2, w3, *rest):
    chunks, out, gath, wall = rest[:8], rest[8], rest[9], rest[10]
    rows = chunks[0].shape[0]
    width = w0.shape[0]
    for i, chunk in enumerate(chunks):
        at = pl.multiple_of(pos[i] * rows, rows)
        gath[pl.ds(at, rows), :] = chunk[...]
    for i, w in enumerate((w0, w1, w2, w3)):
        at = pl.multiple_of(pos[8 + i] * width, width)
        wall[pl.ds(at, width), :] = w[...]
    queries = out.shape[1]
    vals = jnp.dot(wall[...], gath[...], preferred_element_type=F32).astype(BF)
    rest[11][...] = vals
    for x in range(NX):
        for q in range(queries):
            at = pl.multiple_of(idx[x, q] * BLK, BLK)
            out[x, q] = rest[11][x * width : (x + 1) * width, pl.ds(at, BLK)]


def attend(src, got, maps, out):
    acc = jnp.zeros(out.shape[1:], F32)
    for s in range(maps.shape[0]):
        acc += lax.dot_general(
            got[src[s]], maps[s], (((1,), (1,)), ((), ())), preferred_element_type=F32
        )
    acc = acc.astype(BF)
    for k in range(out.shape[0]):
        out[k] = acc


def vmem(n):
    return [pl.BlockSpec(memory_space=pltpu.VMEM)] * n


def smem(n):
    return [pl.BlockSpec(memory_space=pltpu.SMEM)] * n


def body(features, w_value, w_out, maps, lists):
    kv_rows, feat = features.shape
    width = w_value.shape[1]
    x, y, core = (lax.axis_index(a) for a in ("x", "y", "core"))
    frame = lax.axis_index("frame")
    frames = lax.axis_size("frame")
    blocks_dev = kv_rows // BLK
    head = x * NY + y

    ft = features.T
    wt = w_value.T
    far = [lax.ppermute(ft, "y", shift(NY, k)) for k in (1, 3, 2)]
    wx = wt.reshape(width, NX, NY * 2 * feat)

    def w_to(k):
        return lax.dynamic_index_in_dim(wx, lax.rem(x + k, NX), 1, keepdims=False)

    wfar = [lax.ppermute(w_to(k), "x", shift(NX, k)) for k in (1, 3, 2)]
    mine = [ft] + far
    other = [lax.ppermute(c, "core", shift(2, 1)) for c in mine]
    ys = [y] + [lax.rem(y + NY - k, NY) for k in (1, 3, 2)]
    xs = [x] + [lax.rem(x + NX - k, NX) for k in (1, 3, 2)]
    pos = [2 * v + core for v in ys] + [2 * v + 1 - core for v in ys] + xs
    pos = jnp.stack(pos).astype(jnp.int32)

    here = lax.dynamic_index_in_dim(lists.reshape((NX, NY) + lists.shape[1:]), y, 1, keepdims=False)
    hit = here // blocks_dev == frame
    idx = jnp.sum(jnp.where(hit, here - frame * blocks_dev, 0), axis=2).astype(jnp.int32)
    queries = idx.shape[1]

    part = pl.pallas_call(
        project,
        out_shape=jax.ShapeDtypeStruct((NX, queries, width, BLK), BF),
        in_specs=smem(2) + vmem(12),
        out_specs=pl.BlockSpec(memory_space=pltpu.VMEM),
        scratch_shapes=[
            pltpu.VMEM((NY * 2 * feat, kv_rows), BF),
            pltpu.VMEM((NX * width, NY * 2 * feat), BF),
            pltpu.VMEM((NX * width, kv_rows), BF),
        ],
        compiler_params=pltpu.CompilerParams(vmem_limit_bytes=48 * 2**20),
        name="project",
    )(idx, pos, w_to(0), *wfar, *mine, *other)

    part = lax.all_to_all(part, "x", 0, 0, tiled=True)
    blocks = jnp.sum(part.astype(F32), axis=0).astype(BF)
    got = lax.all_to_all(blocks, "frame", 0, 0, tiled=True)

    my_list = lax.dynamic_slice(lists, (head, frame, 0), (1, 1, lists.shape[2])).reshape(-1)
    my_maps = lax.dynamic_index_in_dim(maps[:, 0], head, 0, keepdims=False)
    attn = pl.pallas_call(
        attend,
        out_shape=jax.ShapeDtypeStruct((NX * NY, width, BLK), BF),
        in_specs=smem(1) + vmem(2),
        out_specs=pl.BlockSpec(memory_space=pltpu.VMEM),
        name="attend",
    )((my_list // blocks_dev).astype(jnp.int32), got, my_maps)
    attn = lax.all_to_all(attn, ("x", "y"), 0, 0, tiled=True)
    attn = lax.all_gather(attn.reshape(NX * NY * width, BLK), "core", axis=0, tiled=True)
    wo = w_out.T.reshape(w_out.shape[1], NX * NY, 2, width).transpose(0, 2, 1, 3)
    mixed = jnp.dot(wo.reshape(w_out.shape[1], -1), attn, preferred_element_type=F32)
    return mixed.astype(BF).T


def solution(mesh):
    chan = ("x", "y", "core")
    grid = Mesh(mesh.devices.reshape(-1, NX, NY, 2), ("frame",) + chan)
    in_specs = (
        P("frame", chan),
        P(None, chan),
        P(None, chan),
        P(None, "frame", None, None, None),
        P(),
    )
    return jax.shard_map(body, mesh=grid, in_specs=in_specs, out_specs=P("frame", chan), check_vma=False)
```

time: 174 us -> 137 us (0.79)
  waiting for transfers between devices: 107 us -> 28 us
  starting transfers between devices: 12 us -> 58.5 us
  between operations: 13.5 us -> 0.26 us
  local copies, waits for them, and re-layouts: 0.68 us -> 13.2 us
  matrix products: 10.1 us -> 0.94 us
  Pallas kernels: 0 us -> 5.21 us
  blocking collectives: 29.3 us -> 26.5 us
  other arithmetic: 1.77 us -> 3.94 us
    all_gather x1 -> x0, waiting for transfers between devices: 91.9 us -> none  [body(): lax.all_gather(features, 'chan', axis=1, tiled=True)]
    ppermute x0 -> x10, starting transfers between devices: none -> 40.9 us  [the longest x4 24 us: body(): other = [lax.ppermute(c, 'core', shift(2, 1)) for c in mine]]
    all_gather x1, blocking collectives: 29.3 us -> 11.8 us  [body(): lax.all_gather(attn.reshape(NX * NY * width, BLK), 'core', axis=0, tiled=...]
    all_to_all x0 -> x1, blocking collectives: none -> 14.7 us  [body(): part = lax.all_to_all(part, 'x', 0, 0, tiled=True)]
    ppermute x0 -> x10, waiting for transfers between devices: none -> 11.2 us  [the longest x3 11.2 us: body(): wfar = [lax.ppermute(w_to(k), 'x', shift(NX, k)) for k in (1, 3, 2)]]
    dot_general x4 -> x1, matrix products: 10.1 us -> 0.94 us  [body(): jnp.dot(wo.reshape(w_out.shape[1], -1), attn, preferred_element_type=F32)]
    unnamed x4 -> x23, local copies, waits for them, and re-layouts: 0.01 us -> 7.17 us
    all_to_all x1 -> x2, starting transfers between devices: 12 us -> 17.6 us  [the longest x1 10.9 us: body(): got = lax.all_to_all(blocks, 'frame', 0, 0, tiled=True)]
  transfers between devices with their start and end apart: 2 -> 12, of which waited for: 2 -> 5; matrix products, arithmetic and copies ran while one was open for 1% -> 8% of each run, Pallas kernels for 0% -> 0%
where the time goes in v1:
time: 137 us
  starting transfers between devices  58.5 us (43%)
  waiting for transfers between devices  28 us (20%)
  blocking collectives  26.5 us (19%)
  local copies, waits for them, and re-layouts  13.2 us (10%)
  Pallas kernels  5.21 us (4%)
  other arithmetic  3.94 us (3%)
    ppermute x4, starting transfers between devices, body(): other = [lax.ppermute(c, 'core', shift(2, 1)) for c in mine]  24 us
    all_to_all x1, blocking collectives, body(): part = lax.all_to_all(part, 'x', 0, 0, tiled=True)  14.7 us
    all_gather x1, blocking collectives, body(): lax.all_gather(attn.reshape(NX * NY * width, BLK), 'core', axis=0, tiled=...  11.8 us
    ppermute x3, waiting for transfers between devices, body(): wfar = [lax.ppermute(w_to(k), 'x', shift(NX, k)) for k in (1, 3, 2)]  11.2 us
    ppermute x3, starting transfers between devices, body(): far = [lax.ppermute(ft, 'y', shift(NY, k)) for k in (1, 3, 2)]  11.2 us
    all_to_all x1, starting transfers between devices, body(): got = lax.all_to_all(blocks, 'frame', 0, 0, tiled=True)  10.9 us
    all_to_all x1, waiting for transfers between devices, body(): got = lax.all_to_all(blocks, 'frame', 0, 0, tiled=True)  9.82 us
    unnamed x23, local copies, waits for them, and re-layouts  7.17 us
  transfers between devices with their start and end apart: 12, of which 5 were waited for; matrix products, arithmetic and copies ran while one was open for 8% of the time, Pallas kernels for 0%

profile of v1, /device:TPU:1, one launch (start us, length us, event | category | flops | bytes accessed | tf_op | source)
XLA Modules:
  0.0 136.5 jit_solution(14852975931272075518)
XLA Ops:
  0.0 0.0 copy-start
  0.0 0.0 copy-start.1
  0.0 4.3 %collective-permute-start.3 = (bf16[96,2432]{1,0:T(8,128)(2,1)}, bf16[96,2432]{1,0:T(8,128)(2,1)S(1)}, u32[]{:S(2)}, u32[]{:S(2)}) collective-permute-start(bf16[96,2432]{1,0:T(8,128)(2,1)} %bitcast.68), channel_id=1, source_target_pairs={{0,2},{2,4},{4,6},{6,0},{1,3},{3,5},{5,7},{7,1},{8,10},{10,12},{12... | collective-permute-start | bytes 1400840 | tf_op jit(solution)/shard_map/ppermute | solution.py:68
  4.3 3.4 %collective-permute-start.4 = (bf16[96,2432]{1,0:T(8,128)(2,1)}, bf16[96,2432]{1,0:T(8,128)(2,1)S(1)}, u32[]{:S(2)}, u32[]{:S(2)}) collective-permute-start(bf16[96,2432]{1,0:T(8,128)(2,1)} %bitcast.69), channel_id=1, source_target_pairs={{0,6},{2,0},{4,2},{6,4},{1,7},{3,1},{5,3},{7,5},{8,14},{10,8},{12,... | collective-permute-start | bytes 1400840 | tf_op jit(solution)/shard_map/ppermute | solution.py:68
  7.7 3.5 %collective-permute-start.5 = (bf16[96,2432]{1,0:T(8,128)(2,1)}, bf16[96,2432]{1,0:T(8,128)(2,1)}, u32[]{:S(2)}, u32[]{:S(2)}) collective-permute-start(bf16[96,2432]{1,0:T(8,128)(2,1)} %bitcast.70), channel_id=1, source_target_pairs={{0,4},{2,6},{4,0},{6,2},{1,5},{3,7},{5,1},{7,3},{8,12},{10,14},{12... | collective-permute-start | bytes 1400840 | tf_op jit(solution)/shard_map/ppermute | solution.py:68
  11.2 6.8 %collective-permute-start.6 = (bf16[96,2432]{1,0:T(8,128)(2,1)}, bf16[96,2432]{1,0:T(8,128)(2,1)}, u32[]{:S(2)}, u32[]{:S(2)}) collective-permute-start(bf16[96,2432]{1,0:T(8,128)(2,1)} %bitcast.71), channel_id=1, source_target_pairs={{0,1},{1,0},{2,3},{3,2},{4,5},{5,4},{6,7},{7,6},{8,9},{9,8},{10,11... | collective-permute-start | bytes 1400840 | tf_op jit(solution)/shard_map/ppermute | solution.py:76
  18.0 0.0 collective-permute-done.3.rest_1_
  18.1 12.9 %collective-permute-start.7 = (bf16[96,2432]{1,0:T(8,128)(2,1)S(1)}, bf16[96,2432]{1,0:T(8,128)(2,1)}, u32[]{:S(2)}, u32[]{:S(2)}) collective-permute-start(bf16[96,2432]{1,0:T(8,128)(2,1)S(1)} %collective-permute-done.3.rest_1_), channel_id=1, source_target_pairs={{0,1},{1,0},{2,3},{3,2},{4,5},{5,4},{6,7},{7,6},{8,9},{9,8},{10,11... | collective-permute-start | bytes 1400840 | tf_op jit(solution)/shard_map/ppermute | solution.py:76
  30.9 0.0 collective-permute-done.4.rest_2_
  30.9 1.9 %collective-permute-start.8 = (bf16[96,2432]{1,0:T(8,128)(2,1)S(1)}, bf16[96,2432]{1,0:T(8,128)(2,1)}, u32[]{:S(2)}, u32[]{:S(2)}) collective-permute-start(bf16[96,2432]{1,0:T(8,128)(2,1)S(1)} %collective-permute-done.4.rest_2_), channel_id=1, source_target_pairs={{0,1},{1,0},{2,3},{3,2},{4,5},{5,4},{6,7},{7,6},{8,9},{9,8},{10,11... | collective-permute-start | bytes 1400840 | tf_op jit(solution)/shard_map/ppermute | solution.py:76
  32.9 0.0 collective-permute-done.5.rest_3_
  32.9 2.4 %collective-permute-start.9 = (bf16[96,2432]{1,0:T(8,128)(2,1)}, bf16[96,2432]{1,0:T(8,128)(2,1)}, u32[]{:S(2)}, u32[]{:S(2)}) collective-permute-start(bf16[96,2432]{1,0:T(8,128)(2,1)} %collective-permute-done.5.rest_3_), channel_id=1, source_target_pairs={{0,1},{1,0},{2,3},{3,2},{4,5},{5,4},{6,7},{7,6},{8,9},{9,8},{10,11... | collective-permute-start | bytes 1400840 | tf_op jit(solution)/shard_map/ppermute | solution.py:76
  35.3 2.0 %reshape.41 = bf16[64,4,768]{2,1,0:T(4,128)(2,1)} reshape(bf16[64,3072]{1,0:T(8,128)(2,1)} %bitcast.77) | data formatting | bytes 786432 | tf_op jit(solution)/shard_map/reshape | solution.py:69
  37.4 3.2 %constant_dynamic-slice_fusion.3 = (bf16[64,1,768]{2,1,0:T(2,128)(2,1)S(1)}, bf16[64,1,768]{2,1,0:T(2,128)(2,1)S(1)}, bf16[64,1,768]{2,1,0:T(2,128)(2,1)S(1)}, bf16[64,1,768]{2,1,0:T(2,128)(2,1)}) fusion(bf16[64,4,768]{2,1,0:T(4,128)(2,1)} %reshape.41, s32[]{:T(128)S(6)} %select_n.48, s32[]{:T(128)S(6)} %select_n.47, s32[]{:T(128)S(6)} %select_n.46, ...), kind=kLoop, calls=%fused_computation.24 | loop fusion | bytes 786448 | tf_op jit(solution)/shard_map/jit(dynamic_index_in_dim)/dynamic_slice | solution.py:72
  40.5 1.9 %collective-permute-start = (bf16[64,768]{1,0:T(8,128)(2,1)S(1)}, bf16[64,768]{1,0:T(8,128)(2,1)S(1)}, u32[]{:S(2)}, u32[]{:S(2)}) collective-permute-start(bf16[64,768]{1,0:T(8,128)(2,1)S(1)} %bitcast.79), channel_id=1, source_target_pairs={{0,8},{8,16},{16,24},{24,0},{1,9},{9,17},{17,25},{25,1},{2,10},{10... | collective-permute-start | bytes 294920 | tf_op jit(solution)/shard_map/ppermute | solution.py:74
  42.5 5.6 %collective-permute-done.w1 = bf16[64,768]{1,0:T(8,128)(2,1)S(1)} collective-permute-done((bf16[64,768]{1,0:T(8,128)(2,1)S(1)}, bf16[64,768]{1,0:T(8,128)(2,1)S(1)}, u32[]{:S(2)}, u32[]{:S(2)}) %collective-permute-start) | collective-permute-done | bytes 98336 | tf_op jit(solution)/shard_map/ppermute | solution.py:74
  48.1 0.0 copy-start.3
  48.1 0.6 copy-done.3
  48.7 1.9 %collective-permute-start.1 = (bf16[64,768]{1,0:T(8,128)(2,1)S(1)}, bf16[64,768]{1,0:T(8,128)(2,1)S(1)}, u32[]{:S(2)}, u32[]{:S(2)}) collective-permute-start(bf16[64,768]{1,0:T(8,128)(2,1)S(1)} %bitcast.78), channel_id=1, source_target_pairs={{0,24},{8,0},{16,8},{24,16},{1,25},{9,1},{17,9},{25,17},{2,26},{10... | collective-permute-start | bytes 294920 | tf_op jit(solution)/shard_map/ppermute | solution.py:74
  50.6 0.6 copy.30
  51.3 2.8 %collective-permute-done.1.w2 = bf16[64,768]{1,0:T(8,128)(2,1)S(1)} collective-permute-done((bf16[64,768]{1,0:T(8,128)(2,1)S(1)}, bf16[64,768]{1,0:T(8,128)(2,1)S(1)}, u32[]{:S(2)}, u32[]{:S(2)}) %collective-permute-start.1) | collective-permute-done | bytes 98336 | tf_op jit(solution)/shard_map/ppermute | solution.py:74
  54.1 0.0 copy-start.5
  54.1 0.6 copy-done.5
  54.7 1.9 %collective-permute-start.2 = (bf16[64,768]{1,0:T(8,128)(2,1)}, bf16[64,768]{1,0:T(8,128)(2,1)}, u32[]{:S(2)}, u32[]{:S(2)}) collective-permute-start(bf16[64,768]{1,0:T(8,128)(2,1)} %bitcast.64), channel_id=1, source_target_pairs={{0,16},{8,24},{16,0},{24,8},{1,17},{9,25},{17,1},{25,9},{2,18},{10... | collective-permute-start | bytes 294920 | tf_op jit(solution)/shard_map/ppermute | solution.py:74
  56.6 1.6 %copy.33 = bf16[64,1,768]{2,0,1:T(8,128)(2,1)} copy(bf16[64,1,768]{2,1,0:T(2,128)(2,1)} %get-tuple-element.8) | data formatting | bytes 196608
  58.2 0.1 stack.51.pos
  58.3 0.7 fusion.1.idx
  59.0 2.8 %collective-permute-done.2.w3 = bf16[64,768]{1,0:T(8,128)(2,1)} collective-permute-done((bf16[64,768]{1,0:T(8,128)(2,1)}, bf16[64,768]{1,0:T(8,128)(2,1)}, u32[]{:S(2)}, u32[]{:S(2)}) %collective-permute-start.2) | collective-permute-done | bytes 98336 | tf_op jit(solution)/shard_map/ppermute | solution.py:74
  61.9 0.0 collective-permute-done.6.rest_4_
  61.9 0.0 collective-permute-done.7.rest_5_
  61.9 0.0 collective-permute-done.8.rest_6_
  61.9 0.0 collective-permute-done.9.rest_7_
  61.9 0.0 copy-done.1
  61.9 0.0 copy-start.2
  61.9 0.9 copy-done.2
  62.8 0.0 copy-start.4
  62.8 0.9 copy-done.4
  63.7 0.0 copy-start.6
  63.7 0.9 copy-done.6
  64.6 3.3 %project.1 = bf16[4,16,64,128]{3,2,1,0:T(8,128)(2,1)S(1)} custom-call(s32[4,16]{1,0:T(4,128)S(1)} %fusion.1.idx, s32[12]{0:T(128)S(1)} %stack.51.pos, bf16[64,768]{1,0:T(8,128)(2,1)S(1)} %bitcast.73, bf16[64,768]{1,0:T(8,128)(2,1)S(1)} %copy-done.4, bf16[64,768]{1,0:T(8,128)(2,1)S(1)} %copy-done.6, bf16[64,768]{1,0:T(8,128)(2,1)} %collective-permute-done.2.w3, ...), custom_call_target="tpu_custom_call" | custom-call | tf_op jit(solution)/shard_map/project/pallas_call | solution.py:87
  67.9 14.7 %all_to_all.15 = bf16[4,16,64,128]{3,2,1,0:T(8,128)(2,1)S(1)} all-to-all(bf16[4,16,64,128]{3,2,1,0:T(8,128)(2,1)S(1)} %project.1), channel_id=1, replica_groups=mesh['frame'=16,'x'=4,'y'=4,'core'=2] {'x'}, dimensions={0} | all-to-all | bytes 2097152 | tf_op jit(solution)/shard_map/all_to_all | solution.py:101
  82.5 0.9 reduce_sum.22
  83.5 0.0 copy-start.8
  83.5 10.9 %all-to-all-start.1 = ((bf16[16,64,128]{2,1,0:T(8,128)(2,1)}), bf16[16,64,128]{2,1,0:T(8,128)(2,1)S(1)}, u32[]{:S(2)}, u32[]{:S(2)}) async-start(bf16[16,64,128]{2,1,0:T(8,128)(2,1)} %reduce_sum.22), calls=%async_computation.1 | async-start | bytes 524288 | tf_op jit(solution)/shard_map/all_to_all | solution.py:103
  94.3 0.9 fusion.6
  95.2 0.9 divide_reduce_fusion
  96.1 0.0 copy-done
  96.1 0.7 dynamic-slice_bitcast_fusion.maps
  96.8 0.5 add_select_fusion.1.src
  97.3 9.8 %all-to-all-done.1.got = bf16[16,64,128]{2,1,0:T(8,128)(2,1)S(1)} async-done(((bf16[16,64,128]{2,1,0:T(8,128)(2,1)}), bf16[16,64,128]{2,1,0:T(8,128)(2,1)S(1)}, u32[]{:S(2)}, u32[]{:S(2)}) %all-to-all-start.1) | async-done | bytes 262176 | tf_op jit(solution)/shard_map/all_to_all | solution.py:103
  107.1 0.0 copy-start.7
  107.1 0.7 copy-done.7
  107.8 1.9 %attend.1 = bf16[16,64,128]{2,1,0:T(8,128)(2,1)} custom-call(s32[4]{0:T(128)} %add_select_fusion.1.src, bf16[16,64,128]{2,1,0:T(8,128)(2,1)} %copy-done.7, bf16[4,128,128]{2,1,0:T(8,128)(2,1)} %dynamic-slice_bitcast_fusion.maps), custom_call_target="tpu_custom_call" | custom-call | tf_op jit(solution)/shard_map/attend/pallas_call | solution.py:107
  109.7 6.7 %all-to-all-start.2 = ((bf16[16,64,128]{2,1,0:T(8,128)(2,1)}), bf16[16,64,128]{2,1,0:T(8,128)(2,1)S(1)}, u32[]{:S(2)}, u32[]{:S(2)}) async-start(bf16[16,64,128]{2,1,0:T(8,128)(2,1)} %attend.1), calls=%async_computation.2 | async-start | bytes 524288 | tf_op jit(solution)/shard_map/all_to_all | solution.py:114
  116.5 0.0 copy-done.8
  116.5 0.3 copy.20
  116.8 7.0 %all-to-all-done.2 = bf16[16,64,128]{2,1,0:T(8,128)(2,1)S(1)} async-done(((bf16[16,64,128]{2,1,0:T(8,128)(2,1)}), bf16[16,64,128]{2,1,0:T(8,128)(2,1)S(1)}, u32[]{:S(2)}, u32[]{:S(2)}) %all-to-all-start.2) | async-done | bytes 262176 | tf_op jit(solution)/shard_map/all_to_all | solution.py:114
  123.8 11.8 %all_gather.3 = bf16[2048,128]{1,0:T(8,128)(2,1)S(1)} all-gather(bf16[1024,128]{1,0:T(8,128)(2,1)S(1)} %bitcast.76), channel_id=1, replica_groups=mesh['frame'=16,'x'=4,'y'=4,'core'=2] {'core'}, dimensions={0}, use_global_device_ids=true | all-gather | bytes 786432 | tf_op jit(solution)/shard_map/all_gather | solution.py:115
  135.6 0.9 convolution_convert_fusion
  (3 shorter events, 0.1 us)
Async XLA Ops:
  0.0 96.1 %copy-start = (bf16[16,1,4,128,128]{4,3,2,1,0:T(8,128)(2,1)S(1)}, bf16[16,1,4,128,128]{4,3,2,1,0:T(8,128)(2,1)}, u32[]{:S(2)}) copy-start(bf16[16,1,4,128,128]{4,3,2,1,0:T(8,128)(2,1)} %param.8) | copy-start | bytes 6291460
  0.0 61.9 %copy-start.1 = (bf16[2432,96]{0,1:T(8,128)(2,1)S(1)}, bf16[2432,96]{0,1:T(8,128)(2,1)}, u32[]{:S(2)}) copy-start(bf16[2432,96]{0,1:T(8,128)(2,1)} %param.5) | copy-start | bytes 1400836
  0.0 18.0 %collective-permute-start.3 = (bf16[96,2432]{1,0:T(8,128)(2,1)}, bf16[96,2432]{1,0:T(8,128)(2,1)S(1)}, u32[]{:S(2)}, u32[]{:S(2)}) collective-permute-start(bf16[96,2432]{1,0:T(8,128)(2,1)} %bitcast.68), channel_id=1, source_target_pairs={{0,2},{2,4},{4,6},{6,0},{1,3},{3,5},{5,7},{7,1},{8,10},{10,12},{12... | collective-permute-start | bytes 1400840 | tf_op jit(solution)/shard_map/ppermute | solution.py:68
  4.3 26.6 %collective-permute-start.4 = (bf16[96,2432]{1,0:T(8,128)(2,1)}, bf16[96,2432]{1,0:T(8,128)(2,1)S(1)}, u32[]{:S(2)}, u32[]{:S(2)}) collective-permute-start(bf16[96,2432]{1,0:T(8,128)(2,1)} %bitcast.69), channel_id=1, source_target_pairs={{0,6},{2,0},{4,2},{6,4},{1,7},{3,1},{5,3},{7,5},{8,14},{10,8},{12,... | collective-permute-start | bytes 1400840 | tf_op jit(solution)/shard_map/ppermute | solution.py:68
  7.7 25.2 %collective-permute-start.5 = (bf16[96,2432]{1,0:T(8,128)(2,1)}, bf16[96,2432]{1,0:T(8,128)(2,1)}, u32[]{:S(2)}, u32[]{:S(2)}) collective-permute-start(bf16[96,2432]{1,0:T(8,128)(2,1)} %bitcast.70), channel_id=1, source_target_pairs={{0,4},{2,6},{4,0},{6,2},{1,5},{3,7},{5,1},{7,3},{8,12},{10,14},{12... | collective-permute-start | bytes 1400840 | tf_op jit(solution)/shard_map/ppermute | solution.py:68
  11.2 50.7 %collective-permute-start.6 = (bf16[96,2432]{1,0:T(8,128)(2,1)}, bf16[96,2432]{1,0:T(8,128)(2,1)}, u32[]{:S(2)}, u32[]{:S(2)}) collective-permute-start(bf16[96,2432]{1,0:T(8,128)(2,1)} %bitcast.71), channel_id=1, source_target_pairs={{0,1},{1,0},{2,3},{3,2},{4,5},{5,4},{6,7},{7,6},{8,9},{9,8},{10,11... | collective-permute-start | bytes 1400840 | tf_op jit(solution)/shard_map/ppermute | solution.py:76
  18.1 43.8 %collective-permute-start.7 = (bf16[96,2432]{1,0:T(8,128)(2,1)S(1)}, bf16[96,2432]{1,0:T(8,128)(2,1)}, u32[]{:S(2)}, u32[]{:S(2)}) collective-permute-start(bf16[96,2432]{1,0:T(8,128)(2,1)S(1)} %collective-permute-done.3.rest_1_), channel_id=1, source_target_pairs={{0,1},{1,0},{2,3},{3,2},{4,5},{5,4},{6,7},{7,6},{8,9},{9,8},{10,11... | collective-permute-start | bytes 1400840 | tf_op jit(solution)/shard_map/ppermute | solution.py:76
  30.9 30.9 %collective-permute-start.8 = (bf16[96,2432]{1,0:T(8,128)(2,1)S(1)}, bf16[96,2432]{1,0:T(8,128)(2,1)}, u32[]{:S(2)}, u32[]{:S(2)}) collective-permute-start(bf16[96,2432]{1,0:T(8,128)(2,1)S(1)} %collective-permute-done.4.rest_2_), channel_id=1, source_target_pairs={{0,1},{1,0},{2,3},{3,2},{4,5},{5,4},{6,7},{7,6},{8,9},{9,8},{10,11... | collective-permute-start | bytes 1400840 | tf_op jit(solution)/shard_map/ppermute | solution.py:76
  32.9 29.0 %collective-permute-start.9 = (bf16[96,2432]{1,0:T(8,128)(2,1)}, bf16[96,2432]{1,0:T(8,128)(2,1)}, u32[]{:S(2)}, u32[]{:S(2)}) collective-permute-start(bf16[96,2432]{1,0:T(8,128)(2,1)} %collective-permute-done.5.rest_3_), channel_id=1, source_target_pairs={{0,1},{1,0},{2,3},{3,2},{4,5},{5,4},{6,7},{7,6},{8,9},{9,8},{10,11... | collective-permute-start | bytes 1400840 | tf_op jit(solution)/shard_map/ppermute | solution.py:76
  40.5 7.5 %collective-permute-start = (bf16[64,768]{1,0:T(8,128)(2,1)S(1)}, bf16[64,768]{1,0:T(8,128)(2,1)S(1)}, u32[]{:S(2)}, u32[]{:S(2)}) collective-permute-start(bf16[64,768]{1,0:T(8,128)(2,1)S(1)} %bitcast.79), channel_id=1, source_target_pairs={{0,8},{8,16},{16,24},{24,0},{1,9},{9,17},{17,25},{25,1},{2,10},{10... | collective-permute-start | bytes 294920 | tf_op jit(solution)/shard_map/ppermute | solution.py:74
  48.1 0.6 copy-start.3
  48.7 5.3 %collective-permute-start.1 = (bf16[64,768]{1,0:T(8,128)(2,1)S(1)}, bf16[64,768]{1,0:T(8,128)(2,1)S(1)}, u32[]{:S(2)}, u32[]{:S(2)}) collective-permute-start(bf16[64,768]{1,0:T(8,128)(2,1)S(1)} %bitcast.78), channel_id=1, source_target_pairs={{0,24},{8,0},{16,8},{24,16},{1,25},{9,1},{17,9},{25,17},{2,26},{10... | collective-permute-start | bytes 294920 | tf_op jit(solution)/shard_map/ppermute | solution.py:74
  54.1 0.6 copy-start.5
  54.7 7.2 %collective-permute-start.2 = (bf16[64,768]{1,0:T(8,128)(2,1)}, bf16[64,768]{1,0:T(8,128)(2,1)}, u32[]{:S(2)}, u32[]{:S(2)}) collective-permute-start(bf16[64,768]{1,0:T(8,128)(2,1)} %bitcast.64), channel_id=1, source_target_pairs={{0,16},{8,24},{16,0},{24,8},{1,17},{9,25},{17,1},{25,9},{2,18},{10... | collective-permute-start | bytes 294920 | tf_op jit(solution)/shard_map/ppermute | solution.py:74
  61.9 0.9 copy-start.2
  62.8 0.9 copy-start.4
  63.7 0.9 copy-start.6
  83.5 33.0 %copy-start.8 = (bf16[2048,96]{0,1:T(8,128)(2,1)S(1)}, bf16[2048,96]{0,1:T(8,128)(2,1)}, u32[]{:S(2)}) copy-start(bf16[2048,96]{0,1:T(8,128)(2,1)} %param.7) | copy-start | bytes 1179652
  83.5 23.6 %all-to-all-start.1 = ((bf16[16,64,128]{2,1,0:T(8,128)(2,1)}), bf16[16,64,128]{2,1,0:T(8,128)(2,1)S(1)}, u32[]{:S(2)}, u32[]{:S(2)}) async-start(bf16[16,64,128]{2,1,0:T(8,128)(2,1)} %reduce_sum.22), calls=%async_computation.1 | async-start | bytes 524288 | tf_op jit(solution)/shard_map/all_to_all | solution.py:103
  107.1 0.7 copy-start.7
  109.7 14.0 %all-to-all-start.2 = ((bf16[16,64,128]{2,1,0:T(8,128)(2,1)}), bf16[16,64,128]{2,1,0:T(8,128)(2,1)S(1)}, u32[]{:S(2)}, u32[]{:S(2)}) async-start(bf16[16,64,128]{2,1,0:T(8,128)(2,1)} %attend.1), calls=%async_computation.2 | async-start | bytes 524288 | tf_op jit(solution)/shard_map/all_to_all | solution.py:114

commit v2 on v1

--- a/solution.py
+++ b/solution.py
@@ -16,23 +16,20 @@
     return [(i, (i + k) % n) for i in range(n)]
 
 
-def project(idx, pos, w0, w1, w2, w3, *rest):
-    chunks, out, gath, wall = rest[:8], rest[8], rest[9], rest[10]
+def project(idx, pos, wall, *rest):
+    chunks, out, gath, vals = rest[:8], rest[8], rest[9], rest[10]
     rows = chunks[0].shape[0]
-    width = w0.shape[0]
+    width = wall.shape[1]
     for i, chunk in enumerate(chunks):
         at = pl.multiple_of(pos[i] * rows, rows)
         gath[pl.ds(at, rows), :] = chunk[...]
-    for i, w in enumerate((w0, w1, w2, w3)):
-        at = pl.multiple_of(pos[8 + i] * width, width)
-        wall[pl.ds(at, width), :] = w[...]
     queries = out.shape[1]
-    vals = jnp.dot(wall[...], gath[...], preferred_element_type=F32).astype(BF)
-    rest[11][...] = vals
+    w = wall[...].reshape(NX * width, wall.shape[2])
+    vals[...] = jnp.dot(w, gath[...], preferred_element_type=F32).astype(BF)
     for x in range(NX):
         for q in range(queries):
             at = pl.multiple_of(idx[x, q] * BLK, BLK)
-            out[x, q] = rest[11][x * width : (x + 1) * width, pl.ds(at, BLK)]
+            out[x, q] = vals[x * width : (x + 1) * width, pl.ds(at, BLK)]
 
 
 def attend(src, got, maps, out):
@@ -44,6 +41,18 @@
     acc = acc.astype(BF)
     for k in range(out.shape[0]):
         out[k] = acc
+
+
+def gate(x, *after):
+    return pl.pallas_call(
+        lambda *refs: None,
+        out_shape=jax.ShapeDtypeStruct(x.shape, x.dtype),
+        in_specs=[pl.BlockSpec(memory_space=pl.ANY)] * (1 + len(after)),
+        out_specs=pl.BlockSpec(memory_space=pl.ANY),
+        input_output_aliases={0: 0},
+        compiler_params=pltpu.CompilerParams(vmem_limit_bytes=2**20),
+        name="gate",
+    )(x, *after)
 
 
 def vmem(n):
@@ -66,17 +75,13 @@
     ft = features.T
     wt = w_value.T
     far = [lax.ppermute(ft, "y", shift(NY, k)) for k in (1, 3, 2)]
-    wx = wt.reshape(width, NX, NY * 2 * feat)
-
-    def w_to(k):
-        return lax.dynamic_index_in_dim(wx, lax.rem(x + k, NX), 1, keepdims=False)
-
-    wfar = [lax.ppermute(w_to(k), "x", shift(NX, k)) for k in (1, 3, 2)]
+    wall = wt.reshape(width, NX, NY * 2 * feat).transpose(1, 0, 2)
+    wall = lax.all_to_all(wall, "x", 0, 0, tiled=True)
+    far[0] = gate(far[0], wall)
     mine = [ft] + far
     other = [lax.ppermute(c, "core", shift(2, 1)) for c in mine]
     ys = [y] + [lax.rem(y + NY - k, NY) for k in (1, 3, 2)]
-    xs = [x] + [lax.rem(x + NX - k, NX) for k in (1, 3, 2)]
-    pos = [2 * v + core for v in ys] + [2 * v + 1 - core for v in ys] + xs
+    pos = [2 * v + core for v in ys] + [2 * v + 1 - core for v in ys]
     pos = jnp.stack(pos).astype(jnp.int32)
 
     here = lax.dynamic_index_in_dim(lists.reshape((NX, NY) + lists.shape[1:]), y, 1, keepdims=False)
@@ -87,16 +92,15 @@
     part = pl.pallas_call(
         project,
         out_shape=jax.ShapeDtypeStruct((NX, queries, width, BLK), BF),
-        in_specs=smem(2) + vmem(12),
+        in_specs=smem(2) + vmem(9),
         out_specs=pl.BlockSpec(memory_space=pltpu.VMEM),
         scratch_shapes=[
             pltpu.VMEM((NY * 2 * feat, kv_rows), BF),
-            pltpu.VMEM((NX * width, NY * 2 * feat), BF),
             pltpu.VMEM((NX * width, kv_rows), BF),
         ],
-        compiler_params=pltpu.CompilerParams(vmem_limit_bytes=48 * 2**20),
+        compiler_params=pltpu.CompilerParams(vmem_limit_bytes=20 * 2**20),
         name="project",
-    )(idx, pos, w_to(0), *wfar, *mine, *other)
+    )(idx, pos, wall, *mine, *other)
 
     part = lax.all_to_all(part, "x", 0, 0, tiled=True)
     blocks = jnp.sum(part.astype(F32), axis=0).astype(BF)
@@ -109,6 +113,7 @@
         out_shape=jax.ShapeDtypeStruct((NX * NY, width, BLK), BF),
         in_specs=smem(1) + vmem(2),
         out_specs=pl.BlockSpec(memory_space=pltpu.VMEM),
+        compiler_params=pltpu.CompilerParams(vmem_limit_bytes=4 * 2**20),
         name="attend",
     )((my_list // blocks_dev).astype(jnp.int32), got, my_maps)
     attn = lax.all_to_all(attn, ("x", "y"), 0, 0, tiled=True)

time: 137 us -> 112 us (0.82)
  local copies, waits for them, and re-layouts: 13.2 us -> 3.19 us
  waiting for transfers between devices: 28 us -> 18.2 us
  starting transfers between devices: 58.5 us -> 52.5 us
    ppermute x3 -> x0, waiting for transfers between devices: 11.2 us -> none  [body(): wfar = [lax.ppermute(w_to(k), 'x', shift(NX, k)) for k in (1, 3, 2)]]
    ppermute x4, starting transfers between devices: 24 us -> 17.9 us  [body(): other = [lax.ppermute(c, 'core', shift(2, 1)) for c in mine]]
    unnamed x23 -> x5, local copies, waits for them, and re-layouts: 7.17 us -> 1.28 us
    ppermute x3 -> x0, starting transfers between devices: 5.74 us -> none  [body(): wfar = [lax.ppermute(w_to(k), 'x', shift(NX, k)) for k in (1, 3, 2)]]
    all_to_all x0 -> x1, starting transfers between devices: none -> 4.01 us  [body(): wall = lax.all_to_all(wall, 'x', 0, 0, tiled=True)]
    dynamic_slice x1 -> x0, local copies, waits for them, and re-layouts: 3.18 us -> none  [w_to(): return lax.dynamic_index_in_dim(wx, lax.rem(x + k, NX), 1, keepdims=False)]
    all_to_all x1, blocking collectives: 14.7 us -> 17.3 us  [body(): part = lax.all_to_all(part, 'x', 0, 0, tiled=True)]
    all_gather x1, blocking collectives: 11.8 us -> 10.1 us  [body(): lax.all_gather(attn.reshape(NX * NY * width, BLK), 'core', axis=0, tiled=...]
  transfers between devices with their start and end apart: 12 -> 10, of which waited for: 5 -> 4; matrix products, arithmetic and copies ran while one was open for 8% -> 5% of each run, Pallas kernels for 0% -> 0%
where the time goes in v2:
time: 112 us; the launch traced here: 111 us
  starting transfers between devices  52.5 us (47%)
  blocking collectives  27.4 us (24%)
  waiting for transfers between devices  18.2 us (16%)
  Pallas kernels  4.83 us (4%)
  other arithmetic  3.42 us (3%)
  local copies, waits for them, and re-layouts  3.19 us (3%)
    ppermute x4, starting transfers between devices, body(): other = [lax.ppermute(c, 'core', shift(2, 1)) for c in mine]  17.9 us
    all_to_all x1, blocking collectives, body(): part = lax.all_to_all(part, 'x', 0, 0, tiled=True)  17.3 us
    all_to_all x1, starting transfers between devices, body(): got = lax.all_to_all(blocks, 'frame', 0, 0, tiled=True)  12.1 us
    ppermute x3, starting transfers between devices, body(): far = [lax.ppermute(ft, 'y', shift(NY, k)) for k in (1, 3, 2)]  11.2 us
    all_to_all x1, waiting for transfers between devices, body(): got = lax.all_to_all(blocks, 'frame', 0, 0, tiled=True)  11 us
    all_gather x1, blocking collectives, body(): lax.all_gather(attn.reshape(NX * NY * width, BLK), 'core', axis=0, tiled=...  10.1 us
    all_to_all x1, starting transfers between devices, body(): attn = lax.all_to_all(attn, ('x', 'y'), 0, 0, tiled=True)  7.35 us
    all_to_all x1, waiting for transfers between devices, body(): attn = lax.all_to_all(attn, ('x', 'y'), 0, 0, tiled=True)  6 us
  transfers between devices with their start and end apart: 10, of which 4 were waited for; matrix products, arithmetic and copies ran while one was open for 5% of the time, Pallas kernels for 0%

profile of v2, /device:TPU:1, one launch (start us, length us, event | category | flops | bytes accessed | tf_op | source)
XLA Modules:
  0.0 110.7 jit_solution(12349820891568735420)
XLA Ops:
  0.0 0.0 copy-start
  0.0 0.0 copy-start.1
  0.0 4.3 %collective-permute-start = (bf16[96,2432]{1,0:T(8,128)(2,1)}, bf16[96,2432]{1,0:T(8,128)(2,1)S(1)}, u32[]{:S(2)}, u32[]{:S(2)}) collective-permute-start(bf16[96,2432]{1,0:T(8,128)(2,1)} %bitcast.59), channel_id=1, source_target_pairs={{0,2},{2,4},{4,6},{6,0},{1,3},{3,5},{5,7},{7,1},{8,10},{10,12},{12... | collective-permute-start | bytes 1400840 | tf_op jit(solution)/shard_map/ppermute | solution.py:77
  4.3 3.4 %collective-permute-start.1 = (bf16[96,2432]{1,0:T(8,128)(2,1)}, bf16[96,2432]{1,0:T(8,128)(2,1)}, u32[]{:S(2)}, u32[]{:S(2)}) collective-permute-start(bf16[96,2432]{1,0:T(8,128)(2,1)} %bitcast.60), channel_id=1, source_target_pairs={{0,6},{2,0},{4,2},{6,4},{1,7},{3,1},{5,3},{7,5},{8,14},{10,8},{12,... | collective-permute-start | bytes 1400840 | tf_op jit(solution)/shard_map/ppermute | solution.py:77
  7.7 3.5 %collective-permute-start.2 = (bf16[96,2432]{1,0:T(8,128)(2,1)}, bf16[96,2432]{1,0:T(8,128)(2,1)}, u32[]{:S(2)}, u32[]{:S(2)}) collective-permute-start(bf16[96,2432]{1,0:T(8,128)(2,1)} %bitcast.61), channel_id=1, source_target_pairs={{0,4},{2,6},{4,0},{6,2},{1,5},{3,7},{5,1},{7,3},{8,12},{10,14},{12... | collective-permute-start | bytes 1400840 | tf_op jit(solution)/shard_map/ppermute | solution.py:77
  11.2 1.8 %copy.18 = bf16[8,4,8,768]{3,2,0,1:T(8,128)(2,1)} copy(bf16[8,4,8,768]{3,2,1,0:T(8,128)(2,1)} %bitcast.68) | data formatting | bytes 786432 | tf_op jit(solution)/shard_map/reshape | solution.py:78
  13.0 4.0 %all-to-all-start = ((bf16[4,64,768]{2,1,0:T(8,128)(2,1)}), bf16[4,64,768]{2,1,0:T(8,128)(2,1)S(1)}, u32[]{:S(2)}, u32[]{:S(2)}) async-start(bf16[4,64,768]{2,1,0:T(8,128)(2,1)} %bitcast.66), calls=%async_computation | async-start | bytes 786432 | tf_op jit(solution)/shard_map/all_to_all | solution.py:79
  17.0 6.3 %collective-permute-start.3 = (bf16[96,2432]{1,0:T(8,128)(2,1)}, bf16[96,2432]{1,0:T(8,128)(2,1)}, u32[]{:S(2)}, u32[]{:S(2)}) collective-permute-start(bf16[96,2432]{1,0:T(8,128)(2,1)} %bitcast.62), channel_id=1, source_target_pairs={{0,1},{1,0},{2,3},{3,2},{4,5},{5,4},{6,7},{7,6},{8,9},{9,8},{10,11... | collective-permute-start | bytes 1400840 | tf_op jit(solution)/shard_map/ppermute | solution.py:82
  23.3 0.3 all-to-all-done.refs_1_.wall
  23.6 0.0 collective-permute-done.refs_0_
  23.6 7.3 %collective-permute-start.4 = (bf16[96,2432]{1,0:T(8,128)(2,1)S(1)}, bf16[96,2432]{1,0:T(8,128)(2,1)}, u32[]{:S(2)}, u32[]{:S(2)}) collective-permute-start(bf16[96,2432]{1,0:T(8,128)(2,1)S(1)} %gate.1.rest_1_), channel_id=1, source_target_pairs={{0,1},{1,0},{2,3},{3,2},{4,5},{5,4},{6,7},{7,6},{8,9},{9,8},{10,11... | collective-permute-start | bytes 1400840 | tf_op jit(solution)/shard_map/ppermute | solution.py:82
  30.9 0.0 collective-permute-done.1.rest_2_
  30.9 1.9 %collective-permute-start.5 = (bf16[96,2432]{1,0:T(8,128)(2,1)}, bf16[96,2432]{1,0:T(8,128)(2,1)}, u32[]{:S(2)}, u32[]{:S(2)}) collective-permute-start(bf16[96,2432]{1,0:T(8,128)(2,1)} %collective-permute-done.1.rest_2_), channel_id=1, source_target_pairs={{0,1},{1,0},{2,3},{3,2},{4,5},{5,4},{6,7},{7,6},{8,9},{9,8},{10,11... | collective-permute-start | bytes 1400840 | tf_op jit(solution)/shard_map/ppermute | solution.py:82
  32.9 0.0 collective-permute-done.2.rest_3_
  32.9 2.4 %collective-permute-start.6 = (bf16[96,2432]{1,0:T(8,128)(2,1)}, bf16[96,2432]{1,0:T(8,128)(2,1)}, u32[]{:S(2)}, u32[]{:S(2)}) collective-permute-start(bf16[96,2432]{1,0:T(8,128)(2,1)} %collective-permute-done.2.rest_3_), channel_id=1, source_target_pairs={{0,1},{1,0},{2,3},{3,2},{4,5},{5,4},{6,7},{7,6},{8,9},{9,8},{10,11... | collective-permute-start | bytes 1400840 | tf_op jit(solution)/shard_map/ppermute | solution.py:82
  35.3 0.1 stack.35.pos
  35.4 0.7 fusion.1.idx
  36.1 0.0 collective-permute-done.3.rest_4_
  36.1 0.0 collective-permute-done.4.rest_5_
  36.2 0.0 collective-permute-done.5.rest_6_
  36.2 0.9 collective-permute-done.6.rest_7_
  37.1 0.0 copy-done.1
  37.1 3.4 %project.1 = bf16[4,16,64,128]{3,2,1,0:T(8,128)(2,1)S(1)} custom-call(s32[4,16]{1,0:T(4,128)S(1)} %fusion.1.idx, s32[8]{0:T(128)S(1)} %stack.35.pos, bf16[4,64,768]{2,1,0:T(8,128)(2,1)S(1)} %all-to-all-done.refs_1_.wall, bf16[96,2432]{1,0:T(8,128)(2,1)S(1)} %bitcast.63, bf16[96,2432]{1,0:T(8,128)(2,1)S(1)} %gate.1.rest_1_, ...), custom_call_target="tpu_custom_call" | custom-call | tf_op jit(solution)/shard_map/project/pallas_call | solution.py:92
  40.5 17.3 %all_to_all.20 = bf16[4,16,64,128]{3,2,1,0:T(8,128)(2,1)S(1)} all-to-all(bf16[4,16,64,128]{3,2,1,0:T(8,128)(2,1)S(1)} %project.1), channel_id=1, replica_groups=mesh['frame'=16,'x'=4,'y'=4,'core'=2] {'x'}, dimensions={0} | all-to-all | bytes 2097152 | tf_op jit(solution)/shard_map/all_to_all | solution.py:105
  57.7 0.9 reduce_sum.22
  58.7 12.1 %all-to-all-start.2 = ((bf16[16,64,128]{2,1,0:T(8,128)(2,1)}), bf16[16,64,128]{2,1,0:T(8,128)(2,1)S(1)}, u32[]{:S(2)}, u32[]{:S(2)}) async-start(bf16[16,64,128]{2,1,0:T(8,128)(2,1)} %reduce_sum.22), calls=%async_computation.2 | async-start | bytes 524288 | tf_op jit(solution)/shard_map/all_to_all | solution.py:107
  70.8 0.9 fusion.6
  71.6 0.9 divide_reduce_fusion
  72.5 0.0 copy-done
  72.6 11.0 %all-to-all-done.2.got = bf16[16,64,128]{2,1,0:T(8,128)(2,1)S(1)} async-done(((bf16[16,64,128]{2,1,0:T(8,128)(2,1)}), bf16[16,64,128]{2,1,0:T(8,128)(2,1)S(1)}, u32[]{:S(2)}, u32[]{:S(2)}) %all-to-all-start.2) | async-done | bytes 262176 | tf_op jit(solution)/shard_map/all_to_all | solution.py:107
  83.5 1.4 %attend.1 = bf16[16,64,128]{2,1,0:T(8,128)(2,1)} custom-call(s32[4]{0:T(128)S(1)} %add_select_fusion.1.src, bf16[16,64,128]{2,1,0:T(8,128)(2,1)S(1)} %all-to-all-done.2.got, bf16[4,128,128]{2,1,0:T(8,128)(2,1)S(1)} %dynamic-slice_bitcast_fusion.maps), custom_call_target="tpu_custom_call" | custom-call | tf_op jit(solution)/shard_map/attend/pallas_call | solution.py:111
  85.0 7.3 %all-to-all-start.3 = ((bf16[16,64,128]{2,1,0:T(8,128)(2,1)}), bf16[16,64,128]{2,1,0:T(8,128)(2,1)S(1)}, u32[]{:S(2)}, u32[]{:S(2)}) async-start(bf16[16,64,128]{2,1,0:T(8,128)(2,1)} %attend.1), calls=%async_computation.3 | async-start | bytes 524288 | tf_op jit(solution)/shard_map/all_to_all | solution.py:119
  92.3 1.3 %copy.14 = bf16[2048,96]{1,0:T(8,128)(2,1)S(1)} copy(bf16[2048,96]{0,1:T(8,128)(2,1)} %param.7) | data formatting | bytes 786432 | tf_op args[2]
  93.6 6.0 %all-to-all-done.3 = bf16[16,64,128]{2,1,0:T(8,128)(2,1)S(1)} async-done(((bf16[16,64,128]{2,1,0:T(8,128)(2,1)}), bf16[16,64,128]{2,1,0:T(8,128)(2,1)S(1)}, u32[]{:S(2)}, u32[]{:S(2)}) %all-to-all-start.3) | async-done | bytes 262176 | tf_op jit(solution)/shard_map/all_to_all | solution.py:119
  99.6 10.1 %all_gather.3 = bf16[2048,128]{1,0:T(8,128)(2,1)S(1)} all-gather(bf16[1024,128]{1,0:T(8,128)(2,1)S(1)} %bitcast.67), channel_id=1, replica_groups=mesh['frame'=16,'x'=4,'y'=4,'core'=2] {'core'}, dimensions={0}, use_global_device_ids=true | all-gather | bytes 786432 | tf_op jit(solution)/shard_map/all_gather | solution.py:120
  109.8 0.9 convolution_convert_fusion
  (4 shorter events, 0.1 us)
Async XLA Ops:
  0.0 72.5 %copy-start = (bf16[16,1,4,128,128]{4,3,2,1,0:T(8,128)(2,1)S(1)}, bf16[16,1,4,128,128]{4,3,2,1,0:T(8,128)(2,1)}, u32[]{:S(2)}) copy-start(bf16[16,1,4,128,128]{4,3,2,1,0:T(8,128)(2,1)} %param.8) | copy-start | bytes 6291460
  0.0 37.1 %copy-start.1 = (bf16[2432,96]{0,1:T(8,128)(2,1)S(1)}, bf16[2432,96]{0,1:T(8,128)(2,1)}, u32[]{:S(2)}) copy-start(bf16[2432,96]{0,1:T(8,128)(2,1)} %param.5) | copy-start | bytes 1400836
  0.0 23.6 %collective-permute-start = (bf16[96,2432]{1,0:T(8,128)(2,1)}, bf16[96,2432]{1,0:T(8,128)(2,1)S(1)}, u32[]{:S(2)}, u32[]{:S(2)}) collective-permute-start(bf16[96,2432]{1,0:T(8,128)(2,1)} %bitcast.59), channel_id=1, source_target_pairs={{0,2},{2,4},{4,6},{6,0},{1,3},{3,5},{5,7},{7,1},{8,10},{10,12},{12... | collective-permute-start | bytes 1400840 | tf_op jit(solution)/shard_map/ppermute | solution.py:77
  4.3 26.6 %collective-permute-start.1 = (bf16[96,2432]{1,0:T(8,128)(2,1)}, bf16[96,2432]{1,0:T(8,128)(2,1)}, u32[]{:S(2)}, u32[]{:S(2)}) collective-permute-start(bf16[96,2432]{1,0:T(8,128)(2,1)} %bitcast.60), channel_id=1, source_target_pairs={{0,6},{2,0},{4,2},{6,4},{1,7},{3,1},{5,3},{7,5},{8,14},{10,8},{12,... | collective-permute-start | bytes 1400840 | tf_op jit(solution)/shard_map/ppermute | solution.py:77
  7.7 25.2 %collective-permute-start.2 = (bf16[96,2432]{1,0:T(8,128)(2,1)}, bf16[96,2432]{1,0:T(8,128)(2,1)}, u32[]{:S(2)}, u32[]{:S(2)}) collective-permute-start(bf16[96,2432]{1,0:T(8,128)(2,1)} %bitcast.61), channel_id=1, source_target_pairs={{0,4},{2,6},{4,0},{6,2},{1,5},{3,7},{5,1},{7,3},{8,12},{10,14},{12... | collective-permute-start | bytes 1400840 | tf_op jit(solution)/shard_map/ppermute | solution.py:77
  13.0 10.6 %all-to-all-start = ((bf16[4,64,768]{2,1,0:T(8,128)(2,1)}), bf16[4,64,768]{2,1,0:T(8,128)(2,1)S(1)}, u32[]{:S(2)}, u32[]{:S(2)}) async-start(bf16[4,64,768]{2,1,0:T(8,128)(2,1)} %bitcast.66), calls=%async_computation | async-start | bytes 786432 | tf_op jit(solution)/shard_map/all_to_all | solution.py:79
  17.0 19.1 %collective-permute-start.3 = (bf16[96,2432]{1,0:T(8,128)(2,1)}, bf16[96,2432]{1,0:T(8,128)(2,1)}, u32[]{:S(2)}, u32[]{:S(2)}) collective-permute-start(bf16[96,2432]{1,0:T(8,128)(2,1)} %bitcast.62), channel_id=1, source_target_pairs={{0,1},{1,0},{2,3},{3,2},{4,5},{5,4},{6,7},{7,6},{8,9},{9,8},{10,11... | collective-permute-start | bytes 1400840 | tf_op jit(solution)/shard_map/ppermute | solution.py:82
  23.6 12.5 %collective-permute-start.4 = (bf16[96,2432]{1,0:T(8,128)(2,1)S(1)}, bf16[96,2432]{1,0:T(8,128)(2,1)}, u32[]{:S(2)}, u32[]{:S(2)}) collective-permute-start(bf16[96,2432]{1,0:T(8,128)(2,1)S(1)} %gate.1.rest_1_), channel_id=1, source_target_pairs={{0,1},{1,0},{2,3},{3,2},{4,5},{5,4},{6,7},{7,6},{8,9},{9,8},{10,11... | collective-permute-start | bytes 1400840 | tf_op jit(solution)/shard_map/ppermute | solution.py:82
  30.9 5.2 %collective-permute-start.5 = (bf16[96,2432]{1,0:T(8,128)(2,1)}, bf16[96,2432]{1,0:T(8,128)(2,1)}, u32[]{:S(2)}, u32[]{:S(2)}) collective-permute-start(bf16[96,2432]{1,0:T(8,128)(2,1)} %collective-permute-done.1.rest_2_), channel_id=1, source_target_pairs={{0,1},{1,0},{2,3},{3,2},{4,5},{5,4},{6,7},{7,6},{8,9},{9,8},{10,11... | collective-permute-start | bytes 1400840 | tf_op jit(solution)/shard_map/ppermute | solution.py:82
  32.9 4.2 %collective-permute-start.6 = (bf16[96,2432]{1,0:T(8,128)(2,1)}, bf16[96,2432]{1,0:T(8,128)(2,1)}, u32[]{:S(2)}, u32[]{:S(2)}) collective-permute-start(bf16[96,2432]{1,0:T(8,128)(2,1)} %collective-permute-done.2.rest_3_), channel_id=1, source_target_pairs={{0,1},{1,0},{2,3},{3,2},{4,5},{5,4},{6,7},{7,6},{8,9},{9,8},{10,11... | collective-permute-start | bytes 1400840 | tf_op jit(solution)/shard_map/ppermute | solution.py:82
  58.7 24.9 %all-to-all-start.2 = ((bf16[16,64,128]{2,1,0:T(8,128)(2,1)}), bf16[16,64,128]{2,1,0:T(8,128)(2,1)S(1)}, u32[]{:S(2)}, u32[]{:S(2)}) async-start(bf16[16,64,128]{2,1,0:T(8,128)(2,1)} %reduce_sum.22), calls=%async_computation.2 | async-start | bytes 524288 | tf_op jit(solution)/shard_map/all_to_all | solution.py:107
  85.0 14.7 %all-to-all-start.3 = ((bf16[16,64,128]{2,1,0:T(8,128)(2,1)}), bf16[16,64,128]{2,1,0:T(8,128)(2,1)S(1)}, u32[]{:S(2)}, u32[]{:S(2)}) async-start(bf16[16,64,128]{2,1,0:T(8,128)(2,1)} %attend.1), calls=%async_computation.3 | async-start | bytes 524288 | tf_op jit(solution)/shard_map/all_to_all | solution.py:119

commit v3 on v1

v3 whole, which is shorter than its diff:
```python
import jax
import jax.numpy as jnp
from jax import lax
from jax.experimental import pallas as pl
from jax.experimental.pallas import tpu as pltpu
from jax.sharding import PartitionSpec as P

BLK = 128
SIDE = 4
CORES = 2
BF = jnp.bfloat16
F32 = jnp.float32
R4 = range(SIDE)


def at(x, y, core):
    return ((x % SIDE) * SIDE + y % SIDE) * CORES + core


ALL = [(x, y, c) for x in R4 for y in R4 for c in range(CORES)]
SWAP = [(at(x, y, c), at(x, y, 1 - c)) for x, y, c in ALL]
CROSS = [[at(x, y, 0) for x in R4] for y in R4] + [[at(x, y, 1) for y in R4] for x in R4]
PLANE = [[at(x, y, c) for x in R4 for y in R4] for c in range(CORES)]
PAIRS = [[at(x, y, c) for c in range(CORES)] for x in R4 for y in R4]


def along(k):
    return [(at(x, y, c), at(x, y + k, c) if c == 0 else at(x + k, y, c)) for x, y, c in ALL]


def pack(core, w, own, oth):
    feat = w.shape[1] // (SIDE * SIDE * CORES)

    def cuts(side, a):
        chips = [a * SIDE + b if side == 0 else b * SIDE + a for b in R4]
        starts = [(chip * CORES + side) * feat for chip in chips]
        return jnp.concatenate([w[:, s : s + feat] for s in starts], axis=1)

    for side in range(CORES):

        @pl.when(core[0] == side)
        def _(side=side):
            for a in R4:
                own[a] = cuts(side, a)
                oth[a] = cuts(1 - side, a)


def project(idx, pos, wall, *rest):
    chunks, (out, gath, vals) = rest[:-3], rest[-3:]
    for i, chunk in enumerate(chunks):
        rows = chunk.shape[0]
        gath[pl.ds(pl.multiple_of(pos[i] * rows, rows), rows), :] = chunk[...]
    for a in R4:
        w = wall[a].reshape(-1, wall.shape[3])
        vals[...] = jnp.dot(w, gath[...], preferred_element_type=F32).astype(BF)
        for q in range(out.shape[1]):
            out[a, q] = vals[:, pl.ds(pl.multiple_of(idx[a, q] * BLK, BLK), BLK)]


def fold(part, own, oth):
    width = own.shape[1]
    for q in range(own.shape[0]):
        total = part[0, q].astype(F32)
        for a in R4[1:]:
            total += part[a, q].astype(F32)
        own[q] = total[:width]
        oth[q] = total[width:].astype(BF)


def attend(src, got, maps, out):
    acc = jnp.zeros(out.shape[1:], F32)
    for s in range(maps.shape[0]):
        acc += lax.dot_general(
            got[src[s]], maps[s], (((1,), (1,)), ((), ())), preferred_element_type=F32
        )
    acc = acc.astype(BF)
    for k in range(out.shape[0]):
        out[k] = acc


def vmem(n):
    return [pl.BlockSpec(memory_space=pltpu.VMEM)] * n


def smem(n):
    return [pl.BlockSpec(memory_space=pltpu.SMEM)] * n


def limit(mib):
    return pltpu.CompilerParams(vmem_limit_bytes=mib * 2**20)


def body(features, w_value, w_out, maps, lists):
    kv_rows, feat = features.shape
    width = w_value.shape[1]
    chan = lax.axis_index("chan")
    frame = lax.axis_index("frame")
    x, y, core = chan // (SIDE * CORES), chan // CORES % SIDE, chan % CORES
    b = jnp.where(core == 0, y, x)
    blocks_dev = kv_rows // BLK
    head = chan // CORES

    def send(v, perm):
        return lax.ppermute(v, "chan", perm)

    def trade(v, groups):
        return lax.all_to_all(v, "chan", 0, 0, axis_index_groups=groups, tiled=True)

    ft = features.T
    chunks = [ft] + [send(ft, along(k)) for k in (1, 3, 2)]
    pos = jnp.stack([lax.rem(b + SIDE - k, SIDE) for k in (0, 1, 3, 2)]).astype(jnp.int32)

    half = jax.ShapeDtypeStruct((SIDE, width, SIDE * feat), BF)
    wown, woth = pl.pallas_call(
        pack,
        out_shape=(half, half),
        in_specs=smem(1) + vmem(1),
        out_specs=vmem(2),
        compiler_params=limit(4),
        name="pack",
    )(core.reshape(1).astype(jnp.int32), w_value.T)
    wall = trade(jnp.stack([wown, send(woth, SWAP)], axis=1), CROSS)

    grid = lists.reshape((SIDE, SIDE) + lists.shape[1:])
    here = jnp.where(
        core == 0,
        lax.dynamic_index_in_dim(grid, b, 1, keepdims=False),
        lax.dynamic_index_in_dim(grid, b, 0, keepdims=False),
    )
    hit = here // blocks_dev == frame
    idx = jnp.sum(jnp.where(hit, here - frame * blocks_dev, 0), axis=2).astype(jnp.int32)

    part = pl.pallas_call(
        project,
        out_shape=jax.ShapeDtypeStruct((SIDE, idx.shape[1], CORES * width, BLK), BF),
        in_specs=smem(2) + vmem(5),
        out_specs=vmem(1)[0],
        scratch_shapes=[pltpu.VMEM((SIDE * feat, kv_rows), BF), pltpu.VMEM((CORES * width, kv_rows), BF)],
        compiler_params=limit(20),
        name="project",
    )(idx, pos, wall, *chunks)
    part = trade(part, CROSS)
    side = (part.shape[1], width, BLK)
    mine, other = pl.pallas_call(
        fold,
        out_shape=(jax.ShapeDtypeStruct(side, F32), jax.ShapeDtypeStruct(side, BF)),
        in_specs=vmem(1),
        out_specs=vmem(2),
        compiler_params=limit(8),
        name="fold",
    )(part)
    blocks = (mine + send(other, SWAP).astype(F32)).astype(BF)
    got = lax.all_to_all(blocks, "frame", 0, 0, tiled=True)

    my_list = lax.dynamic_slice(lists, (head, frame, 0), (1, 1, lists.shape[2])).reshape(-1)
    my_maps = lax.dynamic_index_in_dim(maps[:, 0], head, 0, keepdims=False)
    attn = pl.pallas_call(
        attend,
        out_shape=jax.ShapeDtypeStruct((SIDE * SIDE, width, BLK), BF),
        in_specs=smem(1) + vmem(2),
        out_specs=vmem(1)[0],
        compiler_params=limit(4),
        name="attend",
    )((my_list // blocks_dev).astype(jnp.int32), got, my_maps)
    attn = trade(attn, PLANE).reshape(SIDE * SIDE * width, BLK)
    attn = lax.all_gather(attn, "chan", axis=0, tiled=True, axis_index_groups=PAIRS)
    wo = w_out.T.reshape(w_out.shape[1], SIDE * SIDE, CORES, width).transpose(0, 2, 1, 3)
    mixed = jnp.dot(wo.reshape(w_out.shape[1], -1), attn, preferred_element_type=F32)
    return mixed.astype(BF).T


def solution(mesh):
    in_specs = (
        P("frame", "chan"),
        P(None, "chan"),
        P(None, "chan"),
        P(None, "frame", None, None, None),
        P(),
    )
    return jax.shard_map(body, mesh=mesh, in_specs=in_specs, out_specs=P("frame", "chan"), check_vma=False)
```

time: 137 us -> 106 us (0.77)
  starting transfers between devices: 58.5 us -> 39 us
  local copies, waits for them, and re-layouts: 13.2 us -> 2.48 us
  other arithmetic: 3.94 us -> 2.1 us
    ppermute x10 -> x5, starting transfers between devices: 40.9 us -> 20.2 us  [send(): return lax.ppermute(v, 'chan', perm)]
    unnamed x23 -> x9, local copies, waits for them, and re-layouts: 7.17 us -> 2.43 us
    all_to_all x1, blocking collectives: 14.7 us -> 18.9 us  [trade(): return lax.all_to_all(v, 'chan', 0, 0, axis_index_groups=groups, tiled=True)]
    all_to_all x1, waiting for transfers between devices: 9.82 us -> 13.6 us  [body(): got = lax.all_to_all(blocks, 'frame', 0, 0, tiled=True)]
    ppermute x10 -> x5, waiting for transfers between devices: 11.2 us -> 7.62 us  [send(): return lax.ppermute(v, 'chan', perm)]
    all_gather x1, blocking collectives: 11.8 us -> 8.38 us  [body(): lax.all_gather(attn, 'chan', axis=0, tiled=True, axis_index_groups=PAIRS)]
    dynamic_slice x1 -> x0, local copies, waits for them, and re-layouts: 3.18 us -> none  [w_to(): return lax.dynamic_index_in_dim(wx, lax.rem(x + k, NX), 1, keepdims=False)]
    reshape x1 -> x0, local copies, waits for them, and re-layouts: 2.03 us -> none  [body(): wx = wt.reshape(width, NX, NY * 2 * feat)]
  transfers between devices with their start and end apart: 12 -> 8, of which waited for: 5 -> 5; matrix products, arithmetic and copies ran while one was open for 8% -> 3% of each run, Pallas kernels for 0% -> 0%
where the time goes in v3:
time: 106 us
  starting transfers between devices  39 us (37%)
  waiting for transfers between devices  28.4 us (27%)
  blocking collectives  27.3 us (26%)
  Pallas kernels  5.07 us (5%)
  local copies, waits for them, and re-layouts  2.48 us (2%)
  other arithmetic  2.1 us (2%)
    ppermute x5, starting transfers between devices, send(): return lax.ppermute(v, 'chan', perm)  20.2 us
    all_to_all x1, blocking collectives, trade(): return lax.all_to_all(v, 'chan', 0, 0, axis_index_groups=groups, tiled=True)  18.9 us
    all_to_all x1, waiting for transfers between devices, body(): got = lax.all_to_all(blocks, 'frame', 0, 0, tiled=True)  13.6 us
    all_to_all x1, starting transfers between devices, body(): got = lax.all_to_all(blocks, 'frame', 0, 0, tiled=True)  11.3 us
    all_gather x1, blocking collectives, body(): lax.all_gather(attn, 'chan', axis=0, tiled=True, axis_index_groups=PAIRS)  8.38 us
    ppermute x5, waiting for transfers between devices, send(): return lax.ppermute(v, 'chan', perm)  7.62 us
    all_to_all x2, starting transfers between devices, trade(): return lax.all_to_all(v, 'chan', 0, 0, axis_index_groups=groups, tiled=True)  7.47 us
    all_to_all x2, waiting for transfers between devices, trade(): return lax.all_to_all(v, 'chan', 0, 0, axis_index_groups=groups, tiled=True)  7.25 us
  transfers between devices with their start and end apart: 8, of which 5 were waited for; matrix products, arithmetic and copies ran while one was open for 3% of the time, Pallas kernels for 0%

profile of v3, /device:TPU:1, one launch (start us, length us, event | category | flops | bytes accessed | tf_op | source)
XLA Modules:
  0.0 105.6 jit_solution(11954942481052654184)
XLA Ops:
  0.0 0.0 copy-start
  0.0 0.0 copy-start.1
  0.0 0.0 copy-start.2
  0.0 1.1 %copy-done.2 = bf16[3072,64]{0,1:T(8,128)(2,1)S(1)} copy-done((bf16[3072,64]{0,1:T(8,128)(2,1)S(1)}, bf16[3072,64]{0,1:T(8,128)(2,1)}, u32[]{:S(2)}) %copy-start.2) | copy-done | bytes 393240
  1.2 0.0 copy-start.3
  1.2 0.2 pack.1
  1.4 8.8 %collective-permute-start = (bf16[4,64,384]{2,1,0:T(8,128)(2,1)S(1)}, bf16[4,64,384]{2,1,0:T(8,128)(2,1)S(1)}, u32[]{:S(2)}, u32[]{:S(2)}) collective-permute-start(bf16[4,64,384]{2,1,0:T(8,128)(2,1)S(1)} %get-tuple-element.10), channel_id=1, source_target_pairs={{0,1},{1,0},{2,3},{3,2},{4,5},{5,4},{6,7},{7,6},{8,9},{9,8},{10,11... | collective-permute-start | bytes 589832 | tf_op jit(solution)/shard_map/ppermute | solution.py:104
  10.2 1.9 %collective-permute-start.1 = (bf16[96,2432]{1,0:T(8,128)(2,1)}, bf16[96,2432]{1,0:T(8,128)(2,1)S(1)}, u32[]{:S(2)}, u32[]{:S(2)}) collective-permute-start(bf16[96,2432]{1,0:T(8,128)(2,1)} %bitcast.29), channel_id=1, source_target_pairs={{0,2},{1,9},{2,4},{3,11},{4,6},{5,13},{6,0},{7,15},{8,10},{9,17},{... | collective-permute-start | bytes 1400840 | tf_op jit(solution)/shard_map/ppermute | solution.py:104
  12.1 4.6 %collective-permute-start.2 = (bf16[96,2432]{1,0:T(8,128)(2,1)}, bf16[96,2432]{1,0:T(8,128)(2,1)}, u32[]{:S(2)}, u32[]{:S(2)}) collective-permute-start(bf16[96,2432]{1,0:T(8,128)(2,1)} %bitcast.30), channel_id=1, source_target_pairs={{0,6},{1,25},{2,0},{3,27},{4,2},{5,29},{6,4},{7,31},{8,14},{9,1},{... | collective-permute-start | bytes 1400840 | tf_op jit(solution)/shard_map/ppermute | solution.py:104
  16.7 1.9 %collective-permute-start.3 = (bf16[96,2432]{1,0:T(8,128)(2,1)}, bf16[96,2432]{1,0:T(8,128)(2,1)}, u32[]{:S(2)}, u32[]{:S(2)}) collective-permute-start(bf16[96,2432]{1,0:T(8,128)(2,1)} %bitcast.31), channel_id=1, source_target_pairs={{0,4},{1,17},{2,6},{3,19},{4,0},{5,21},{6,2},{7,23},{8,12},{9,25},... | collective-permute-start | bytes 1400840 | tf_op jit(solution)/shard_map/ppermute | solution.py:104
  18.6 0.0 collective-permute-done
  18.7 0.8 pad_maximum_fusion
  19.5 3.5 %all-to-all-start = ((bf16[4,2,64,384]{3,2,1,0:T(8,128)(2,1)}), bf16[4,2,64,384]{3,2,1,0:T(8,128)(2,1)S(1)}, u32[]{:S(2)}, u32[]{:S(2)}) async-start(bf16[4,2,64,384]{3,2,1,0:T(8,128)(2,1)} %pad_maximum_fusion), calls=%async_computation | async-start | bytes 786432 | tf_op jit(solution)/shard_map/all_to_all | solution.py:107
  23.0 0.0 copy-done.3
  23.1 0.1 pad_add_fusion.pos
  23.2 0.0 collective-permute-done.1.rest_1_
  23.2 6.5 %collective-permute-done.2.rest_2_ = bf16[96,2432]{1,0:T(8,128)(2,1)} collective-permute-done((bf16[96,2432]{1,0:T(8,128)(2,1)}, bf16[96,2432]{1,0:T(8,128)(2,1)}, u32[]{:S(2)}, u32[]{:S(2)}) %collective-permute-start.2) | collective-permute-done | bytes 466976 | tf_op jit(solution)/shard_map/ppermute | solution.py:104
  29.6 0.0 collective-permute-done.3.rest_3_
  29.6 1.2 %all-to-all-done.wall = bf16[4,2,64,384]{3,2,1,0:T(8,128)(2,1)S(1)} async-done(((bf16[4,2,64,384]{3,2,1,0:T(8,128)(2,1)}), bf16[4,2,64,384]{3,2,1,0:T(8,128)(2,1)S(1)}, u32[]{:S(2)}, u32[]{:S(2)}) %all-to-all-start) | async-done | bytes 393248 | tf_op jit(solution)/shard_map/all_to_all | solution.py:107
  30.9 0.0 copy-done.1
  30.9 3.1 %project.1 = bf16[4,16,128,128]{3,2,1,0:T(8,128)(2,1)S(1)} custom-call(s32[4,16]{1,0:T(4,128)S(1)} %select_reduce_fusion.idx, s32[4]{0:T(128)S(1)} %pad_add_fusion.pos, bf16[4,2,64,384]{3,2,1,0:T(8,128)(2,1)S(1)} %all-to-all-done.wall, bf16[96,2432]{1,0:T(8,128)(2,1)S(1)} %bitcast.32, bf16[96,2432]{1,0:T(8,128)(2,1)S(1)} %collective-permute-done.1.rest_1_, ...), custom_call_target="tpu_custom_call" | custom-call | tf_op jit(solution)/shard_map/project/pallas_call | solution.py:133
  34.0 18.9 %all_to_all.20.part = bf16[4,16,128,128]{3,2,1,0:T(8,128)(2,1)S(1)} all-to-all(bf16[4,16,128,128]{3,2,1,0:T(8,128)(2,1)S(1)} %project.1), channel_id=1, replica_groups={{0,8,16,24},{2,10,18,26},{4,12,20,28},{6,14,22,30},{1,3,5,7},{9,11,13,1..., dimensions={0} | all-to-all | bytes 4194304 | tf_op jit(solution)/shard_map/all_to_all | solution.py:107
  53.0 0.2 fold.1
  53.2 3.0 %collective-permute-start.4 = (bf16[16,64,128]{2,1,0:T(8,128)(2,1)S(1)}, bf16[16,64,128]{2,1,0:T(8,128)(2,1)S(1)}, u32[]{:S(2)}, u32[]{:S(2)}) collective-permute-start(bf16[16,64,128]{2,1,0:T(8,128)(2,1)S(1)} %get-tuple-element.12), channel_id=1, source_target_pairs={{0,1},{1,0},{2,3},{3,2},{4,5},{5,4},{6,7},{7,6},{8,9},{9,8},{10,11... | collective-permute-start | bytes 786440 | tf_op jit(solution)/shard_map/ppermute | solution.py:104
  56.2 1.1 %collective-permute-done.4 = bf16[16,64,128]{2,1,0:T(8,128)(2,1)S(1)} collective-permute-done((bf16[16,64,128]{2,1,0:T(8,128)(2,1)S(1)}, bf16[16,64,128]{2,1,0:T(8,128)(2,1)S(1)}, u32[]{:S(2)}, u32[]{:S(2)}) %collective-permute-start.4) | collective-permute-done | bytes 262176 | tf_op jit(solution)/shard_map/ppermute | solution.py:104
  57.4 0.8 add_convert_fusion
  58.2 11.3 %all-to-all-start.2 = ((bf16[16,64,128]{2,1,0:T(8,128)(2,1)}), bf16[16,64,128]{2,1,0:T(8,128)(2,1)S(1)}, u32[]{:S(2)}, u32[]{:S(2)}) async-start(bf16[16,64,128]{2,1,0:T(8,128)(2,1)} %add_convert_fusion), calls=%async_computation.2 | async-start | bytes 524288 | tf_op jit(solution)/shard_map/all_to_all | solution.py:153
  69.5 0.2 fusion.3
  69.7 0.2 divide_reduce_fusion
  69.8 0.0 copy-done
  69.9 13.6 %all-to-all-done.2.got = bf16[16,64,128]{2,1,0:T(8,128)(2,1)S(1)} async-done(((bf16[16,64,128]{2,1,0:T(8,128)(2,1)}), bf16[16,64,128]{2,1,0:T(8,128)(2,1)S(1)}, u32[]{:S(2)}, u32[]{:S(2)}) %all-to-all-start.2) | async-done | bytes 262176 | tf_op jit(solution)/shard_map/all_to_all | solution.py:153
  83.5 1.5 %attend.1 = bf16[16,64,128]{2,1,0:T(8,128)(2,1)} custom-call(s32[4]{0:T(128)S(1)} %add_select_fusion.1.src, bf16[16,64,128]{2,1,0:T(8,128)(2,1)S(1)} %all-to-all-done.2.got, bf16[4,128,128]{2,1,0:T(8,128)(2,1)S(1)} %dynamic-slice_bitcast_fusion.maps), custom_call_target="tpu_custom_call" | custom-call | tf_op jit(solution)/shard_map/attend/pallas_call | solution.py:157
  84.9 4.0 %all-to-all-start.3 = ((bf16[16,64,128]{2,1,0:T(8,128)(2,1)}), bf16[16,64,128]{2,1,0:T(8,128)(2,1)S(1)}, u32[]{:S(2)}, u32[]{:S(2)}) async-start(bf16[16,64,128]{2,1,0:T(8,128)(2,1)} %attend.1), calls=%async_computation.3 | async-start | bytes 524288 | tf_op jit(solution)/shard_map/all_to_all | solution.py:107
  88.9 1.3 %copy.6 = bf16[2048,96]{1,0:T(8,128)(2,1)S(1)} copy(bf16[2048,96]{0,1:T(8,128)(2,1)} %param.7) | data formatting | bytes 786432 | tf_op args[2]
  90.3 6.0 %all-to-all-done.3 = bf16[16,64,128]{2,1,0:T(8,128)(2,1)S(1)} async-done(((bf16[16,64,128]{2,1,0:T(8,128)(2,1)}), bf16[16,64,128]{2,1,0:T(8,128)(2,1)S(1)}, u32[]{:S(2)}, u32[]{:S(2)}) %all-to-all-start.3) | async-done | bytes 262176 | tf_op jit(solution)/shard_map/all_to_all | solution.py:107
  96.3 8.4 %all_gather.3 = bf16[2048,128]{1,0:T(8,128)(2,1)S(1)} all-gather(bf16[1024,128]{1,0:T(8,128)(2,1)S(1)} %bitcast.37), channel_id=1, replica_groups={{0,1},{2,3},{4,5},{6,7},{8,9},{10,11},{12,13},{14,15},{16,17},{18,19},{..., dimensions={0}, use_global_device_ids=true | all-gather | bytes 786432 | tf_op jit(solution)/shard_map/all_gather | solution.py:166
  104.6 1.0 convolution_convert_fusion
  (4 shorter events, 0.1 us)
Async XLA Ops:
  0.0 69.9 %copy-start = (bf16[16,1,4,128,128]{4,3,2,1,0:T(8,128)(2,1)S(1)}, bf16[16,1,4,128,128]{4,3,2,1,0:T(8,128)(2,1)}, u32[]{:S(2)}) copy-start(bf16[16,1,4,128,128]{4,3,2,1,0:T(8,128)(2,1)} %param.8) | copy-start | bytes 6291460
  0.0 30.9 %copy-start.1 = (bf16[2432,96]{0,1:T(8,128)(2,1)S(1)}, bf16[2432,96]{0,1:T(8,128)(2,1)}, u32[]{:S(2)}) copy-start(bf16[2432,96]{0,1:T(8,128)(2,1)} %param.5) | copy-start | bytes 1400836
  0.0 1.2 %copy-start.2 = (bf16[3072,64]{0,1:T(8,128)(2,1)S(1)}, bf16[3072,64]{0,1:T(8,128)(2,1)}, u32[]{:S(2)}) copy-start(bf16[3072,64]{0,1:T(8,128)(2,1)} %param.6) | copy-start | bytes 1179652
  1.2 21.9 %copy-start.3 = (s32[16,16,4]{1,2,0:T(4,128)S(1)}, s32[16,16,4]{1,2,0:T(4,128)}, u32[]{:S(2)}) copy-start(s32[16,16,4]{1,2,0:T(4,128)} %param.9) | copy-start | bytes 12292
  1.4 17.3 %collective-permute-start = (bf16[4,64,384]{2,1,0:T(8,128)(2,1)S(1)}, bf16[4,64,384]{2,1,0:T(8,128)(2,1)S(1)}, u32[]{:S(2)}, u32[]{:S(2)}) collective-permute-start(bf16[4,64,384]{2,1,0:T(8,128)(2,1)S(1)} %get-tuple-element.10), channel_id=1, source_target_pairs={{0,1},{1,0},{2,3},{3,2},{4,5},{5,4},{6,7},{7,6},{8,9},{9,8},{10,11... | collective-permute-start | bytes 589832 | tf_op jit(solution)/shard_map/ppermute | solution.py:104
  10.2 13.0 %collective-permute-start.1 = (bf16[96,2432]{1,0:T(8,128)(2,1)}, bf16[96,2432]{1,0:T(8,128)(2,1)S(1)}, u32[]{:S(2)}, u32[]{:S(2)}) collective-permute-start(bf16[96,2432]{1,0:T(8,128)(2,1)} %bitcast.29), channel_id=1, source_target_pairs={{0,2},{1,9},{2,4},{3,11},{4,6},{5,13},{6,0},{7,15},{8,10},{9,17},{... | collective-permute-start | bytes 1400840 | tf_op jit(solution)/shard_map/ppermute | solution.py:104
  12.1 17.5 %collective-permute-start.2 = (bf16[96,2432]{1,0:T(8,128)(2,1)}, bf16[96,2432]{1,0:T(8,128)(2,1)}, u32[]{:S(2)}, u32[]{:S(2)}) collective-permute-start(bf16[96,2432]{1,0:T(8,128)(2,1)} %bitcast.30), channel_id=1, source_target_pairs={{0,6},{1,25},{2,0},{3,27},{4,2},{5,29},{6,4},{7,31},{8,14},{9,1},{... | collective-permute-start | bytes 1400840 | tf_op jit(solution)/shard_map/ppermute | solution.py:104
  16.7 12.9 %collective-permute-start.3 = (bf16[96,2432]{1,0:T(8,128)(2,1)}, bf16[96,2432]{1,0:T(8,128)(2,1)}, u32[]{:S(2)}, u32[]{:S(2)}) collective-permute-start(bf16[96,2432]{1,0:T(8,128)(2,1)} %bitcast.31), channel_id=1, source_target_pairs={{0,4},{1,17},{2,6},{3,19},{4,0},{5,21},{6,2},{7,23},{8,12},{9,25},... | collective-permute-start | bytes 1400840 | tf_op jit(solution)/shard_map/ppermute | solution.py:104
  19.5 11.4 %all-to-all-start = ((bf16[4,2,64,384]{3,2,1,0:T(8,128)(2,1)}), bf16[4,2,64,384]{3,2,1,0:T(8,128)(2,1)S(1)}, u32[]{:S(2)}, u32[]{:S(2)}) async-start(bf16[4,2,64,384]{3,2,1,0:T(8,128)(2,1)} %pad_maximum_fusion), calls=%async_computation | async-start | bytes 786432 | tf_op jit(solution)/shard_map/all_to_all | solution.py:107
  53.2 4.2 %collective-permute-start.4 = (bf16[16,64,128]{2,1,0:T(8,128)(2,1)S(1)}, bf16[16,64,128]{2,1,0:T(8,128)(2,1)S(1)}, u32[]{:S(2)}, u32[]{:S(2)}) collective-permute-start(bf16[16,64,128]{2,1,0:T(8,128)(2,1)S(1)} %get-tuple-element.12), channel_id=1, source_target_pairs={{0,1},{1,0},{2,3},{3,2},{4,5},{5,4},{6,7},{7,6},{8,9},{9,8},{10,11... | collective-permute-start | bytes 786440 | tf_op jit(solution)/shard_map/ppermute | solution.py:104
  58.2 25.3 %all-to-all-start.2 = ((bf16[16,64,128]{2,1,0:T(8,128)(2,1)}), bf16[16,64,128]{2,1,0:T(8,128)(2,1)S(1)}, u32[]{:S(2)}, u32[]{:S(2)}) async-start(bf16[16,64,128]{2,1,0:T(8,128)(2,1)} %add_convert_fusion), calls=%async_computation.2 | async-start | bytes 524288 | tf_op jit(solution)/shard_map/all_to_all | solution.py:153
  84.9 11.3 %all-to-all-start.3 = ((bf16[16,64,128]{2,1,0:T(8,128)(2,1)}), bf16[16,64,128]{2,1,0:T(8,128)(2,1)S(1)}, u32[]{:S(2)}, u32[]{:S(2)}) async-start(bf16[16,64,128]{2,1,0:T(8,128)(2,1)} %attend.1), calls=%async_computation.3 | async-start | bytes 524288 | tf_op jit(solution)/shard_map/all_to_all | solution.py:107

commit v4 on v3

--- a/solution.py
+++ b/solution.py
@@ -78,6 +78,20 @@
         out[k] = acc
 
 
+def hold(xs):
+    whole = [pl.BlockSpec(memory_space=pl.ANY)] * len(xs)
+    return pl.pallas_call(
+        lambda *refs: None,
+        out_shape=[jax.ShapeDtypeStruct(x.shape, x.dtype) for x in xs],
+        in_specs=whole,
+        out_specs=whole,
+        input_output_aliases={i: i for i in range(len(xs))},
+        cost_estimate=pl.CostEstimate(flops=2 * 10**10, bytes_accessed=10**7, transcendentals=0),
+        compiler_params=limit(1),
+        name="hold",
+    )(*xs)
+
+
 def vmem(n):
     return [pl.BlockSpec(memory_space=pltpu.VMEM)] * n
 
@@ -107,7 +121,7 @@
         return lax.all_to_all(v, "chan", 0, 0, axis_index_groups=groups, tiled=True)
 
     ft = features.T
-    chunks = [ft] + [send(ft, along(k)) for k in (1, 3, 2)]
+    chunks = [ft, *hold([send(ft, along(k)) for k in (1, 3, 2)])]
     pos = jnp.stack([lax.rem(b + SIDE - k, SIDE) for k in (0, 1, 3, 2)]).astype(jnp.int32)
 
     half = jax.ShapeDtypeStruct((SIDE, width, SIDE * feat), BF)

time: 106 us -> 107 us (level)
  starting transfers between devices: 39 us -> 41.5 us
  other arithmetic: 2.1 us -> 4.23 us
  waiting for transfers between devices: 28.4 us -> 26.6 us
  local copies, waits for them, and re-layouts: 2.48 us -> 1.33 us
  blocking collectives: 27.3 us -> 26.2 us
    ppermute x5, waiting for transfers between devices: 7.62 us -> 1.22 us  [send(): return lax.ppermute(v, 'chan', perm)]
    all_to_all x2, waiting for transfers between devices: 7.25 us -> 13.2 us  [trade(): return lax.all_to_all(v, 'chan', 0, 0, axis_index_groups=groups, tiled=True)]
    all_to_all x1, waiting for transfers between devices: 13.6 us -> 12.2 us  [body(): got = lax.all_to_all(blocks, 'frame', 0, 0, tiled=True)]
    unnamed x9, local copies, waits for them, and re-layouts: 2.43 us -> 1.27 us
    all_to_all x1, starting transfers between devices: 11.3 us -> 12.4 us  [body(): got = lax.all_to_all(blocks, 'frame', 0, 0, tiled=True)]
  transfers between devices with their start and end apart: 8 -> 8, of which waited for: 5 -> 5; matrix products, arithmetic and copies ran while one was open for 3% -> 4% of each run, Pallas kernels for 0% -> 0%
where the time goes in v4:
time: 107 us; the launch traced here: 106 us
  starting transfers between devices  41.5 us (39%)
  waiting for transfers between devices  26.6 us (25%)
  blocking collectives  26.2 us (24%)
  Pallas kernels  5.06 us (5%)
  other arithmetic  4.23 us (4%)
  local copies, waits for them, and re-layouts  1.33 us (1%)
    ppermute x5, starting transfers between devices, send(): return lax.ppermute(v, 'chan', perm)  21.1 us
    all_to_all x1, blocking collectives, trade(): return lax.all_to_all(v, 'chan', 0, 0, axis_index_groups=groups, tiled=True)  18.1 us
    all_to_all x2, waiting for transfers between devices, trade(): return lax.all_to_all(v, 'chan', 0, 0, axis_index_groups=groups, tiled=True)  13.2 us
    all_to_all x1, starting transfers between devices, body(): got = lax.all_to_all(blocks, 'frame', 0, 0, tiled=True)  12.4 us
    all_to_all x1, waiting for transfers between devices, body(): got = lax.all_to_all(blocks, 'frame', 0, 0, tiled=True)  12.2 us
    all_gather x1, blocking collectives, body(): lax.all_gather(attn, 'chan', axis=0, tiled=True, axis_index_groups=PAIRS)  8.12 us
    all_to_all x2, starting transfers between devices, trade(): return lax.all_to_all(v, 'chan', 0, 0, axis_index_groups=groups, tiled=True)  8.04 us
    pallas_call x1, Pallas kernels, body(): pl.pallas_call(project, out_shape=jax.ShapeDtypeStruct((SIDE, idx.shape[1...  3.13 us
  transfers between devices with their start and end apart: 8, of which 5 were waited for; matrix products, arithmetic and copies ran while one was open for 4% of the time, Pallas kernels for 0%

profile of v4, /device:TPU:1, one launch (start us, length us, event | category | flops | bytes accessed | tf_op | source)
XLA Modules:
  0.0 106.2 jit_solution(10587522609818018814)
XLA Ops:
  0.0 0.0 copy-start
  0.0 4.1 %collective-permute-start.1 = (bf16[96,2432]{1,0:T(8,128)(2,1)}, bf16[96,2432]{1,0:T(8,128)(2,1)S(1)}, u32[]{:S(2)}, u32[]{:S(2)}) collective-permute-start(bf16[96,2432]{1,0:T(8,128)(2,1)} %bitcast.29), channel_id=1, source_target_pairs={{0,2},{1,9},{2,4},{3,11},{4,6},{5,13},{6,0},{7,15},{8,10},{9,17},{... | collective-permute-start | bytes 1400840 | tf_op jit(solution)/shard_map/ppermute | solution.py:118
  4.1 3.2 %collective-permute-start.2 = (bf16[96,2432]{1,0:T(8,128)(2,1)}, bf16[96,2432]{1,0:T(8,128)(2,1)}, u32[]{:S(2)}, u32[]{:S(2)}) collective-permute-start(bf16[96,2432]{1,0:T(8,128)(2,1)} %bitcast.30), channel_id=1, source_target_pairs={{0,6},{1,25},{2,0},{3,27},{4,2},{5,29},{6,4},{7,31},{8,14},{9,1},{... | collective-permute-start | bytes 1400840 | tf_op jit(solution)/shard_map/ppermute | solution.py:118
  7.3 3.6 %collective-permute-start.3 = (bf16[96,2432]{1,0:T(8,128)(2,1)}, bf16[96,2432]{1,0:T(8,128)(2,1)}, u32[]{:S(2)}, u32[]{:S(2)}) collective-permute-start(bf16[96,2432]{1,0:T(8,128)(2,1)} %bitcast.31), channel_id=1, source_target_pairs={{0,4},{1,17},{2,6},{3,19},{4,0},{5,21},{6,2},{7,23},{8,12},{9,25},... | collective-permute-start | bytes 1400840 | tf_op jit(solution)/shard_map/ppermute | solution.py:118
  10.9 0.0 copy-start.2
  10.9 1.0 copy-done.2
  11.9 0.2 pack.1
  12.2 7.0 %collective-permute-start = (bf16[4,64,384]{2,1,0:T(8,128)(2,1)S(1)}, bf16[4,64,384]{2,1,0:T(8,128)(2,1)S(1)}, u32[]{:S(2)}, u32[]{:S(2)}) collective-permute-start(bf16[4,64,384]{2,1,0:T(8,128)(2,1)S(1)} %get-tuple-element.13), channel_id=1, source_target_pairs={{0,1},{1,0},{2,3},{3,2},{4,5},{5,4},{6,7},{7,6},{8,9},{9,8},{10,11... | collective-permute-start | bytes 589832 | tf_op jit(solution)/shard_map/ppermute | solution.py:118
  19.3 0.8 select_reduce_fusion.idx
  20.1 0.1 pad_add_fusion.pos
  20.2 0.1 collective-permute-done
  20.2 0.8 pad_maximum_fusion
  21.0 4.5 %all-to-all-start = ((bf16[4,2,64,384]{3,2,1,0:T(8,128)(2,1)}), bf16[4,2,64,384]{3,2,1,0:T(8,128)(2,1)S(1)}, u32[]{:S(2)}, u32[]{:S(2)}) async-start(bf16[4,2,64,384]{3,2,1,0:T(8,128)(2,1)} %pad_maximum_fusion), calls=%async_computation | async-start | bytes 786432 | tf_op jit(solution)/shard_map/all_to_all | solution.py:121
  25.5 0.0 copy-start.1
  25.5 0.0 collective-permute-done.1.refs_0_
  25.5 0.0 collective-permute-done.2.refs_1_
  25.5 0.0 collective-permute-done.3.refs_2_
  25.6 6.2 %all-to-all-done.wall = bf16[4,2,64,384]{3,2,1,0:T(8,128)(2,1)S(1)} async-done(((bf16[4,2,64,384]{3,2,1,0:T(8,128)(2,1)}), bf16[4,2,64,384]{3,2,1,0:T(8,128)(2,1)S(1)}, u32[]{:S(2)}, u32[]{:S(2)}) %all-to-all-start) | async-done | bytes 393248 | tf_op jit(solution)/shard_map/all_to_all | solution.py:121
  31.8 0.0 copy-done.1
  31.8 3.1 %project.1 = bf16[4,16,128,128]{3,2,1,0:T(8,128)(2,1)S(1)} custom-call(s32[4,16]{1,0:T(4,128)S(1)} %select_reduce_fusion.idx, s32[4]{0:T(128)S(1)} %pad_add_fusion.pos, bf16[4,2,64,384]{3,2,1,0:T(8,128)(2,1)S(1)} %all-to-all-done.wall, bf16[96,2432]{1,0:T(8,128)(2,1)S(1)} %bitcast.32, bf16[96,2432]{1,0:T(8,128)(2,1)S(1)} %get-tuple-element.14.rest_1_, ...), custom_call_target="tpu_custom_call" | custom-call | tf_op jit(solution)/shard_map/project/pallas_call | solution.py:147
  35.0 18.1 %all_to_all.20.part = bf16[4,16,128,128]{3,2,1,0:T(8,128)(2,1)S(1)} all-to-all(bf16[4,16,128,128]{3,2,1,0:T(8,128)(2,1)S(1)} %project.1), channel_id=1, replica_groups={{0,8,16,24},{2,10,18,26},{4,12,20,28},{6,14,22,30},{1,3,5,7},{9,11,13,1..., dimensions={0} | all-to-all | bytes 4194304 | tf_op jit(solution)/shard_map/all_to_all | solution.py:121
  53.1 0.0 copy-start.3
  53.1 0.2 fold.1
  53.3 3.2 %collective-permute-start.4 = (bf16[16,64,128]{2,1,0:T(8,128)(2,1)S(1)}, bf16[16,64,128]{2,1,0:T(8,128)(2,1)S(1)}, u32[]{:S(2)}, u32[]{:S(2)}) collective-permute-start(bf16[16,64,128]{2,1,0:T(8,128)(2,1)S(1)} %get-tuple-element.18), channel_id=1, source_target_pairs={{0,1},{1,0},{2,3},{3,2},{4,5},{5,4},{6,7},{7,6},{8,9},{9,8},{10,11... | collective-permute-start | bytes 786440 | tf_op jit(solution)/shard_map/ppermute | solution.py:118
  56.5 1.1 %collective-permute-done.4 = bf16[16,64,128]{2,1,0:T(8,128)(2,1)S(1)} collective-permute-done((bf16[16,64,128]{2,1,0:T(8,128)(2,1)S(1)}, bf16[16,64,128]{2,1,0:T(8,128)(2,1)S(1)}, u32[]{:S(2)}, u32[]{:S(2)}) %collective-permute-start.4) | collective-permute-done | bytes 262176 | tf_op jit(solution)/shard_map/ppermute | solution.py:118
  57.6 0.8 add_convert_fusion
  58.4 12.4 %all-to-all-start.2 = ((bf16[16,64,128]{2,1,0:T(8,128)(2,1)}), bf16[16,64,128]{2,1,0:T(8,128)(2,1)S(1)}, u32[]{:S(2)}, u32[]{:S(2)}) async-start(bf16[16,64,128]{2,1,0:T(8,128)(2,1)} %add_convert_fusion), calls=%async_computation.2 | async-start | bytes 524288 | tf_op jit(solution)/shard_map/all_to_all | solution.py:167
  70.8 0.9 fusion.3
  71.7 0.9 divide_reduce_fusion
  72.6 0.0 copy-done
  72.6 12.2 %all-to-all-done.2.got = bf16[16,64,128]{2,1,0:T(8,128)(2,1)S(1)} async-done(((bf16[16,64,128]{2,1,0:T(8,128)(2,1)}), bf16[16,64,128]{2,1,0:T(8,128)(2,1)S(1)}, u32[]{:S(2)}, u32[]{:S(2)}) %all-to-all-start.2) | async-done | bytes 262176 | tf_op jit(solution)/shard_map/all_to_all | solution.py:167
  84.8 1.5 %attend.1 = bf16[16,64,128]{2,1,0:T(8,128)(2,1)} custom-call(s32[4]{0:T(128)S(1)} %add_select_fusion.1.src, bf16[16,64,128]{2,1,0:T(8,128)(2,1)S(1)} %all-to-all-done.2.got, bf16[4,128,128]{2,1,0:T(8,128)(2,1)S(1)} %dynamic-slice_bitcast_fusion.maps), custom_call_target="tpu_custom_call" | custom-call | tf_op jit(solution)/shard_map/attend/pallas_call | solution.py:171
  86.3 3.5 %all-to-all-start.3 = ((bf16[16,64,128]{2,1,0:T(8,128)(2,1)}), bf16[16,64,128]{2,1,0:T(8,128)(2,1)S(1)}, u32[]{:S(2)}, u32[]{:S(2)}) async-start(bf16[16,64,128]{2,1,0:T(8,128)(2,1)} %attend.1), calls=%async_computation.3 | async-start | bytes 524288 | tf_op jit(solution)/shard_map/all_to_all | solution.py:121
  89.8 0.0 copy-done.3
  89.8 0.3 copy.9
  90.2 7.0 %all-to-all-done.3 = bf16[16,64,128]{2,1,0:T(8,128)(2,1)S(1)} async-done(((bf16[16,64,128]{2,1,0:T(8,128)(2,1)}), bf16[16,64,128]{2,1,0:T(8,128)(2,1)S(1)}, u32[]{:S(2)}, u32[]{:S(2)}) %all-to-all-start.3) | async-done | bytes 262176 | tf_op jit(solution)/shard_map/all_to_all | solution.py:121
  97.1 8.1 %all_gather.3 = bf16[2048,128]{1,0:T(8,128)(2,1)S(1)} all-gather(bf16[1024,128]{1,0:T(8,128)(2,1)S(1)} %bitcast.37), channel_id=1, replica_groups={{0,1},{2,3},{4,5},{6,7},{8,9},{10,11},{12,13},{14,15},{16,17},{18,19},{..., dimensions={0}, use_global_device_ids=true | all-gather | bytes 786432 | tf_op jit(solution)/shard_map/all_gather | solution.py:180
  105.2 0.9 convolution_convert_fusion
  (4 shorter events, 0.1 us)
Async XLA Ops:
  0.0 72.6 %copy-start = (bf16[16,1,4,128,128]{4,3,2,1,0:T(8,128)(2,1)S(1)}, bf16[16,1,4,128,128]{4,3,2,1,0:T(8,128)(2,1)}, u32[]{:S(2)}) copy-start(bf16[16,1,4,128,128]{4,3,2,1,0:T(8,128)(2,1)} %param.8) | copy-start | bytes 6291460
  0.0 25.5 %collective-permute-start.1 = (bf16[96,2432]{1,0:T(8,128)(2,1)}, bf16[96,2432]{1,0:T(8,128)(2,1)S(1)}, u32[]{:S(2)}, u32[]{:S(2)}) collective-permute-start(bf16[96,2432]{1,0:T(8,128)(2,1)} %bitcast.29), channel_id=1, source_target_pairs={{0,2},{1,9},{2,4},{3,11},{4,6},{5,13},{6,0},{7,15},{8,10},{9,17},{... | collective-permute-start | bytes 1400840 | tf_op jit(solution)/shard_map/ppermute | solution.py:118
  4.1 21.5 %collective-permute-start.2 = (bf16[96,2432]{1,0:T(8,128)(2,1)}, bf16[96,2432]{1,0:T(8,128)(2,1)}, u32[]{:S(2)}, u32[]{:S(2)}) collective-permute-start(bf16[96,2432]{1,0:T(8,128)(2,1)} %bitcast.30), channel_id=1, source_target_pairs={{0,6},{1,25},{2,0},{3,27},{4,2},{5,29},{6,4},{7,31},{8,14},{9,1},{... | collective-permute-start | bytes 1400840 | tf_op jit(solution)/shard_map/ppermute | solution.py:118
  7.3 18.3 %collective-permute-start.3 = (bf16[96,2432]{1,0:T(8,128)(2,1)}, bf16[96,2432]{1,0:T(8,128)(2,1)}, u32[]{:S(2)}, u32[]{:S(2)}) collective-permute-start(bf16[96,2432]{1,0:T(8,128)(2,1)} %bitcast.31), channel_id=1, source_target_pairs={{0,4},{1,17},{2,6},{3,19},{4,0},{5,21},{6,2},{7,23},{8,12},{9,25},... | collective-permute-start | bytes 1400840 | tf_op jit(solution)/shard_map/ppermute | solution.py:118
  10.9 1.0 copy-start.2
  12.2 8.1 %collective-permute-start = (bf16[4,64,384]{2,1,0:T(8,128)(2,1)S(1)}, bf16[4,64,384]{2,1,0:T(8,128)(2,1)S(1)}, u32[]{:S(2)}, u32[]{:S(2)}) collective-permute-start(bf16[4,64,384]{2,1,0:T(8,128)(2,1)S(1)} %get-tuple-element.13), channel_id=1, source_target_pairs={{0,1},{1,0},{2,3},{3,2},{4,5},{5,4},{6,7},{7,6},{8,9},{9,8},{10,11... | collective-permute-start | bytes 589832 | tf_op jit(solution)/shard_map/ppermute | solution.py:118
  21.0 10.8 %all-to-all-start = ((bf16[4,2,64,384]{3,2,1,0:T(8,128)(2,1)}), bf16[4,2,64,384]{3,2,1,0:T(8,128)(2,1)S(1)}, u32[]{:S(2)}, u32[]{:S(2)}) async-start(bf16[4,2,64,384]{3,2,1,0:T(8,128)(2,1)} %pad_maximum_fusion), calls=%async_computation | async-start | bytes 786432 | tf_op jit(solution)/shard_map/all_to_all | solution.py:121
  25.5 6.3 %copy-start.1 = (bf16[2432,96]{0,1:T(8,128)(2,1)S(1)}, bf16[2432,96]{0,1:T(8,128)(2,1)}, u32[]{:S(2)}) copy-start(bf16[2432,96]{0,1:T(8,128)(2,1)} %param.5) | copy-start | bytes 1400836
  53.1 36.7 %copy-start.3 = (bf16[2048,96]{0,1:T(8,128)(2,1)S(1)}, bf16[2048,96]{0,1:T(8,128)(2,1)}, u32[]{:S(2)}) copy-start(bf16[2048,96]{0,1:T(8,128)(2,1)} %param.7) | copy-start | bytes 1179652
  53.3 4.3 %collective-permute-start.4 = (bf16[16,64,128]{2,1,0:T(8,128)(2,1)S(1)}, bf16[16,64,128]{2,1,0:T(8,128)(2,1)S(1)}, u32[]{:S(2)}, u32[]{:S(2)}) collective-permute-start(bf16[16,64,128]{2,1,0:T(8,128)(2,1)S(1)} %get-tuple-element.18), channel_id=1, source_target_pairs={{0,1},{1,0},{2,3},{3,2},{4,5},{5,4},{6,7},{7,6},{8,9},{9,8},{10,11... | collective-permute-start | bytes 786440 | tf_op jit(solution)/shard_map/ppermute | solution.py:118
  58.4 26.4 %all-to-all-start.2 = ((bf16[16,64,128]{2,1,0:T(8,128)(2,1)}), bf16[16,64,128]{2,1,0:T(8,128)(2,1)S(1)}, u32[]{:S(2)}, u32[]{:S(2)}) async-start(bf16[16,64,128]{2,1,0:T(8,128)(2,1)} %add_convert_fusion), calls=%async_computation.2 | async-start | bytes 524288 | tf_op jit(solution)/shard_map/all_to_all | solution.py:167
  86.3 10.8 %all-to-all-start.3 = ((bf16[16,64,128]{2,1,0:T(8,128)(2,1)}), bf16[16,64,128]{2,1,0:T(8,128)(2,1)S(1)}, u32[]{:S(2)}, u32[]{:S(2)}) async-start(bf16[16,64,128]{2,1,0:T(8,128)(2,1)} %attend.1), calls=%async_computation.3 | async-start | bytes 524288 | tf_op jit(solution)/shard_map/all_to_all | solution.py:121

commit v5 on v3

--- a/solution.py
+++ b/solution.py
@@ -1,3 +1,5 @@
+import functools
+
 import jax
 import jax.numpy as jnp
 from jax import lax
@@ -43,6 +45,23 @@
             for a in R4:
                 own[a] = cuts(side, a)
                 oth[a] = cuts(1 - side, a)
+
+
+def prepare(blocks_dev, pos, lists, maps, idx, src, mine, sem):
+    core, b, head, frame = (pos[i] for i in range(4))
+    copy = pltpu.make_async_copy(maps.at[head, 0], mine, sem)
+    copy.start()
+    for a in R4:
+        partner = jnp.where(core == 0, a * SIDE + b, b * SIDE + a)
+        for q in range(idx.shape[1]):
+            place = jnp.int32(0)
+            for s in range(lists.shape[1]):
+                local = lists[partner, s, q] - frame * blocks_dev
+                place = jnp.where((local >= 0) & (local < blocks_dev), local, place)
+            idx[a, q] = place
+    for s in range(lists.shape[1]):
+        src[s] = lax.div(lists[head, s, frame], jnp.int32(blocks_dev))
+    copy.wait()
 
 
 def project(idx, pos, wall, *rest):
@@ -67,6 +86,10 @@
         oth[q] = total[width:].astype(BF)
 
 
+def merge(core, mine, pair, out):
+    out[...] = (mine[...] + pair[1 - core[0]].astype(F32)).astype(BF)
+
+
 def attend(src, got, maps, out):
     acc = jnp.zeros(out.shape[1:], F32)
     for s in range(maps.shape[0]):
@@ -78,6 +101,11 @@
         out[k] = acc
 
 
+def output(attn, w, out):
+    rows = [attn[c, chip] for chip in range(attn.shape[1]) for c in range(CORES)]
+    out[...] = jnp.dot(w[...], jnp.concatenate(rows, axis=0), preferred_element_type=F32).astype(BF)
+
+
 def vmem(n):
     return [pl.BlockSpec(memory_space=pltpu.VMEM)] * n
 
@@ -97,7 +125,6 @@
     frame = lax.axis_index("frame")
     x, y, core = chan // (SIDE * CORES), chan // CORES % SIDE, chan % CORES
     b = jnp.where(core == 0, y, x)
-    blocks_dev = kv_rows // BLK
     head = chan // CORES
 
     def send(v, perm):
@@ -121,14 +148,20 @@
     )(core.reshape(1).astype(jnp.int32), w_value.T)
     wall = trade(jnp.stack([wown, send(woth, SWAP)], axis=1), CROSS)
 
-    grid = lists.reshape((SIDE, SIDE) + lists.shape[1:])
-    here = jnp.where(
-        core == 0,
-        lax.dynamic_index_in_dim(grid, b, 1, keepdims=False),
-        lax.dynamic_index_in_dim(grid, b, 0, keepdims=False),
-    )
-    hit = here // blocks_dev == frame
-    idx = jnp.sum(jnp.where(hit, here - frame * blocks_dev, 0), axis=2).astype(jnp.int32)
+    slots = lists.shape[2]
+    idx, src, my_maps = pl.pallas_call(
+        functools.partial(prepare, kv_rows // BLK),
+        out_shape=(
+            jax.ShapeDtypeStruct((SIDE, lists.shape[1]), jnp.int32),
+            jax.ShapeDtypeStruct((slots,), jnp.int32),
+            jax.ShapeDtypeStruct((slots, BLK, BLK), BF),
+        ),
+        in_specs=smem(2) + [pl.BlockSpec(memory_space=pltpu.HBM)],
+        out_specs=smem(2) + vmem(1),
+        scratch_shapes=[pltpu.SemaphoreType.DMA],
+        compiler_params=limit(4),
+        name="prepare",
+    )(jnp.stack([core, b, head, frame]).astype(jnp.int32), lists.transpose(0, 2, 1), maps)
 
     part = pl.pallas_call(
         project,
@@ -149,11 +182,16 @@
         compiler_params=limit(8),
         name="fold",
     )(part)
-    blocks = (mine + send(other, SWAP).astype(F32)).astype(BF)
+    pair = lax.all_gather(other, "chan", axis_index_groups=PAIRS)
+    blocks = pl.pallas_call(
+        merge,
+        out_shape=jax.ShapeDtypeStruct(side, BF),
+        in_specs=smem(1) + vmem(2),
+        out_specs=vmem(1)[0],
+        compiler_params=limit(4),
+        name="merge",
+    )(core.reshape(1).astype(jnp.int32), mine, pair)
     got = lax.all_to_all(blocks, "frame", 0, 0, tiled=True)
-
-    my_list = lax.dynamic_slice(lists, (head, frame, 0), (1, 1, lists.shape[2])).reshape(-1)
-    my_maps = lax.dynamic_index_in_dim(maps[:, 0], head, 0, keepdims=False)
     attn = pl.pallas_call(
         attend,
         out_shape=jax.ShapeDtypeStruct((SIDE * SIDE, width, BLK), BF),
@@ -161,12 +199,17 @@
         out_specs=vmem(1)[0],
         compiler_params=limit(4),
         name="attend",
-    )((my_list // blocks_dev).astype(jnp.int32), got, my_maps)
-    attn = trade(attn, PLANE).reshape(SIDE * SIDE * width, BLK)
-    attn = lax.all_gather(attn, "chan", axis=0, tiled=True, axis_index_groups=PAIRS)
-    wo = w_out.T.reshape(w_out.shape[1], SIDE * SIDE, CORES, width).transpose(0, 2, 1, 3)
-    mixed = jnp.dot(wo.reshape(w_out.shape[1], -1), attn, preferred_element_type=F32)
-    return mixed.astype(BF).T
+    )(src, got, my_maps)
+    attn = lax.all_gather(trade(attn, PLANE), "chan", axis_index_groups=PAIRS)
+    mixed = pl.pallas_call(
+        output,
+        out_shape=jax.ShapeDtypeStruct((w_out.shape[1], BLK), BF),
+        in_specs=vmem(2),
+        out_specs=vmem(1)[0],
+        compiler_params=limit(4),
+        name="output",
+    )(attn, w_out.T)
+    return mixed.T
 
 
 def solution(mesh):

time: 106 us -> 104 us (0.981)
  blocking collectives: 27.3 us -> 67.8 us
  waiting for transfers between devices: 28.4 us -> 3.37 us
  starting transfers between devices: 39 us -> 19.5 us
  Pallas kernels: 5.07 us -> 7.68 us
  local copies, waits for them, and re-layouts: 2.48 us -> 3.77 us
  other arithmetic: 2.1 us -> 0.97 us
    all_to_all x0 -> x1, blocking collectives: none -> 27.8 us  [body(): got = lax.all_to_all(blocks, 'frame', 0, 0, tiled=True)]
    all_to_all x1 -> x0, waiting for transfers between devices: 13.6 us -> none  [body(): got = lax.all_to_all(blocks, 'frame', 0, 0, tiled=True)]
    all_to_all x1 -> x0, starting transfers between devices: 11.3 us -> none  [body(): got = lax.all_to_all(blocks, 'frame', 0, 0, tiled=True)]
    all_to_all x1 -> x2, blocking collectives: 18.9 us -> 28.6 us  [trade(): return lax.all_to_all(v, 'chan', 0, 0, axis_index_groups=groups, tiled=True)]
    ppermute x5 -> x4, waiting for transfers between devices: 7.62 us -> 0.33 us  [send(): return lax.ppermute(v, 'chan', perm)]
    ppermute x5 -> x4, starting transfers between devices: 20.2 us -> 16 us  [send(): return lax.ppermute(v, 'chan', perm)]
    all_to_all x2 -> x1, waiting for transfers between devices: 7.25 us -> 3.04 us  [trade(): return lax.all_to_all(v, 'chan', 0, 0, axis_index_groups=groups, tiled=True)]
    all_to_all x2 -> x1, starting transfers between devices: 7.47 us -> 3.46 us  [trade(): return lax.all_to_all(v, 'chan', 0, 0, axis_index_groups=groups, tiled=True)]
  transfers between devices with their start and end apart: 8 -> 5, of which waited for: 5 -> 2; matrix products, arithmetic and copies ran while one was open for 3% -> 1% of each run, Pallas kernels for 0% -> 2%
where the time goes in v5:
time: 104 us; the launch traced here: 103 us
  blocking collectives  67.8 us (65%)
  starting transfers between devices  19.5 us (19%)
  Pallas kernels  7.68 us (7%)
  local copies, waits for them, and re-layouts  3.77 us (4%)
  waiting for transfers between devices  3.37 us (3%)
    all_to_all x2, blocking collectives, trade(): return lax.all_to_all(v, 'chan', 0, 0, axis_index_groups=groups, tiled=True)  28.6 us
    all_to_all x1, blocking collectives, body(): got = lax.all_to_all(blocks, 'frame', 0, 0, tiled=True)  27.8 us
    ppermute x4, starting transfers between devices, send(): return lax.ppermute(v, 'chan', perm)  16 us
    all_gather x1, blocking collectives, body(): attn = lax.all_gather(trade(attn, PLANE), 'chan', axis_index_groups=PAIRS)  8.38 us
    unnamed x18, local copies, waits for them, and re-layouts  3.77 us
    all_to_all x1, starting transfers between devices, trade(): return lax.all_to_all(v, 'chan', 0, 0, axis_index_groups=groups, tiled=True)  3.46 us
    pallas_call x1, Pallas kernels, body(): pl.pallas_call(project, out_shape=jax.ShapeDtypeStruct((SIDE, idx.shape[1...  3.15 us
    all_to_all x1, waiting for transfers between devices, trade(): return lax.all_to_all(v, 'chan', 0, 0, axis_index_groups=groups, tiled=True)  3.04 us
  transfers between devices with their start and end apart: 5, of which 2 were waited for; matrix products, arithmetic and copies ran while one was open for 1% of the time, Pallas kernels for 2%

profile of v5, /device:TPU:1, one launch (start us, length us, event | category | flops | bytes accessed | tf_op | source)
XLA Modules:
  0.0 103.2 jit_solution(2493945607677585914)
XLA Ops:
  0.0 0.0 copy-start
  0.0 0.0 copy-start.3
  0.0 1.1 %copy-done.3 = bf16[3072,64]{0,1:T(8,128)(2,1)S(1)} copy-done((bf16[3072,64]{0,1:T(8,128)(2,1)S(1)}, bf16[3072,64]{0,1:T(8,128)(2,1)}, u32[]{:S(2)}) %copy-start.3) | copy-done | bytes 393240
  1.1 0.0 copy-start.1
  1.2 0.2 pack.1
  1.4 8.8 %collective-permute-start = (bf16[4,64,384]{2,1,0:T(8,128)(2,1)S(1)}, bf16[4,64,384]{2,1,0:T(8,128)(2,1)S(1)}, u32[]{:S(2)}, u32[]{:S(2)}) collective-permute-start(bf16[4,64,384]{2,1,0:T(8,128)(2,1)S(1)} %get-tuple-element.15), channel_id=1, source_target_pairs={{0,1},{1,0},{2,3},{3,2},{4,5},{5,4},{6,7},{7,6},{8,9},{9,8},{10,11... | collective-permute-start | bytes 589832 | tf_op jit(solution)/shard_map/ppermute | solution.py:131
  10.2 1.9 %collective-permute-start.3 = (bf16[96,2432]{1,0:T(8,128)(2,1)}, bf16[96,2432]{1,0:T(8,128)(2,1)S(1)}, u32[]{:S(2)}, u32[]{:S(2)}) collective-permute-start(bf16[96,2432]{1,0:T(8,128)(2,1)} %bitcast.19), channel_id=1, source_target_pairs={{0,4},{1,17},{2,6},{3,19},{4,0},{5,21},{6,2},{7,23},{8,12},{9,25},... | collective-permute-start | bytes 1400840 | tf_op jit(solution)/shard_map/ppermute | solution.py:131
  12.1 1.9 %collective-permute-start.2 = (bf16[96,2432]{1,0:T(8,128)(2,1)}, bf16[96,2432]{1,0:T(8,128)(2,1)}, u32[]{:S(2)}, u32[]{:S(2)}) collective-permute-start(bf16[96,2432]{1,0:T(8,128)(2,1)} %bitcast.20), channel_id=1, source_target_pairs={{0,6},{1,25},{2,0},{3,27},{4,2},{5,29},{6,4},{7,31},{8,14},{9,1},{... | collective-permute-start | bytes 1400840 | tf_op jit(solution)/shard_map/ppermute | solution.py:131
  14.1 3.4 %collective-permute-start.1 = (bf16[96,2432]{1,0:T(8,128)(2,1)}, bf16[96,2432]{1,0:T(8,128)(2,1)}, u32[]{:S(2)}, u32[]{:S(2)}) collective-permute-start(bf16[96,2432]{1,0:T(8,128)(2,1)} %bitcast.21), channel_id=1, source_target_pairs={{0,2},{1,9},{2,4},{3,11},{4,6},{5,13},{6,0},{7,15},{8,10},{9,17},{... | collective-permute-start | bytes 1400840 | tf_op jit(solution)/shard_map/ppermute | solution.py:131
  17.4 0.0 collective-permute-done
  17.4 0.8 pad_maximum_fusion
  18.3 3.5 %all-to-all-start = ((bf16[4,2,64,384]{3,2,1,0:T(8,128)(2,1)}), bf16[4,2,64,384]{3,2,1,0:T(8,128)(2,1)S(1)}, u32[]{:S(2)}, u32[]{:S(2)}) async-start(bf16[4,2,64,384]{3,2,1,0:T(8,128)(2,1)} %pad_maximum_fusion), calls=%async_computation | async-start | bytes 786432 | tf_op jit(solution)/shard_map/all_to_all | solution.py:134
  21.8 0.1 pad_add_fusion.pos
  21.9 0.0 copy-done
  21.9 0.0 copy-start.4
  21.9 0.8 copy-done.4
  22.6 2.4 %prepare.1 = (s32[4,16]{1,0:T(4,128)S(1)}, s32[4]{0:T(128)S(1)}, bf16[4,128,128]{2,1,0:T(8,128)(2,1)S(1)}) custom-call(s32[4]{0:T(128)S(1)} %pad_add_fusion.pos, s32[16,4,16]{2,1,0:T(4,128)S(1)} %bitcast.26, bf16[16,1,4,128,128]{4,3,2,1,0:T(8,128)(2,1)S(1)} %copy-done), custom_call_target="tpu_custom_call" | custom-call | tf_op jit(solution)/shard_map/prepare/pallas_call | solution.py:152
  25.0 0.0 copy-start.5
  25.1 0.6 copy-done.5
  25.6 0.0 copy-start.7
  25.6 0.6 copy-done.7
  26.2 0.1 pad_add_fusion.1.pos
  26.3 0.0 collective-permute-done.3.rest_3_
  26.3 0.0 collective-permute-done.2.rest_2_
  26.3 0.3 collective-permute-done.1.rest_1_
  26.6 3.0 %all-to-all-done.wall = bf16[4,2,64,384]{3,2,1,0:T(8,128)(2,1)S(1)} async-done(((bf16[4,2,64,384]{3,2,1,0:T(8,128)(2,1)}), bf16[4,2,64,384]{3,2,1,0:T(8,128)(2,1)S(1)}, u32[]{:S(2)}, u32[]{:S(2)}) %all-to-all-start) | async-done | bytes 393248 | tf_op jit(solution)/shard_map/all_to_all | solution.py:134
  29.7 0.0 copy-done.1
  29.7 0.0 copy-start.6
  29.7 0.7 copy-done.6
  30.3 3.1 %project.1 = bf16[4,16,128,128]{3,2,1,0:T(8,128)(2,1)S(1)} custom-call(s32[4,16]{1,0:T(4,128)S(1)} %copy-done.6, s32[4]{0:T(128)S(1)} %pad_add_fusion.1.pos, bf16[4,2,64,384]{3,2,1,0:T(8,128)(2,1)S(1)} %all-to-all-done.wall, bf16[96,2432]{1,0:T(8,128)(2,1)S(1)} %bitcast.22, bf16[96,2432]{1,0:T(8,128)(2,1)} %collective-permute-done.1.rest_1_, ...), custom_call_target="tpu_custom_call" | custom-call | tf_op jit(solution)/shard_map/project/pallas_call | solution.py:166
  33.5 17.9 %all_to_all.20.part = bf16[4,16,128,128]{3,2,1,0:T(8,128)(2,1)S(1)} all-to-all(bf16[4,16,128,128]{3,2,1,0:T(8,128)(2,1)S(1)} %project.1), channel_id=1, replica_groups={{0,8,16,24},{2,10,18,26},{4,12,20,28},{6,14,22,30},{1,3,5,7},{9,11,13,1..., dimensions={0} | all-to-all | bytes 4194304 | tf_op jit(solution)/shard_map/all_to_all | solution.py:134
  51.4 0.0 copy-start.8
  51.4 0.2 fold.1
  51.6 2.9 %all-gather = bf16[32,64,128]{2,1,0:T(8,128)(2,1)S(1)} all-gather(bf16[16,64,128]{2,1,0:T(8,128)(2,1)S(1)} %get-tuple-element.17), channel_id=2, replica_groups={{0,1},{2,3},{4,5},{6,7},{8,9},{10,11},{12,13},{14,15},{16,17},{18,19},{..., dimensions={0}, use_global_device_ids=true | all-gather | bytes 786432 | tf_op jit(solution)/shard_map/all_gather | solution.py:185
  54.5 0.0 copy-start.2
  54.6 27.8 %all_to_all.21.got = bf16[16,64,128]{2,1,0:T(8,128)(2,1)S(1)} all-to-all(bf16[16,64,128]{2,1,0:T(8,128)(2,1)S(1)} %merge.1), channel_id=1, replica_groups=mesh['frame'=16,'chan'=32] {'frame'}, dimensions={0} | all-to-all | bytes 524288 | tf_op jit(solution)/shard_map/all_to_all | solution.py:194
  82.4 0.0 copy-done.8
  82.4 0.8 attend.1
  83.2 10.8 %all_to_all.22 = bf16[16,64,128]{2,1,0:T(8,128)(2,1)S(1)} all-to-all(bf16[16,64,128]{2,1,0:T(8,128)(2,1)S(1)} %attend.1), channel_id=1, replica_groups={{0,2,4,6,8,10,12,14,16,18,20,22,24,26,28,30},{1,3,5,7,9,11,13,15,17,19,..., dimensions={0} | all-to-all | bytes 524288 | tf_op jit(solution)/shard_map/all_to_all | solution.py:134
  93.9 8.4 %all-gather.1 = bf16[32,64,128]{2,1,0:T(8,128)(2,1)S(1)} all-gather(bf16[16,64,128]{2,1,0:T(8,128)(2,1)S(1)} %all_to_all.22), channel_id=3, replica_groups={{0,1},{2,3},{4,5},{6,7},{8,9},{10,11},{12,13},{14,15},{16,17},{18,19},{..., dimensions={0}, use_global_device_ids=true | all-gather | bytes 786432 | tf_op jit(solution)/shard_map/all_gather | solution.py:203
  102.3 0.0 copy-done.2
  102.3 0.9 output.1
  (1 shorter events, 0.0 us)
Async XLA Ops:
  0.0 21.9 %copy-start = (bf16[16,1,4,128,128]{4,3,2,1,0:T(8,128)(2,1)S(1)}, bf16[16,1,4,128,128]{4,3,2,1,0:T(8,128)(2,1)}, u32[]{:S(2)}) copy-start(bf16[16,1,4,128,128]{4,3,2,1,0:T(8,128)(2,1)} %maps.1) | copy-start | bytes 6291460
  0.0 1.1 %copy-start.3 = (bf16[3072,64]{0,1:T(8,128)(2,1)S(1)}, bf16[3072,64]{0,1:T(8,128)(2,1)}, u32[]{:S(2)}) copy-start(bf16[3072,64]{0,1:T(8,128)(2,1)} %param.6) | copy-start | bytes 1179652
  1.1 28.5 %copy-start.1 = (bf16[2432,96]{0,1:T(8,128)(2,1)S(1)}, bf16[2432,96]{0,1:T(8,128)(2,1)}, u32[]{:S(2)}) copy-start(bf16[2432,96]{0,1:T(8,128)(2,1)} %param.5) | copy-start | bytes 1400836
  1.4 16.0 %collective-permute-start = (bf16[4,64,384]{2,1,0:T(8,128)(2,1)S(1)}, bf16[4,64,384]{2,1,0:T(8,128)(2,1)S(1)}, u32[]{:S(2)}, u32[]{:S(2)}) collective-permute-start(bf16[4,64,384]{2,1,0:T(8,128)(2,1)S(1)} %get-tuple-element.15), channel_id=1, source_target_pairs={{0,1},{1,0},{2,3},{3,2},{4,5},{5,4},{6,7},{7,6},{8,9},{9,8},{10,11... | collective-permute-start | bytes 589832 | tf_op jit(solution)/shard_map/ppermute | solution.py:131
  10.2 16.1 %collective-permute-start.3 = (bf16[96,2432]{1,0:T(8,128)(2,1)}, bf16[96,2432]{1,0:T(8,128)(2,1)S(1)}, u32[]{:S(2)}, u32[]{:S(2)}) collective-permute-start(bf16[96,2432]{1,0:T(8,128)(2,1)} %bitcast.19), channel_id=1, source_target_pairs={{0,4},{1,17},{2,6},{3,19},{4,0},{5,21},{6,2},{7,23},{8,12},{9,25},... | collective-permute-start | bytes 1400840 | tf_op jit(solution)/shard_map/ppermute | solution.py:131
  12.1 14.2 %collective-permute-start.2 = (bf16[96,2432]{1,0:T(8,128)(2,1)}, bf16[96,2432]{1,0:T(8,128)(2,1)}, u32[]{:S(2)}, u32[]{:S(2)}) collective-permute-start(bf16[96,2432]{1,0:T(8,128)(2,1)} %bitcast.20), channel_id=1, source_target_pairs={{0,6},{1,25},{2,0},{3,27},{4,2},{5,29},{6,4},{7,31},{8,14},{9,1},{... | collective-permute-start | bytes 1400840 | tf_op jit(solution)/shard_map/ppermute | solution.py:131
  14.1 12.6 %collective-permute-start.1 = (bf16[96,2432]{1,0:T(8,128)(2,1)}, bf16[96,2432]{1,0:T(8,128)(2,1)}, u32[]{:S(2)}, u32[]{:S(2)}) collective-permute-start(bf16[96,2432]{1,0:T(8,128)(2,1)} %bitcast.21), channel_id=1, source_target_pairs={{0,2},{1,9},{2,4},{3,11},{4,6},{5,13},{6,0},{7,15},{8,10},{9,17},{... | collective-permute-start | bytes 1400840 | tf_op jit(solution)/shard_map/ppermute | solution.py:131
  18.3 11.4 %all-to-all-start = ((bf16[4,2,64,384]{3,2,1,0:T(8,128)(2,1)}), bf16[4,2,64,384]{3,2,1,0:T(8,128)(2,1)S(1)}, u32[]{:S(2)}, u32[]{:S(2)}) async-start(bf16[4,2,64,384]{3,2,1,0:T(8,128)(2,1)} %pad_maximum_fusion), calls=%async_computation | async-start | bytes 786432 | tf_op jit(solution)/shard_map/all_to_all | solution.py:134
  21.9 0.8 copy-start.4
  25.0 0.6 copy-start.5
  25.6 0.6 copy-start.7
  29.7 0.7 copy-start.6
  51.4 31.1 %copy-start.8 = (s32[4]{0:T(128)S(1)}, s32[4]{0:T(128)}, u32[]{:S(2)}) copy-start(s32[4]{0:T(128)} %copy-done.7) | copy-start | bytes 52
  54.5 47.8 %copy-start.2 = (bf16[2048,96]{0,1:T(8,128)(2,1)S(1)}, bf16[2048,96]{0,1:T(8,128)(2,1)}, u32[]{:S(2)}) copy-start(bf16[2048,96]{0,1:T(8,128)(2,1)} %param.7) | copy-start | bytes 1179652

commit v6 on v5

v6 whole, which is shorter than its diff:
```python
import functools

import jax
import jax.numpy as jnp
from jax import lax
from jax.experimental import pallas as pl
from jax.experimental.pallas import tpu as pltpu
from jax.sharding import PartitionSpec as P

BLK = 128
SIDE = 4
CORES = 2
BF = jnp.bfloat16
F32 = jnp.float32
R4 = range(SIDE)


def at(x, y, core):
    return ((x % SIDE) * SIDE + y % SIDE) * CORES + core


ALL = [(x, y, c) for x in R4 for y in R4 for c in range(CORES)]
CROSS = [[at(x, y, 0) for x in R4] for y in R4] + [[at(x, y, 1) for y in R4] for x in R4]
PLANE = [[at(x, y, c) for x in R4 for y in R4] for c in range(CORES)]
PAIRS = [[at(x, y, c) for c in range(CORES)] for x in R4 for y in R4]


def along(k):
    return [(at(x, y, c), at(x, y + k, c) if c == 0 else at(x + k, y, c)) for x, y, c in ALL]


def halve(core, both, out):
    size = out.shape[1]
    for c in range(CORES):

        @pl.when(core[0] == c)
        def _(start=c * (both.shape[2] - size)):
            out[...] = jnp.concatenate([both[i, :, start : start + size] for i in range(CORES)], axis=0)


def pack(core, w, out):
    span = w.shape[2] // SIDE
    piece = span // SIDE
    cols = jnp.concatenate([w[0], w[1]], axis=0)

    @pl.when(core[0] == 0)
    def _():
        for a in R4:
            out[a] = cols[:, a * span : (a + 1) * span]

    @pl.when(core[0] == 1)
    def _():
        for a in R4:
            starts = [(b * SIDE + a) * piece for b in R4]
            out[a] = jnp.concatenate([cols[:, s : s + piece] for s in starts], axis=1)


def prepare(blocks_dev, pos, lists, maps, idx, src, mine, sem):
    head, frame = pos[0], pos[1]
    copy = pltpu.make_async_copy(maps.at[head, 0], mine, sem)
    copy.start()
    for q in range(idx.shape[0]):
        place = jnp.int32(0)
        for s in range(lists.shape[1]):
            local = lists[head, s, q] - frame * blocks_dev
            place = jnp.where((local >= 0) & (local < blocks_dev), local, place)
        idx[q] = place
    for s in range(lists.shape[1]):
        src[s] = lax.div(lists[head, s, frame], jnp.int32(blocks_dev))
    copy.wait()


def project(pos, idx, wall, *rest):
    chunks, (out, gath) = rest[:-2], rest[-2:]
    for i, chunk in enumerate(chunks):
        rows = chunk.shape[0]
        gath[pl.ds(pl.multiple_of(pos[i] * rows, rows), rows), :] = chunk[...]
    w = wall[...].reshape(-1, wall.shape[2])
    out[...] = jnp.dot(w, gath[...], preferred_element_type=F32).astype(BF).reshape(out.shape)


def fold(first, core, idx, part, own, oth, vals):
    total = part[0].astype(F32)
    for a in R4[1:]:
        total += part[a].astype(F32)
    vals[...] = total.astype(BF)
    width = own.shape[1]
    mine = pl.ds(pl.multiple_of(core[0] * width, width), width)
    theirs = pl.ds(pl.multiple_of((1 - core[0]) * width, width), width)
    last = vals.shape[1] // BLK - 1
    for q in range(own.shape[0]):
        block = jnp.clip(idx[q] - core[0] * first, 0, last)
        at_q = pl.ds(pl.multiple_of(block * BLK, BLK), BLK)
        own[q] = vals[mine, at_q]
        oth[q] = vals[theirs, at_q]


def merge(half, core, idx, own, pair, out):
    for q in range(out.shape[0]):
        here = (idx[q] < half) == (core[0] == 0)

        @pl.when(here)
        def _(q=q):
            out[q] = own[q]

        @pl.when(jnp.logical_not(here))
        def _(q=q):
            out[q] = pair[1 - core[0], q]


def attend(src, got, maps, out):
    acc = jnp.zeros(out.shape[1:], F32)
    for s in range(maps.shape[0]):
        acc += lax.dot_general(
            got[src[s]], maps[s], (((1,), (1,)), ((), ())), preferred_element_type=F32
        )
    acc = acc.astype(BF)
    for k in range(out.shape[0]):
        out[k] = acc


def output(attn, w, out):
    rows = [attn[c, chip] for chip in range(attn.shape[1]) for c in range(CORES)]
    out[...] = jnp.dot(w[...], jnp.concatenate(rows, axis=0), preferred_element_type=F32).astype(BF)


def hold(xs):
    whole = [pl.BlockSpec(memory_space=pl.ANY)] * len(xs)
    return pl.pallas_call(
        lambda *refs: None,
        out_shape=[jax.ShapeDtypeStruct(x.shape, x.dtype) for x in xs],
        in_specs=whole,
        out_specs=whole,
        input_output_aliases={i: i for i in range(len(xs))},
        cost_estimate=pl.CostEstimate(flops=2 * 10**10, bytes_accessed=10**7, transcendentals=0),
        compiler_params=limit(1),
        name="hold",
    )(*xs)


def vmem(n):
    return [pl.BlockSpec(memory_space=pltpu.VMEM)] * n


def smem(n):
    return [pl.BlockSpec(memory_space=pltpu.SMEM)] * n


def limit(mib):
    return pltpu.CompilerParams(vmem_limit_bytes=mib * 2**20)


def body(features, w_value, w_out, maps, lists):
    kv_rows, feat = features.shape
    width = w_value.shape[1]
    chan = lax.axis_index("chan")
    frame = lax.axis_index("frame")
    x, y, core = chan // (SIDE * CORES), chan // CORES % SIDE, chan % CORES
    b = jnp.where(core == 0, y, x)
    head = chan // CORES

    def send(v, perm):
        return lax.ppermute(v, "chan", perm)

    def trade(v, groups):
        return lax.all_to_all(v, "chan", 0, 0, axis_index_groups=groups, tiled=True)

    def pair(v):
        return lax.all_gather(v, "chan", axis_index_groups=PAIRS)

    blocks_dev = kv_rows // BLK
    half = (blocks_dev + 1) // CORES
    one = core.reshape(1).astype(jnp.int32)
    both = pl.pallas_call(
        halve,
        out_shape=jax.ShapeDtypeStruct((CORES * feat, half * BLK), BF),
        in_specs=smem(1) + vmem(1),
        out_specs=vmem(1)[0],
        compiler_params=limit(4),
        name="halve",
    )(one, pair(features.T))
    chunks = [both, *hold([send(both, along(k)) for k in (1, 3, 2)])]
    pos = jnp.stack([lax.rem(b + SIDE - k, SIDE) for k in (0, 1, 3, 2)]).astype(jnp.int32)

    wall = pl.pallas_call(
        pack,
        out_shape=jax.ShapeDtypeStruct((SIDE, CORES * width, SIDE * CORES * feat), BF),
        in_specs=smem(1) + vmem(1),
        out_specs=vmem(1)[0],
        compiler_params=limit(4),
        name="pack",
    )(one, pair(w_value.T))
    wall = trade(wall, CROSS)

    queries, slots = lists.shape[1:]
    idx, src, my_maps = pl.pallas_call(
        functools.partial(prepare, blocks_dev),
        out_shape=(
            jax.ShapeDtypeStruct((queries,), jnp.int32),
            jax.ShapeDtypeStruct((slots,), jnp.int32),
            jax.ShapeDtypeStruct((slots, BLK, BLK), BF),
        ),
        in_specs=smem(2) + [pl.BlockSpec(memory_space=pltpu.HBM)],
        out_specs=smem(2) + vmem(1),
        scratch_shapes=[pltpu.SemaphoreType.DMA],
        compiler_params=limit(4),
        name="prepare",
    )(jnp.stack([head, frame]).astype(jnp.int32), lists.transpose(0, 2, 1), maps)

    part = pl.pallas_call(
        project,
        out_shape=jax.ShapeDtypeStruct((SIDE, CORES * width, half * BLK), BF),
        in_specs=smem(1) + [pl.BlockSpec(memory_space=pl.ANY)] + vmem(5),
        out_specs=vmem(1)[0],
        scratch_shapes=[pltpu.VMEM((SIDE * CORES * feat, half * BLK), BF)],
        compiler_params=limit(20),
        name="project",
    )(pos, idx, wall, *chunks)
    part = trade(part, CROSS)
    side = jax.ShapeDtypeStruct((queries, width, BLK), BF)
    own, oth = pl.pallas_call(
        functools.partial(fold, blocks_dev - half),
        out_shape=(side, side),
        in_specs=smem(2) + vmem(1),
        out_specs=vmem(2),
        scratch_shapes=[pltpu.VMEM((CORES * width, half * BLK), BF)],
        compiler_params=limit(8),
        name="fold",
    )(one, idx, part)
    blocks = pl.pallas_call(
        functools.partial(merge, half),
        out_shape=side,
        in_specs=smem(2) + vmem(2),
        out_specs=vmem(1)[0],
        compiler_params=limit(4),
        name="merge",
    )(one, idx, own, pair(oth))
    got = lax.all_to_all(blocks, "frame", 0, 0, tiled=True)
    attn = pl.pallas_call(
        attend,
        out_shape=jax.ShapeDtypeStruct((SIDE * SIDE, width, BLK), BF),
        in_specs=smem(1) + vmem(2),
        out_specs=vmem(1)[0],
        compiler_params=limit(4),
        name="attend",
    )(src, got, my_maps)
    attn = pair(trade(attn, PLANE))
    mixed = pl.pallas_call(
        output,
        out_shape=jax.ShapeDtypeStruct((w_out.shape[1], BLK), BF),
        in_specs=vmem(2),
        out_specs=vmem(1)[0],
        compiler_params=limit(4),
        name="output",
    )(attn, w_out.T)
    return mixed.T


def solution(mesh):
    in_specs = (
        P("frame", "chan"),
        P(None, "chan"),
        P(None, "chan"),
        P(None, "frame", None, None, None),
        P(),
    )
    return jax.shard_map(body, mesh=mesh, in_specs=in_specs, out_specs=P("frame", "chan"), check_vma=False)
```

time: 104 us -> 103 us (level)
  starting transfers between devices: 19.5 us -> 12.9 us
  blocking collectives: 67.8 us -> 74 us
  local copies, waits for them, and re-layouts: 3.77 us -> 0.02 us
  waiting for transfers between devices: 3.37 us -> 6.33 us
  Pallas kernels: 7.68 us -> 9.2 us
    all_gather x2 -> x4, blocking collectives: 11.3 us -> 23.6 us  [pair(): return lax.all_gather(v, 'chan', axis_index_groups=PAIRS)]
    ppermute x4 -> x3, starting transfers between devices: 16 us -> 8.42 us  [send(): return lax.ppermute(v, 'chan', perm)]
    all_to_all x2, blocking collectives: 28.6 us -> 24.2 us  [trade(): return lax.all_to_all(v, 'chan', 0, 0, axis_index_groups=groups, tiled=True)]
    unnamed x18 -> x8, local copies, waits for them, and re-layouts: 3.77 us -> 0.02 us
    all_to_all x1, waiting for transfers between devices: 3.04 us -> 6.32 us  [trade(): return lax.all_to_all(v, 'chan', 0, 0, axis_index_groups=groups, tiled=True)]
    all_to_all x1, blocking collectives: 27.8 us -> 26.1 us  [body(): got = lax.all_to_all(blocks, 'frame', 0, 0, tiled=True)]
    pallas_call x5 -> x7, Pallas kernels: 6.06 us -> 7.58 us  [the longest x1 2.65 us: body(): pl.pallas_call(project, out_shape=jax.ShapeDtypeStruct((SIDE, CORES * wid...]
    all_to_all x1, starting transfers between devices: 3.46 us -> 4.51 us  [trade(): return lax.all_to_all(v, 'chan', 0, 0, axis_index_groups=groups, tiled=True)]
  transfers between devices with their start and end apart: 5 -> 4, of which waited for: 2 -> 1; matrix products, arithmetic and copies ran while one was open for 1% -> 0% of each run, Pallas kernels for 2% -> 3%
where the time goes in v6:
time: 103 us
  blocking collectives  74 us (72%)
  starting transfers between devices  12.9 us (13%)
  Pallas kernels  9.2 us (9%)
  waiting for transfers between devices  6.33 us (6%)
    all_to_all x1, blocking collectives, body(): got = lax.all_to_all(blocks, 'frame', 0, 0, tiled=True)  26.1 us
    all_to_all x2, blocking collectives, trade(): return lax.all_to_all(v, 'chan', 0, 0, axis_index_groups=groups, tiled=True)  24.2 us
    all_gather x4, blocking collectives, pair(): return lax.all_gather(v, 'chan', axis_index_groups=PAIRS)  23.6 us
    ppermute x3, starting transfers between devices, send(): return lax.ppermute(v, 'chan', perm)  8.42 us
    all_to_all x1, waiting for transfers between devices, trade(): return lax.all_to_all(v, 'chan', 0, 0, axis_index_groups=groups, tiled=True)  6.32 us
    all_to_all x1, starting transfers between devices, trade(): return lax.all_to_all(v, 'chan', 0, 0, axis_index_groups=groups, tiled=True)  4.51 us
    pallas_call x1, Pallas kernels, body(): pl.pallas_call(project, out_shape=jax.ShapeDtypeStruct((SIDE, CORES * wid...  2.65 us
  transfers between devices with their start and end apart: 4, of which 1 were waited for; matrix products, arithmetic and copies ran while one was open for 0% of the time, Pallas kernels for 3%

profile of v6, /device:TPU:1, one launch (start us, length us, event | category | flops | bytes accessed | tf_op | source)
XLA Modules:
  0.0 102.7 jit_solution(10369735257407853828)
XLA Ops:
  0.0 0.0 copy-start.3
  0.0 9.3 %all-gather.1 = bf16[192,2432]{1,0:T(8,128)(2,1)S(1)} all-gather(bf16[96,2432]{1,0:T(8,128)(2,1)} %bitcast.22), channel_id=3, replica_groups={{0,1},{2,3},{4,5},{6,7},{8,9},{10,11},{12,13},{14,15},{16,17},{18,19},{..., dimensions={0}, use_global_device_ids=true | all-gather | bytes 1400832 | tf_op jit(solution)/shard_map/all_gather | solution.py:169
  9.3 1.9 %collective-permute-start = (bf16[192,1280]{1,0:T(8,128)(2,1)S(1)}, bf16[192,1280]{1,0:T(8,128)(2,1)}, u32[]{:S(2)}, u32[]{:S(2)}) collective-permute-start(bf16[192,1280]{1,0:T(8,128)(2,1)S(1)} %halve.1.rest_0_), channel_id=1, source_target_pairs={{0,2},{1,9},{2,4},{3,11},{4,6},{5,13},{6,0},{7,15},{8,10},{9,17},{... | collective-permute-start | bytes 1474568 | tf_op jit(solution)/shard_map/ppermute | solution.py:163
  11.3 4.6 %collective-permute-start.1 = (bf16[192,1280]{1,0:T(8,128)(2,1)S(1)}, bf16[192,1280]{1,0:T(8,128)(2,1)}, u32[]{:S(2)}, u32[]{:S(2)}) collective-permute-start(bf16[192,1280]{1,0:T(8,128)(2,1)S(1)} %halve.1.rest_0_), channel_id=1, source_target_pairs={{0,6},{1,25},{2,0},{3,27},{4,2},{5,29},{6,4},{7,31},{8,14},{9,1},{... | collective-permute-start | bytes 1474568 | tf_op jit(solution)/shard_map/ppermute | solution.py:163
  15.9 1.9 %collective-permute-start.2 = (bf16[192,1280]{1,0:T(8,128)(2,1)S(1)}, bf16[192,1280]{1,0:T(8,128)(2,1)}, u32[]{:S(2)}, u32[]{:S(2)}) collective-permute-start(bf16[192,1280]{1,0:T(8,128)(2,1)S(1)} %halve.1.rest_0_), channel_id=1, source_target_pairs={{0,4},{1,17},{2,6},{3,19},{4,0},{5,21},{6,2},{7,23},{8,12},{9,25},... | collective-permute-start | bytes 1474568 | tf_op jit(solution)/shard_map/ppermute | solution.py:163
  17.8 0.0 copy-done.3
  17.8 2.9 %all-gather = bf16[128,3072]{1,0:T(8,128)(2,1)S(1)} all-gather(bf16[64,3072]{1,0:T(8,128)(2,1)S(1)} %bitcast.23), channel_id=2, replica_groups={{0,1},{2,3},{4,5},{6,7},{8,9},{10,11},{12,13},{14,15},{16,17},{18,19},{..., dimensions={0}, use_global_device_ids=true | all-gather | bytes 1179648 | tf_op jit(solution)/shard_map/all_gather | solution.py:169
  20.7 0.0 copy-start
  20.7 0.0 copy-start.2
  20.7 1.2 %pack.1 = bf16[4,128,768]{2,1,0:T(8,128)(2,1)} custom-call(s32[1]{0:T(128)} %bitcast.3.core, bf16[2,64,3072]{2,1,0:T(8,128)(2,1)S(1)} %bitcast.17), custom_call_target="tpu_custom_call" | custom-call | tf_op jit(solution)/shard_map/pack/pallas_call | solution.py:185
  21.9 4.5 %all-to-all-start = ((bf16[4,128,768]{2,1,0:T(8,128)(2,1)}), bf16[4,128,768]{2,1,0:T(8,128)(2,1)S(1)}, u32[]{:S(2)}, u32[]{:S(2)}) async-start(bf16[4,128,768]{2,1,0:T(8,128)(2,1)} %pack.1), calls=%async_computation | async-start | bytes 1572864 | tf_op jit(solution)/shard_map/all_to_all | solution.py:166
  26.4 0.1 pad_add_fusion.pos
  26.5 0.0 copy-done
  26.5 0.0 copy-done.2
  26.5 2.0 %prepare.1 = (s32[16]{0:T(128)S(1)}, s32[4]{0:T(128)S(1)}, bf16[4,128,128]{2,1,0:T(8,128)(2,1)S(1)}) custom-call(s32[2]{0:T(128)S(1)} %pad_add_fusion.pos, s32[16,4,16]{2,1,0:T(4,128)S(1)} %bitcast.21, bf16[16,1,4,128,128]{4,3,2,1,0:T(8,128)(2,1)S(1)} %copy-done), custom_call_target="tpu_custom_call" | custom-call | tf_op jit(solution)/shard_map/prepare/pallas_call | solution.py:196
  28.5 0.1 pad_add_fusion.1.pos
  28.6 0.0 collective-permute-done.refs_0_
  28.6 0.0 collective-permute-done.1.refs_1_
  28.6 0.0 collective-permute-done.2.refs_2_
  28.6 6.3 %all-to-all-done.wall = bf16[4,128,768]{2,1,0:T(8,128)(2,1)S(1)} async-done(((bf16[4,128,768]{2,1,0:T(8,128)(2,1)}), bf16[4,128,768]{2,1,0:T(8,128)(2,1)S(1)}, u32[]{:S(2)}, u32[]{:S(2)}) %all-to-all-start) | async-done | bytes 786464 | tf_op jit(solution)/shard_map/all_to_all | solution.py:166
  34.9 2.7 %project.1 = bf16[4,128,1280]{2,1,0:T(8,128)(2,1)S(1)} custom-call(s32[4]{0:T(128)S(1)} %pad_add_fusion.1.pos, s32[16]{0:T(128)S(1)} %get-tuple-element.14.idx, bf16[4,128,768]{2,1,0:T(8,128)(2,1)S(1)} %all-to-all-done.wall, bf16[192,1280]{1,0:T(8,128)(2,1)S(1)} %halve.1.rest_0_, bf16[192,1280]{1,0:T(8,128)(2,1)} %get-tuple-element.15.rest_1_, ...), custom_call_target="tpu_custom_call" | custom-call | tf_op jit(solution)/shard_map/project/pallas_call | solution.py:210
  37.6 13.9 %all_to_all.20.part = bf16[4,128,1280]{2,1,0:T(8,128)(2,1)S(1)} all-to-all(bf16[4,128,1280]{2,1,0:T(8,128)(2,1)S(1)} %project.1), channel_id=1, replica_groups={{0,8,16,24},{2,10,18,26},{4,12,20,28},{6,14,22,30},{1,3,5,7},{9,11,13,1..., dimensions={0} | all-to-all | bytes 2621440 | tf_op jit(solution)/shard_map/all_to_all | solution.py:166
  51.5 0.9 fold.1
  52.4 3.1 %all-gather.2 = bf16[32,64,128]{2,1,0:T(8,128)(2,1)S(1)} all-gather(bf16[16,64,128]{2,1,0:T(8,128)(2,1)S(1)} %get-tuple-element.19), channel_id=4, replica_groups={{0,1},{2,3},{4,5},{6,7},{8,9},{10,11},{12,13},{14,15},{16,17},{18,19},{..., dimensions={0}, use_global_device_ids=true | all-gather | bytes 786432 | tf_op jit(solution)/shard_map/all_gather | solution.py:169
  55.5 0.8 merge.1
  56.3 0.0 copy-start.1
  56.3 26.1 %all_to_all.21.got = bf16[16,64,128]{2,1,0:T(8,128)(2,1)S(1)} all-to-all(bf16[16,64,128]{2,1,0:T(8,128)(2,1)S(1)} %merge.1), channel_id=1, replica_groups=mesh['frame'=16,'chan'=32] {'frame'}, dimensions={0} | all-to-all | bytes 524288 | tf_op jit(solution)/shard_map/all_to_all | solution.py:238
  82.4 0.8 attend.1
  83.1 10.4 %all_to_all.22 = bf16[16,64,128]{2,1,0:T(8,128)(2,1)S(1)} all-to-all(bf16[16,64,128]{2,1,0:T(8,128)(2,1)S(1)} %attend.1), channel_id=1, replica_groups={{0,2,4,6,8,10,12,14,16,18,20,22,24,26,28,30},{1,3,5,7,9,11,13,15,17,19,..., dimensions={0} | all-to-all | bytes 524288 | tf_op jit(solution)/shard_map/all_to_all | solution.py:166
  93.5 8.3 %all-gather.3 = bf16[32,64,128]{2,1,0:T(8,128)(2,1)S(1)} all-gather(bf16[16,64,128]{2,1,0:T(8,128)(2,1)S(1)} %all_to_all.22), channel_id=5, replica_groups={{0,1},{2,3},{4,5},{6,7},{8,9},{10,11},{12,13},{14,15},{16,17},{18,19},{..., dimensions={0}, use_global_device_ids=true | all-gather | bytes 786432 | tf_op jit(solution)/shard_map/all_gather | solution.py:169
  101.8 0.0 copy-done.1
  101.8 0.9 output.1
  (2 shorter events, 0.0 us)
Async XLA Ops:
  0.0 17.8 %copy-start.3 = (bf16[3072,64]{0,1:T(8,128)(2,1)S(1)}, bf16[3072,64]{0,1:T(8,128)(2,1)}, u32[]{:S(2)}) copy-start(bf16[3072,64]{0,1:T(8,128)(2,1)} %param.6) | copy-start | bytes 1179652
  9.3 19.2 %collective-permute-start = (bf16[192,1280]{1,0:T(8,128)(2,1)S(1)}, bf16[192,1280]{1,0:T(8,128)(2,1)}, u32[]{:S(2)}, u32[]{:S(2)}) collective-permute-start(bf16[192,1280]{1,0:T(8,128)(2,1)S(1)} %halve.1.rest_0_), channel_id=1, source_target_pairs={{0,2},{1,9},{2,4},{3,11},{4,6},{5,13},{6,0},{7,15},{8,10},{9,17},{... | collective-permute-start | bytes 1474568 | tf_op jit(solution)/shard_map/ppermute | solution.py:163
  11.3 17.3 %collective-permute-start.1 = (bf16[192,1280]{1,0:T(8,128)(2,1)S(1)}, bf16[192,1280]{1,0:T(8,128)(2,1)}, u32[]{:S(2)}, u32[]{:S(2)}) collective-permute-start(bf16[192,1280]{1,0:T(8,128)(2,1)S(1)} %halve.1.rest_0_), channel_id=1, source_target_pairs={{0,6},{1,25},{2,0},{3,27},{4,2},{5,29},{6,4},{7,31},{8,14},{9,1},{... | collective-permute-start | bytes 1474568 | tf_op jit(solution)/shard_map/ppermute | solution.py:163
  15.9 12.7 %collective-permute-start.2 = (bf16[192,1280]{1,0:T(8,128)(2,1)S(1)}, bf16[192,1280]{1,0:T(8,128)(2,1)}, u32[]{:S(2)}, u32[]{:S(2)}) collective-permute-start(bf16[192,1280]{1,0:T(8,128)(2,1)S(1)} %halve.1.rest_0_), channel_id=1, source_target_pairs={{0,4},{1,17},{2,6},{3,19},{4,0},{5,21},{6,2},{7,23},{8,12},{9,25},... | collective-permute-start | bytes 1474568 | tf_op jit(solution)/shard_map/ppermute | solution.py:163
  20.7 5.7 %copy-start = (bf16[16,1,4,128,128]{4,3,2,1,0:T(8,128)(2,1)S(1)}, bf16[16,1,4,128,128]{4,3,2,1,0:T(8,128)(2,1)}, u32[]{:S(2)}) copy-start(bf16[16,1,4,128,128]{4,3,2,1,0:T(8,128)(2,1)} %maps.1) | copy-start | bytes 6291460
  20.7 5.7 %copy-start.2 = (s32[16,16,4]{1,2,0:T(4,128)S(1)}, s32[16,16,4]{1,2,0:T(4,128)}, u32[]{:S(2)}) copy-start(s32[16,16,4]{1,2,0:T(4,128)} %param.9) | copy-start | bytes 12292
  21.9 13.0 %all-to-all-start = ((bf16[4,128,768]{2,1,0:T(8,128)(2,1)}), bf16[4,128,768]{2,1,0:T(8,128)(2,1)S(1)}, u32[]{:S(2)}, u32[]{:S(2)}) async-start(bf16[4,128,768]{2,1,0:T(8,128)(2,1)} %pack.1), calls=%async_computation | async-start | bytes 1572864 | tf_op jit(solution)/shard_map/all_to_all | solution.py:166
  56.3 45.6 %copy-start.1 = (bf16[2048,96]{0,1:T(8,128)(2,1)S(1)}, bf16[2048,96]{0,1:T(8,128)(2,1)}, u32[]{:S(2)}) copy-start(bf16[2048,96]{0,1:T(8,128)(2,1)} %param.7) | copy-start | bytes 1179652

commit v7 on v6

--- a/solution.py
+++ b/solution.py
@@ -79,33 +79,25 @@
     out[...] = jnp.dot(w, gath[...], preferred_element_type=F32).astype(BF).reshape(out.shape)
 
 
-def fold(first, core, idx, part, own, oth, vals):
+def fold(blocks_dev, core, idx, part, own, oth, vals):
     total = part[0].astype(F32)
     for a in R4[1:]:
         total += part[a].astype(F32)
     vals[...] = total.astype(BF)
     width = own.shape[1]
+    half = vals.shape[1] // BLK
     mine = pl.ds(pl.multiple_of(core[0] * width, width), width)
     theirs = pl.ds(pl.multiple_of((1 - core[0]) * width, width), width)
-    last = vals.shape[1] // BLK - 1
     for q in range(own.shape[0]):
-        block = jnp.clip(idx[q] - core[0] * first, 0, last)
+        here = (idx[q] < half) == (core[0] == 0)
+        block = jnp.clip(idx[q] - core[0] * (blocks_dev - half), 0, half - 1)
         at_q = pl.ds(pl.multiple_of(block * BLK, BLK), BLK)
-        own[q] = vals[mine, at_q]
-        oth[q] = vals[theirs, at_q]
-
-
-def merge(half, core, idx, own, pair, out):
-    for q in range(out.shape[0]):
-        here = (idx[q] < half) == (core[0] == 0)
-
-        @pl.when(here)
-        def _(q=q):
-            out[q] = own[q]
-
-        @pl.when(jnp.logical_not(here))
-        def _(q=q):
-            out[q] = pair[1 - core[0], q]
+        own[q] = jnp.where(here, vals[mine, at_q], jnp.zeros((), BF))
+        oth[q] = jnp.where(here, vals[theirs, at_q], jnp.zeros((), BF))
+
+
+def merge(core, own, pair, out):
+    out[...] = own[...] + pair[1 - core[0]]
 
 
 def attend(src, got, maps, out):
@@ -219,7 +211,7 @@
     part = trade(part, CROSS)
     side = jax.ShapeDtypeStruct((queries, width, BLK), BF)
     own, oth = pl.pallas_call(
-        functools.partial(fold, blocks_dev - half),
+        functools.partial(fold, blocks_dev),
         out_shape=(side, side),
         in_specs=smem(2) + vmem(1),
         out_specs=vmem(2),
@@ -228,13 +220,13 @@
         name="fold",
     )(one, idx, part)
     blocks = pl.pallas_call(
-        functools.partial(merge, half),
+        merge,
         out_shape=side,
-        in_specs=smem(2) + vmem(2),
+        in_specs=smem(1) + vmem(2),
         out_specs=vmem(1)[0],
         compiler_params=limit(4),
         name="merge",
-    )(one, idx, own, pair(oth))
+    )(one, own, pair(oth))
     got = lax.all_to_all(blocks, "frame", 0, 0, tiled=True)
     attn = pl.pallas_call(
         attend,

time: 103 us -> 102 us (level)
  no operation moved by 1% of the time
where the time goes in v7:
time: 102 us
  blocking collectives  74 us (73%)
  starting transfers between devices  12.9 us (13%)
  Pallas kernels  8.51 us (8%)
  waiting for transfers between devices  6.33 us (6%)
    all_to_all x1, blocking collectives, body(): got = lax.all_to_all(blocks, 'frame', 0, 0, tiled=True)  26.1 us
    all_to_all x2, blocking collectives, trade(): return lax.all_to_all(v, 'chan', 0, 0, axis_index_groups=groups, tiled=True)  24.2 us
    all_gather x4, blocking collectives, pair(): return lax.all_gather(v, 'chan', axis_index_groups=PAIRS)  23.7 us
    ppermute x3, starting transfers between devices, send(): return lax.ppermute(v, 'chan', perm)  8.42 us
    all_to_all x1, waiting for transfers between devices, trade(): return lax.all_to_all(v, 'chan', 0, 0, axis_index_groups=groups, tiled=True)  6.32 us
    all_to_all x1, starting transfers between devices, trade(): return lax.all_to_all(v, 'chan', 0, 0, axis_index_groups=groups, tiled=True)  4.51 us
    pallas_call x1, Pallas kernels, body(): pl.pallas_call(project, out_shape=jax.ShapeDtypeStruct((SIDE, CORES * wid...  2.65 us
  transfers between devices with their start and end apart: 4, of which 1 were waited for; matrix products, arithmetic and copies ran while one was open for 0% of the time, Pallas kernels for 3%

profile of v7, /device:TPU:1, one launch (start us, length us, event | category | flops | bytes accessed | tf_op | source)
XLA Modules:
  0.0 102.0 jit_solution(7832139193635671580)
XLA Ops:
  0.0 0.0 copy-start.3
  0.0 9.3 %all-gather.1 = bf16[192,2432]{1,0:T(8,128)(2,1)S(1)} all-gather(bf16[96,2432]{1,0:T(8,128)(2,1)} %bitcast.22), channel_id=3, replica_groups={{0,1},{2,3},{4,5},{6,7},{8,9},{10,11},{12,13},{14,15},{16,17},{18,19},{..., dimensions={0}, use_global_device_ids=true | all-gather | bytes 1400832 | tf_op jit(solution)/shard_map/all_gather | solution.py:161
  9.3 1.9 %collective-permute-start = (bf16[192,1280]{1,0:T(8,128)(2,1)S(1)}, bf16[192,1280]{1,0:T(8,128)(2,1)}, u32[]{:S(2)}, u32[]{:S(2)}) collective-permute-start(bf16[192,1280]{1,0:T(8,128)(2,1)S(1)} %halve.1.rest_0_), channel_id=1, source_target_pairs={{0,2},{1,9},{2,4},{3,11},{4,6},{5,13},{6,0},{7,15},{8,10},{9,17},{... | collective-permute-start | bytes 1474568 | tf_op jit(solution)/shard_map/ppermute | solution.py:155
  11.3 4.6 %collective-permute-start.1 = (bf16[192,1280]{1,0:T(8,128)(2,1)S(1)}, bf16[192,1280]{1,0:T(8,128)(2,1)}, u32[]{:S(2)}, u32[]{:S(2)}) collective-permute-start(bf16[192,1280]{1,0:T(8,128)(2,1)S(1)} %halve.1.rest_0_), channel_id=1, source_target_pairs={{0,6},{1,25},{2,0},{3,27},{4,2},{5,29},{6,4},{7,31},{8,14},{9,1},{... | collective-permute-start | bytes 1474568 | tf_op jit(solution)/shard_map/ppermute | solution.py:155
  15.9 1.9 %collective-permute-start.2 = (bf16[192,1280]{1,0:T(8,128)(2,1)S(1)}, bf16[192,1280]{1,0:T(8,128)(2,1)}, u32[]{:S(2)}, u32[]{:S(2)}) collective-permute-start(bf16[192,1280]{1,0:T(8,128)(2,1)S(1)} %halve.1.rest_0_), channel_id=1, source_target_pairs={{0,4},{1,17},{2,6},{3,19},{4,0},{5,21},{6,2},{7,23},{8,12},{9,25},... | collective-permute-start | bytes 1474568 | tf_op jit(solution)/shard_map/ppermute | solution.py:155
  17.8 0.0 copy-done.3
  17.8 2.9 %all-gather = bf16[128,3072]{1,0:T(8,128)(2,1)S(1)} all-gather(bf16[64,3072]{1,0:T(8,128)(2,1)S(1)} %bitcast.23), channel_id=2, replica_groups={{0,1},{2,3},{4,5},{6,7},{8,9},{10,11},{12,13},{14,15},{16,17},{18,19},{..., dimensions={0}, use_global_device_ids=true | all-gather | bytes 1179648 | tf_op jit(solution)/shard_map/all_gather | solution.py:161
  20.7 0.0 copy-start
  20.7 0.0 copy-start.2
  20.7 1.2 %pack.1 = bf16[4,128,768]{2,1,0:T(8,128)(2,1)} custom-call(s32[1]{0:T(128)} %bitcast.3.core, bf16[2,64,3072]{2,1,0:T(8,128)(2,1)S(1)} %bitcast.17), custom_call_target="tpu_custom_call" | custom-call | tf_op jit(solution)/shard_map/pack/pallas_call | solution.py:177
  21.9 4.5 %all-to-all-start = ((bf16[4,128,768]{2,1,0:T(8,128)(2,1)}), bf16[4,128,768]{2,1,0:T(8,128)(2,1)S(1)}, u32[]{:S(2)}, u32[]{:S(2)}) async-start(bf16[4,128,768]{2,1,0:T(8,128)(2,1)} %pack.1), calls=%async_computation | async-start | bytes 1572864 | tf_op jit(solution)/shard_map/all_to_all | solution.py:158
  26.4 0.1 pad_add_fusion.pos
  26.5 0.0 copy-done
  26.5 0.0 copy-done.2
  26.5 2.0 %prepare.1 = (s32[16]{0:T(128)S(1)}, s32[4]{0:T(128)S(1)}, bf16[4,128,128]{2,1,0:T(8,128)(2,1)S(1)}) custom-call(s32[2]{0:T(128)S(1)} %pad_add_fusion.pos, s32[16,4,16]{2,1,0:T(4,128)S(1)} %bitcast.21, bf16[16,1,4,128,128]{4,3,2,1,0:T(8,128)(2,1)S(1)} %copy-done), custom_call_target="tpu_custom_call" | custom-call | tf_op jit(solution)/shard_map/prepare/pallas_call | solution.py:188
  28.5 0.1 pad_add_fusion.1.pos
  28.6 0.0 collective-permute-done.refs_0_
  28.6 0.0 collective-permute-done.1.refs_1_
  28.6 0.0 collective-permute-done.2.refs_2_
  28.6 6.3 %all-to-all-done.wall = bf16[4,128,768]{2,1,0:T(8,128)(2,1)S(1)} async-done(((bf16[4,128,768]{2,1,0:T(8,128)(2,1)}), bf16[4,128,768]{2,1,0:T(8,128)(2,1)S(1)}, u32[]{:S(2)}, u32[]{:S(2)}) %all-to-all-start) | async-done | bytes 786464 | tf_op jit(solution)/shard_map/all_to_all | solution.py:158
  34.9 2.7 %project.1 = bf16[4,128,1280]{2,1,0:T(8,128)(2,1)S(1)} custom-call(s32[4]{0:T(128)S(1)} %pad_add_fusion.1.pos, s32[16]{0:T(128)S(1)} %get-tuple-element.14.idx, bf16[4,128,768]{2,1,0:T(8,128)(2,1)S(1)} %all-to-all-done.wall, bf16[192,1280]{1,0:T(8,128)(2,1)S(1)} %halve.1.rest_0_, bf16[192,1280]{1,0:T(8,128)(2,1)} %get-tuple-element.15.rest_1_, ...), custom_call_target="tpu_custom_call" | custom-call | tf_op jit(solution)/shard_map/project/pallas_call | solution.py:202
  37.6 13.9 %all_to_all.20.part = bf16[4,128,1280]{2,1,0:T(8,128)(2,1)S(1)} all-to-all(bf16[4,128,1280]{2,1,0:T(8,128)(2,1)S(1)} %project.1), channel_id=1, replica_groups={{0,8,16,24},{2,10,18,26},{4,12,20,28},{6,14,22,30},{1,3,5,7},{9,11,13,1..., dimensions={0} | all-to-all | bytes 2621440 | tf_op jit(solution)/shard_map/all_to_all | solution.py:158
  51.5 1.0 fold.1
  52.4 3.1 %all-gather.2 = bf16[32,64,128]{2,1,0:T(8,128)(2,1)S(1)} all-gather(bf16[16,64,128]{2,1,0:T(8,128)(2,1)S(1)} %get-tuple-element.19), channel_id=4, replica_groups={{0,1},{2,3},{4,5},{6,7},{8,9},{10,11},{12,13},{14,15},{16,17},{18,19},{..., dimensions={0}, use_global_device_ids=true | all-gather | bytes 786432 | tf_op jit(solution)/shard_map/all_gather | solution.py:161
  55.5 0.1 merge.1
  55.6 0.0 copy-start.1
  55.6 26.1 %all_to_all.21.got = bf16[16,64,128]{2,1,0:T(8,128)(2,1)S(1)} all-to-all(bf16[16,64,128]{2,1,0:T(8,128)(2,1)S(1)} %merge.1), channel_id=1, replica_groups=mesh['frame'=16,'chan'=32] {'frame'}, dimensions={0} | all-to-all | bytes 524288 | tf_op jit(solution)/shard_map/all_to_all | solution.py:230
  81.6 0.8 attend.1
  82.4 10.4 %all_to_all.22 = bf16[16,64,128]{2,1,0:T(8,128)(2,1)S(1)} all-to-all(bf16[16,64,128]{2,1,0:T(8,128)(2,1)S(1)} %attend.1), channel_id=1, replica_groups={{0,2,4,6,8,10,12,14,16,18,20,22,24,26,28,30},{1,3,5,7,9,11,13,15,17,19,..., dimensions={0} | all-to-all | bytes 524288 | tf_op jit(solution)/shard_map/all_to_all | solution.py:158
  92.8 8.4 %all-gather.3 = bf16[32,64,128]{2,1,0:T(8,128)(2,1)S(1)} all-gather(bf16[16,64,128]{2,1,0:T(8,128)(2,1)S(1)} %all_to_all.22), channel_id=5, replica_groups={{0,1},{2,3},{4,5},{6,7},{8,9},{10,11},{12,13},{14,15},{16,17},{18,19},{..., dimensions={0}, use_global_device_ids=true | all-gather | bytes 786432 | tf_op jit(solution)/shard_map/all_gather | solution.py:161
  101.1 0.0 copy-done.1
  101.1 0.9 output.1
  (2 shorter events, 0.0 us)
Async XLA Ops:
  0.0 17.8 %copy-start.3 = (bf16[3072,64]{0,1:T(8,128)(2,1)S(1)}, bf16[3072,64]{0,1:T(8,128)(2,1)}, u32[]{:S(2)}) copy-start(bf16[3072,64]{0,1:T(8,128)(2,1)} %param.6) | copy-start | bytes 1179652
  9.3 19.2 %collective-permute-start = (bf16[192,1280]{1,0:T(8,128)(2,1)S(1)}, bf16[192,1280]{1,0:T(8,128)(2,1)}, u32[]{:S(2)}, u32[]{:S(2)}) collective-permute-start(bf16[192,1280]{1,0:T(8,128)(2,1)S(1)} %halve.1.rest_0_), channel_id=1, source_target_pairs={{0,2},{1,9},{2,4},{3,11},{4,6},{5,13},{6,0},{7,15},{8,10},{9,17},{... | collective-permute-start | bytes 1474568 | tf_op jit(solution)/shard_map/ppermute | solution.py:155
  11.3 17.3 %collective-permute-start.1 = (bf16[192,1280]{1,0:T(8,128)(2,1)S(1)}, bf16[192,1280]{1,0:T(8,128)(2,1)}, u32[]{:S(2)}, u32[]{:S(2)}) collective-permute-start(bf16[192,1280]{1,0:T(8,128)(2,1)S(1)} %halve.1.rest_0_), channel_id=1, source_target_pairs={{0,6},{1,25},{2,0},{3,27},{4,2},{5,29},{6,4},{7,31},{8,14},{9,1},{... | collective-permute-start | bytes 1474568 | tf_op jit(solution)/shard_map/ppermute | solution.py:155
  15.9 12.7 %collective-permute-start.2 = (bf16[192,1280]{1,0:T(8,128)(2,1)S(1)}, bf16[192,1280]{1,0:T(8,128)(2,1)}, u32[]{:S(2)}, u32[]{:S(2)}) collective-permute-start(bf16[192,1280]{1,0:T(8,128)(2,1)S(1)} %halve.1.rest_0_), channel_id=1, source_target_pairs={{0,4},{1,17},{2,6},{3,19},{4,0},{5,21},{6,2},{7,23},{8,12},{9,25},... | collective-permute-start | bytes 1474568 | tf_op jit(solution)/shard_map/ppermute | solution.py:155
  20.7 5.7 %copy-start = (bf16[16,1,4,128,128]{4,3,2,1,0:T(8,128)(2,1)S(1)}, bf16[16,1,4,128,128]{4,3,2,1,0:T(8,128)(2,1)}, u32[]{:S(2)}) copy-start(bf16[16,1,4,128,128]{4,3,2,1,0:T(8,128)(2,1)} %maps.1) | copy-start | bytes 6291460
  20.7 5.7 %copy-start.2 = (s32[16,16,4]{1,2,0:T(4,128)S(1)}, s32[16,16,4]{1,2,0:T(4,128)}, u32[]{:S(2)}) copy-start(s32[16,16,4]{1,2,0:T(4,128)} %param.9) | copy-start | bytes 12292
  21.9 13.0 %all-to-all-start = ((bf16[4,128,768]{2,1,0:T(8,128)(2,1)}), bf16[4,128,768]{2,1,0:T(8,128)(2,1)S(1)}, u32[]{:S(2)}, u32[]{:S(2)}) async-start(bf16[4,128,768]{2,1,0:T(8,128)(2,1)} %pack.1), calls=%async_computation | async-start | bytes 1572864 | tf_op jit(solution)/shard_map/all_to_all | solution.py:158
  55.6 45.6 %copy-start.1 = (bf16[2048,96]{0,1:T(8,128)(2,1)S(1)}, bf16[2048,96]{0,1:T(8,128)(2,1)}, u32[]{:S(2)}) copy-start(bf16[2048,96]{0,1:T(8,128)(2,1)} %param.7) | copy-start | bytes 1179652

commit v8 on v7

--- a/solution.py
+++ b/solution.py
@@ -13,6 +13,7 @@
 BF = jnp.bfloat16
 F32 = jnp.float32
 R4 = range(SIDE)
+STEPS = (0, 1, 3, 2)
 
 
 def at(x, y, core):
@@ -29,34 +30,42 @@
     return [(at(x, y, c), at(x, y + k, c) if c == 0 else at(x + k, y, c)) for x, y, c in ALL]
 
 
-def halve(core, both, out):
+def here_at():
+    chan = lax.axis_index("chan")
+    head, core = lax.div(chan, CORES), lax.rem(chan, CORES)
+    return core, jnp.where(core == 0, lax.rem(head, SIDE), lax.div(head, SIDE)), head
+
+
+def halve(both, out):
     size = out.shape[1]
+    core = here_at()[0]
     for c in range(CORES):
 
-        @pl.when(core[0] == c)
+        @pl.when(core == c)
         def _(start=c * (both.shape[2] - size)):
             out[...] = jnp.concatenate([both[i, :, start : start + size] for i in range(CORES)], axis=0)
 
 
-def pack(core, w, out):
+def pack(w, out):
     span = w.shape[2] // SIDE
     piece = span // SIDE
     cols = jnp.concatenate([w[0], w[1]], axis=0)
-
-    @pl.when(core[0] == 0)
+    core = here_at()[0]
+
+    @pl.when(core == 0)
     def _():
         for a in R4:
             out[a] = cols[:, a * span : (a + 1) * span]
 
-    @pl.when(core[0] == 1)
+    @pl.when(core == 1)
     def _():
         for a in R4:
             starts = [(b * SIDE + a) * piece for b in R4]
             out[a] = jnp.concatenate([cols[:, s : s + piece] for s in starts], axis=1)
 
 
-def prepare(blocks_dev, pos, lists, maps, idx, src, mine, sem):
-    head, frame = pos[0], pos[1]
+def prepare(blocks_dev, lists, maps, idx, src, mine, sem):
+    head, frame = here_at()[2], lax.axis_index("frame")
     copy = pltpu.make_async_copy(maps.at[head, 0], mine, sem)
     copy.start()
     for q in range(idx.shape[0]):
@@ -70,34 +79,40 @@
     copy.wait()
 
 
-def project(pos, idx, wall, *rest):
+def project(idx, wall, *rest):
     chunks, (out, gath) = rest[:-2], rest[-2:]
-    for i, chunk in enumerate(chunks):
+    b = here_at()[1]
+    for k, chunk in zip(STEPS, chunks):
         rows = chunk.shape[0]
-        gath[pl.ds(pl.multiple_of(pos[i] * rows, rows), rows), :] = chunk[...]
+        start = pl.multiple_of(lax.rem(b + SIDE - k, SIDE) * rows, rows)
+        gath[pl.ds(start, rows), :] = chunk[...]
     w = wall[...].reshape(-1, wall.shape[2])
     out[...] = jnp.dot(w, gath[...], preferred_element_type=F32).astype(BF).reshape(out.shape)
 
 
-def fold(blocks_dev, core, idx, part, own, oth, vals):
+def fold(blocks_dev, idx_from, part, own, oth, vals, idx, sem):
+    fetch = pltpu.make_async_copy(idx_from, idx, sem)
+    fetch.start()
     total = part[0].astype(F32)
     for a in R4[1:]:
         total += part[a].astype(F32)
     vals[...] = total.astype(BF)
+    fetch.wait()
+    core = here_at()[0]
     width = own.shape[1]
     half = vals.shape[1] // BLK
-    mine = pl.ds(pl.multiple_of(core[0] * width, width), width)
-    theirs = pl.ds(pl.multiple_of((1 - core[0]) * width, width), width)
+    mine = pl.ds(pl.multiple_of(core * width, width), width)
+    theirs = pl.ds(pl.multiple_of((1 - core) * width, width), width)
     for q in range(own.shape[0]):
-        here = (idx[q] < half) == (core[0] == 0)
-        block = jnp.clip(idx[q] - core[0] * (blocks_dev - half), 0, half - 1)
+        here = (idx[q] < half) == (core == 0)
+        block = jnp.clip(idx[q] - core * (blocks_dev - half), 0, half - 1)
         at_q = pl.ds(pl.multiple_of(block * BLK, BLK), BLK)
         own[q] = jnp.where(here, vals[mine, at_q], jnp.zeros((), BF))
         oth[q] = jnp.where(here, vals[theirs, at_q], jnp.zeros((), BF))
 
 
-def merge(core, own, pair, out):
-    out[...] = own[...] + pair[1 - core[0]]
+def merge(own, pair, out):
+    out[...] = own[...] + pair[1 - here_at()[0]]
 
 
 def attend(src, got, maps, out):
@@ -145,12 +160,6 @@
 def body(features, w_value, w_out, maps, lists):
     kv_rows, feat = features.shape
     width = w_value.shape[1]
-    chan = lax.axis_index("chan")
-    frame = lax.axis_index("frame")
-    x, y, core = chan // (SIDE * CORES), chan // CORES % SIDE, chan % CORES
-    b = jnp.where(core == 0, y, x)
-    head = chan // CORES
-
     def send(v, perm):
         return lax.ppermute(v, "chan", perm)
 
@@ -162,26 +171,23 @@
 
     blocks_dev = kv_rows // BLK
     half = (blocks_dev + 1) // CORES
-    one = core.reshape(1).astype(jnp.int32)
     both = pl.pallas_call(
         halve,
         out_shape=jax.ShapeDtypeStruct((CORES * feat, half * BLK), BF),
-        in_specs=smem(1) + vmem(1),
+        in_specs=vmem(1),
         out_specs=vmem(1)[0],
         compiler_params=limit(4),
         name="halve",
-    )(one, pair(features.T))
-    chunks = [both, *hold([send(both, along(k)) for k in (1, 3, 2)])]
-    pos = jnp.stack([lax.rem(b + SIDE - k, SIDE) for k in (0, 1, 3, 2)]).astype(jnp.int32)
-
+    )(pair(features.T))
+    chunks = [both, *hold([send(both, along(k)) for k in STEPS[1:]])]
     wall = pl.pallas_call(
         pack,
         out_shape=jax.ShapeDtypeStruct((SIDE, CORES * width, SIDE * CORES * feat), BF),
-        in_specs=smem(1) + vmem(1),
+        in_specs=vmem(1),
         out_specs=vmem(1)[0],
         compiler_params=limit(4),
         name="pack",
-    )(one, pair(w_value.T))
+    )(pair(w_value.T))
     wall = trade(wall, CROSS)
 
     queries, slots = lists.shape[1:]
@@ -192,41 +198,45 @@
             jax.ShapeDtypeStruct((slots,), jnp.int32),
             jax.ShapeDtypeStruct((slots, BLK, BLK), BF),
         ),
-        in_specs=smem(2) + [pl.BlockSpec(memory_space=pltpu.HBM)],
+        in_specs=smem(1) + [pl.BlockSpec(memory_space=pltpu.HBM)],
         out_specs=smem(2) + vmem(1),
         scratch_shapes=[pltpu.SemaphoreType.DMA],
         compiler_params=limit(4),
         name="prepare",
-    )(jnp.stack([head, frame]).astype(jnp.int32), lists.transpose(0, 2, 1), maps)
+    )(lists.transpose(0, 2, 1), maps)
 
     part = pl.pallas_call(
         project,
         out_shape=jax.ShapeDtypeStruct((SIDE, CORES * width, half * BLK), BF),
-        in_specs=smem(1) + [pl.BlockSpec(memory_space=pl.ANY)] + vmem(5),
+        in_specs=[pl.BlockSpec(memory_space=pl.ANY)] + vmem(5),
         out_specs=vmem(1)[0],
         scratch_shapes=[pltpu.VMEM((SIDE * CORES * feat, half * BLK), BF)],
         compiler_params=limit(20),
         name="project",
-    )(pos, idx, wall, *chunks)
+    )(idx, wall, *chunks)
     part = trade(part, CROSS)
     side = jax.ShapeDtypeStruct((queries, width, BLK), BF)
     own, oth = pl.pallas_call(
         functools.partial(fold, blocks_dev),
         out_shape=(side, side),
-        in_specs=smem(2) + vmem(1),
+        in_specs=[pl.BlockSpec(memory_space=pl.ANY)] + vmem(1),
         out_specs=vmem(2),
-        scratch_shapes=[pltpu.VMEM((CORES * width, half * BLK), BF)],
+        scratch_shapes=[
+            pltpu.VMEM((CORES * width, half * BLK), BF),
+            pltpu.SMEM((queries,), jnp.int32),
+            pltpu.SemaphoreType.DMA,
+        ],
         compiler_params=limit(8),
         name="fold",
-    )(one, idx, part)
+    )(idx, part)
     blocks = pl.pallas_call(
         merge,
         out_shape=side,
-        in_specs=smem(1) + vmem(2),
+        in_specs=vmem(2),
         out_specs=vmem(1)[0],
         compiler_params=limit(4),
         name="merge",
-    )(one, own, pair(oth))
+    )(own, pair(oth))
     got = lax.all_to_all(blocks, "frame", 0, 0, tiled=True)
     attn = pl.pallas_call(
         attend,

time: 102 us -> 102 us (level)
  no operation moved by 1% of the time
where the time goes in v8:
time: 102 us
  blocking collectives  74 us (73%)
  starting transfers between devices  12.9 us (13%)
  Pallas kernels  8.17 us (8%)
  waiting for transfers between devices  6.46 us (6%)
    all_to_all x1, blocking collectives, body(): got = lax.all_to_all(blocks, 'frame', 0, 0, tiled=True)  26 us
    all_to_all x2, blocking collectives, trade(): return lax.all_to_all(v, 'chan', 0, 0, axis_index_groups=groups, tiled=True)  24.2 us
    all_gather x4, blocking collectives, pair(): return lax.all_gather(v, 'chan', axis_index_groups=PAIRS)  23.7 us
    ppermute x3, starting transfers between devices, send(): return lax.ppermute(v, 'chan', perm)  8.42 us
    all_to_all x1, waiting for transfers between devices, trade(): return lax.all_to_all(v, 'chan', 0, 0, axis_index_groups=groups, tiled=True)  6.46 us
    all_to_all x1, starting transfers between devices, trade(): return lax.all_to_all(v, 'chan', 0, 0, axis_index_groups=groups, tiled=True)  4.51 us
    pallas_call x1, Pallas kernels, body(): pl.pallas_call(project, out_shape=jax.ShapeDtypeStruct((SIDE, CORES * wid...  2.56 us
  transfers between devices with their start and end apart: 4, of which 1 were waited for; matrix products, arithmetic and copies ran while one was open for 0% of the time, Pallas kernels for 3%

profile of v8, /device:TPU:1, one launch (start us, length us, event | category | flops | bytes accessed | tf_op | source)
XLA Modules:
  0.0 101.7 jit_solution(17267656862320152599)
XLA Ops:
  0.0 0.0 copy-start.3
  0.0 9.3 %all-gather.1 = bf16[192,2432]{1,0:T(8,128)(2,1)S(1)} all-gather(bf16[96,2432]{1,0:T(8,128)(2,1)} %bitcast.15), channel_id=3, replica_groups={{0,1},{2,3},{4,5},{6,7},{8,9},{10,11},{12,13},{14,15},{16,17},{18,19},{..., dimensions={0}, use_global_device_ids=true | all-gather | bytes 1400832 | tf_op jit(solution)/shard_map/all_gather | solution.py:170
  9.3 1.9 %collective-permute-start = (bf16[192,1280]{1,0:T(8,128)(2,1)S(1)}, bf16[192,1280]{1,0:T(8,128)(2,1)}, u32[]{:S(2)}, u32[]{:S(2)}) collective-permute-start(bf16[192,1280]{1,0:T(8,128)(2,1)S(1)} %halve.1.rest_0_), channel_id=1, source_target_pairs={{0,2},{1,9},{2,4},{3,11},{4,6},{5,13},{6,0},{7,15},{8,10},{9,17},{... | collective-permute-start | bytes 1474568 | tf_op jit(solution)/shard_map/ppermute | solution.py:164
  11.3 4.6 %collective-permute-start.1 = (bf16[192,1280]{1,0:T(8,128)(2,1)S(1)}, bf16[192,1280]{1,0:T(8,128)(2,1)}, u32[]{:S(2)}, u32[]{:S(2)}) collective-permute-start(bf16[192,1280]{1,0:T(8,128)(2,1)S(1)} %halve.1.rest_0_), channel_id=1, source_target_pairs={{0,6},{1,25},{2,0},{3,27},{4,2},{5,29},{6,4},{7,31},{8,14},{9,1},{... | collective-permute-start | bytes 1474568 | tf_op jit(solution)/shard_map/ppermute | solution.py:164
  15.9 1.9 %collective-permute-start.2 = (bf16[192,1280]{1,0:T(8,128)(2,1)S(1)}, bf16[192,1280]{1,0:T(8,128)(2,1)}, u32[]{:S(2)}, u32[]{:S(2)}) collective-permute-start(bf16[192,1280]{1,0:T(8,128)(2,1)S(1)} %halve.1.rest_0_), channel_id=1, source_target_pairs={{0,4},{1,17},{2,6},{3,19},{4,0},{5,21},{6,2},{7,23},{8,12},{9,25},... | collective-permute-start | bytes 1474568 | tf_op jit(solution)/shard_map/ppermute | solution.py:164
  17.8 0.0 copy-done.3
  17.8 2.9 %all-gather = bf16[128,3072]{1,0:T(8,128)(2,1)S(1)} all-gather(bf16[64,3072]{1,0:T(8,128)(2,1)S(1)} %bitcast.16), channel_id=2, replica_groups={{0,1},{2,3},{4,5},{6,7},{8,9},{10,11},{12,13},{14,15},{16,17},{18,19},{..., dimensions={0}, use_global_device_ids=true | all-gather | bytes 1179648 | tf_op jit(solution)/shard_map/all_gather | solution.py:170
  20.7 0.0 copy-start
  20.7 0.0 copy-start.2
  20.7 1.2 %pack.1 = bf16[4,128,768]{2,1,0:T(8,128)(2,1)} custom-call(bf16[2,64,3072]{2,1,0:T(8,128)(2,1)S(1)} %bitcast.10), custom_call_target="tpu_custom_call" | custom-call | tf_op jit(solution)/shard_map/pack/pallas_call | solution.py:183
  21.9 4.5 %all-to-all-start = ((bf16[4,128,768]{2,1,0:T(8,128)(2,1)}), bf16[4,128,768]{2,1,0:T(8,128)(2,1)S(1)}, u32[]{:S(2)}, u32[]{:S(2)}) async-start(bf16[4,128,768]{2,1,0:T(8,128)(2,1)} %pack.1), calls=%async_computation | async-start | bytes 1572864 | tf_op jit(solution)/shard_map/all_to_all | solution.py:167
  26.4 0.0 copy-done
  26.4 0.0 copy-done.2
  26.4 2.0 %prepare.1 = (s32[16]{0:T(128)S(1)}, s32[4]{0:T(128)S(1)}, bf16[4,128,128]{2,1,0:T(8,128)(2,1)S(1)}) custom-call(s32[16,4,16]{2,1,0:T(4,128)S(1)} %bitcast.14, bf16[16,1,4,128,128]{4,3,2,1,0:T(8,128)(2,1)S(1)} %copy-done), custom_call_target="tpu_custom_call" | custom-call | tf_op jit(solution)/shard_map/prepare/pallas_call | solution.py:194
  28.4 0.0 collective-permute-done.refs_0_
  28.4 0.0 collective-permute-done.1.refs_1_
  28.4 0.0 collective-permute-done.2.refs_2_
  28.5 6.5 %all-to-all-done.wall = bf16[4,128,768]{2,1,0:T(8,128)(2,1)S(1)} async-done(((bf16[4,128,768]{2,1,0:T(8,128)(2,1)}), bf16[4,128,768]{2,1,0:T(8,128)(2,1)S(1)}, u32[]{:S(2)}, u32[]{:S(2)}) %all-to-all-start) | async-done | bytes 786464 | tf_op jit(solution)/shard_map/all_to_all | solution.py:167
  34.9 2.6 %project.1 = bf16[4,128,1280]{2,1,0:T(8,128)(2,1)S(1)} custom-call(s32[16]{0:T(128)S(1)} %get-tuple-element.14.idx.idx_from, bf16[4,128,768]{2,1,0:T(8,128)(2,1)S(1)} %all-to-all-done.wall, bf16[192,1280]{1,0:T(8,128)(2,1)S(1)} %halve.1.rest_0_, bf16[192,1280]{1,0:T(8,128)(2,1)} %get-tuple-element.15.rest_1_, bf16[192,1280]{1,0:T(8,128)(2,1)} %get-tuple-element.16.rest_2_, ...), custom_call_target="tpu_custom_call" | custom-call | tf_op jit(solution)/shard_map/project/pallas_call | solution.py:208
  37.5 13.9 %all_to_all.20.part = bf16[4,128,1280]{2,1,0:T(8,128)(2,1)S(1)} all-to-all(bf16[4,128,1280]{2,1,0:T(8,128)(2,1)S(1)} %project.1), channel_id=1, replica_groups={{0,8,16,24},{2,10,18,26},{4,12,20,28},{6,14,22,30},{1,3,5,7},{9,11,13,1..., dimensions={0} | all-to-all | bytes 2621440 | tf_op jit(solution)/shard_map/all_to_all | solution.py:167
  51.4 0.7 fold.1
  52.1 3.1 %all-gather.2 = bf16[32,64,128]{2,1,0:T(8,128)(2,1)S(1)} all-gather(bf16[16,64,128]{2,1,0:T(8,128)(2,1)S(1)} %get-tuple-element.19), channel_id=4, replica_groups={{0,1},{2,3},{4,5},{6,7},{8,9},{10,11},{12,13},{14,15},{16,17},{18,19},{..., dimensions={0}, use_global_device_ids=true | all-gather | bytes 786432 | tf_op jit(solution)/shard_map/all_gather | solution.py:170
  55.2 0.1 merge.1
  55.2 0.0 copy-start.1
  55.2 26.0 %all_to_all.21.got = bf16[16,64,128]{2,1,0:T(8,128)(2,1)S(1)} all-to-all(bf16[16,64,128]{2,1,0:T(8,128)(2,1)S(1)} %merge.1), channel_id=1, replica_groups=mesh['frame'=16,'chan'=32] {'frame'}, dimensions={0} | all-to-all | bytes 524288 | tf_op jit(solution)/shard_map/all_to_all | solution.py:240
  81.3 0.8 attend.1
  82.0 10.4 %all_to_all.22 = bf16[16,64,128]{2,1,0:T(8,128)(2,1)S(1)} all-to-all(bf16[16,64,128]{2,1,0:T(8,128)(2,1)S(1)} %attend.1), channel_id=1, replica_groups={{0,2,4,6,8,10,12,14,16,18,20,22,24,26,28,30},{1,3,5,7,9,11,13,15,17,19,..., dimensions={0} | all-to-all | bytes 524288 | tf_op jit(solution)/shard_map/all_to_all | solution.py:167
  92.4 8.4 %all-gather.3 = bf16[32,64,128]{2,1,0:T(8,128)(2,1)S(1)} all-gather(bf16[16,64,128]{2,1,0:T(8,128)(2,1)S(1)} %all_to_all.22), channel_id=5, replica_groups={{0,1},{2,3},{4,5},{6,7},{8,9},{10,11},{12,13},{14,15},{16,17},{18,19},{..., dimensions={0}, use_global_device_ids=true | all-gather | bytes 786432 | tf_op jit(solution)/shard_map/all_gather | solution.py:170
  100.8 0.0 copy-done.1
  100.8 0.9 output.1
  (2 shorter events, 0.0 us)
Async XLA Ops:
  0.0 17.8 %copy-start.3 = (bf16[3072,64]{0,1:T(8,128)(2,1)S(1)}, bf16[3072,64]{0,1:T(8,128)(2,1)}, u32[]{:S(2)}) copy-start(bf16[3072,64]{0,1:T(8,128)(2,1)} %param.6) | copy-start | bytes 1179652
  9.3 19.1 %collective-permute-start = (bf16[192,1280]{1,0:T(8,128)(2,1)S(1)}, bf16[192,1280]{1,0:T(8,128)(2,1)}, u32[]{:S(2)}, u32[]{:S(2)}) collective-permute-start(bf16[192,1280]{1,0:T(8,128)(2,1)S(1)} %halve.1.rest_0_), channel_id=1, source_target_pairs={{0,2},{1,9},{2,4},{3,11},{4,6},{5,13},{6,0},{7,15},{8,10},{9,17},{... | collective-permute-start | bytes 1474568 | tf_op jit(solution)/shard_map/ppermute | solution.py:164
  11.3 17.2 %collective-permute-start.1 = (bf16[192,1280]{1,0:T(8,128)(2,1)S(1)}, bf16[192,1280]{1,0:T(8,128)(2,1)}, u32[]{:S(2)}, u32[]{:S(2)}) collective-permute-start(bf16[192,1280]{1,0:T(8,128)(2,1)S(1)} %halve.1.rest_0_), channel_id=1, source_target_pairs={{0,6},{1,25},{2,0},{3,27},{4,2},{5,29},{6,4},{7,31},{8,14},{9,1},{... | collective-permute-start | bytes 1474568 | tf_op jit(solution)/shard_map/ppermute | solution.py:164
  15.9 12.6 %collective-permute-start.2 = (bf16[192,1280]{1,0:T(8,128)(2,1)S(1)}, bf16[192,1280]{1,0:T(8,128)(2,1)}, u32[]{:S(2)}, u32[]{:S(2)}) collective-permute-start(bf16[192,1280]{1,0:T(8,128)(2,1)S(1)} %halve.1.rest_0_), channel_id=1, source_target_pairs={{0,4},{1,17},{2,6},{3,19},{4,0},{5,21},{6,2},{7,23},{8,12},{9,25},... | collective-permute-start | bytes 1474568 | tf_op jit(solution)/shard_map/ppermute | solution.py:164
  20.7 5.7 %copy-start = (bf16[16,1,4,128,128]{4,3,2,1,0:T(8,128)(2,1)S(1)}, bf16[16,1,4,128,128]{4,3,2,1,0:T(8,128)(2,1)}, u32[]{:S(2)}) copy-start(bf16[16,1,4,128,128]{4,3,2,1,0:T(8,128)(2,1)} %maps.1) | copy-start | bytes 6291460
  20.7 5.7 %copy-start.2 = (s32[16,16,4]{1,2,0:T(4,128)S(1)}, s32[16,16,4]{1,2,0:T(4,128)}, u32[]{:S(2)}) copy-start(s32[16,16,4]{1,2,0:T(4,128)} %param.9) | copy-start | bytes 12292
  21.9 13.0 %all-to-all-start = ((bf16[4,128,768]{2,1,0:T(8,128)(2,1)}), bf16[4,128,768]{2,1,0:T(8,128)(2,1)S(1)}, u32[]{:S(2)}, u32[]{:S(2)}) async-start(bf16[4,128,768]{2,1,0:T(8,128)(2,1)} %pack.1), calls=%async_computation | async-start | bytes 1572864 | tf_op jit(solution)/shard_map/all_to_all | solution.py:167
  55.2 45.6 %copy-start.1 = (bf16[2048,96]{0,1:T(8,128)(2,1)S(1)}, bf16[2048,96]{0,1:T(8,128)(2,1)}, u32[]{:S(2)}) copy-start(bf16[2048,96]{0,1:T(8,128)(2,1)} %param.7) | copy-start | bytes 1179652

commit v9 on v8

--- a/solution.py
+++ b/solution.py
@@ -79,13 +79,16 @@
     copy.wait()
 
 
-def project(idx, wall, *rest):
-    chunks, (out, gath) = rest[:-2], rest[-2:]
+def assemble(*refs):
+    chunks, gath = refs[:-1], refs[-1]
     b = here_at()[1]
     for k, chunk in zip(STEPS, chunks):
         rows = chunk.shape[0]
         start = pl.multiple_of(lax.rem(b + SIDE - k, SIDE) * rows, rows)
         gath[pl.ds(start, rows), :] = chunk[...]
+
+
+def project(idx, wall, gath, out):
     w = wall[...].reshape(-1, wall.shape[2])
     out[...] = jnp.dot(w, gath[...], preferred_element_type=F32).astype(BF).reshape(out.shape)
 
@@ -131,20 +134,6 @@
     out[...] = jnp.dot(w[...], jnp.concatenate(rows, axis=0), preferred_element_type=F32).astype(BF)
 
 
-def hold(xs):
-    whole = [pl.BlockSpec(memory_space=pl.ANY)] * len(xs)
-    return pl.pallas_call(
-        lambda *refs: None,
-        out_shape=[jax.ShapeDtypeStruct(x.shape, x.dtype) for x in xs],
-        in_specs=whole,
-        out_specs=whole,
-        input_output_aliases={i: i for i in range(len(xs))},
-        cost_estimate=pl.CostEstimate(flops=2 * 10**10, bytes_accessed=10**7, transcendentals=0),
-        compiler_params=limit(1),
-        name="hold",
-    )(*xs)
-
-
 def vmem(n):
     return [pl.BlockSpec(memory_space=pltpu.VMEM)] * n
 
@@ -179,7 +168,17 @@
         compiler_params=limit(4),
         name="halve",
     )(pair(features.T))
-    chunks = [both, *hold([send(both, along(k)) for k in STEPS[1:]])]
+    chunks = [both] + [send(both, along(k)) for k in STEPS[1:]]
+    gath = pl.pallas_call(
+        assemble,
+        out_shape=jax.ShapeDtypeStruct((SIDE * CORES * feat, half * BLK), BF),
+        in_specs=vmem(SIDE),
+        out_specs=vmem(1)[0],
+        cost_estimate=pl.CostEstimate(flops=2 * 10**10, bytes_accessed=10**7, transcendentals=0),
+        compiler_params=limit(8),
+        name="assemble",
+    )(*chunks)
+
     wall = pl.pallas_call(
         pack,
         out_shape=jax.ShapeDtypeStruct((SIDE, CORES * width, SIDE * CORES * feat), BF),
@@ -208,12 +207,11 @@
     part = pl.pallas_call(
         project,
         out_shape=jax.ShapeDtypeStruct((SIDE, CORES * width, half * BLK), BF),
-        in_specs=[pl.BlockSpec(memory_space=pl.ANY)] + vmem(5),
-        out_specs=vmem(1)[0],
-        scratch_shapes=[pltpu.VMEM((SIDE * CORES * feat, half * BLK), BF)],
-        compiler_params=limit(20),
+        in_specs=[pl.BlockSpec(memory_space=pl.ANY)] + vmem(2),
+        out_specs=vmem(1)[0],
+        compiler_params=limit(16),
         name="project",
-    )(idx, wall, *chunks)
+    )(idx, wall, gath)
     part = trade(part, CROSS)
     side = jax.ShapeDtypeStruct((queries, width, BLK), BF)
     own, oth = pl.pallas_call(

time: 102 us -> 101 us (level)
  waiting for transfers between devices: 6.46 us -> 4.99 us
    pallas_call x1, Pallas kernels: 0.01 us -> 1.48 us  [body(): pl.pallas_call(assemble, out_shape=jax.ShapeDtypeStruct((SIDE * CORES * f...]
    all_to_all x1, waiting for transfers between devices: 6.46 us -> 4.99 us  [trade(): return lax.all_to_all(v, 'chan', 0, 0, axis_index_groups=groups, tiled=True)]
    pallas_call x1, Pallas kernels: 2.56 us -> 1.18 us  [body(): pl.pallas_call(project, out_shape=jax.ShapeDtypeStruct((SIDE, CORES * wid...]
  transfers between devices with their start and end apart: 4 -> 4, of which waited for: 1 -> 1; matrix products, arithmetic and copies ran while one was open for 0% -> 0% of each run, Pallas kernels for 3% -> 5%
where the time goes in v9:
time: 101 us; the launch traced here: 100 us
  blocking collectives  74.1 us (73%)
  starting transfers between devices  12.9 us (13%)
  Pallas kernels  8.25 us (8%)
  waiting for transfers between devices  4.99 us (5%)
    all_to_all x1, blocking collectives, body(): got = lax.all_to_all(blocks, 'frame', 0, 0, tiled=True)  26 us
    all_to_all x2, blocking collectives, trade(): return lax.all_to_all(v, 'chan', 0, 0, axis_index_groups=groups, tiled=True)  24.2 us
    all_gather x4, blocking collectives, pair(): return lax.all_gather(v, 'chan', axis_index_groups=PAIRS)  23.8 us
    ppermute x3, starting transfers between devices, send(): return lax.ppermute(v, 'chan', perm)  8.42 us
    all_to_all x1, waiting for transfers between devices, trade(): return lax.all_to_all(v, 'chan', 0, 0, axis_index_groups=groups, tiled=True)  4.99 us
    all_to_all x1, starting transfers between devices, trade(): return lax.all_to_all(v, 'chan', 0, 0, axis_index_groups=groups, tiled=True)  4.51 us
  transfers between devices with their start and end apart: 4, of which 1 were waited for; matrix products, arithmetic and copies ran while one was open for 0% of the time, Pallas kernels for 5%

profile of v9, /device:TPU:1, one launch (start us, length us, event | category | flops | bytes accessed | tf_op | source)
XLA Modules:
  0.0 100.4 jit_solution(10924210801880980931)
XLA Ops:
  0.0 0.0 copy-start.3
  0.0 9.3 %all-gather.1 = bf16[192,2432]{1,0:T(8,128)(2,1)S(1)} all-gather(bf16[96,2432]{1,0:T(8,128)(2,1)} %bitcast.15), channel_id=3, replica_groups={{0,1},{2,3},{4,5},{6,7},{8,9},{10,11},{12,13},{14,15},{16,17},{18,19},{..., dimensions={0}, use_global_device_ids=true | all-gather | bytes 1400832 | tf_op jit(solution)/shard_map/all_gather | solution.py:159
  9.3 1.9 %collective-permute-start = (bf16[192,1280]{1,0:T(8,128)(2,1)S(1)}, bf16[192,1280]{1,0:T(8,128)(2,1)}, u32[]{:S(2)}, u32[]{:S(2)}) collective-permute-start(bf16[192,1280]{1,0:T(8,128)(2,1)S(1)} %halve.1.refs_0_), channel_id=1, source_target_pairs={{0,2},{1,9},{2,4},{3,11},{4,6},{5,13},{6,0},{7,15},{8,10},{9,17},{... | collective-permute-start | bytes 1474568 | tf_op jit(solution)/shard_map/ppermute | solution.py:153
  11.3 4.6 %collective-permute-start.1 = (bf16[192,1280]{1,0:T(8,128)(2,1)S(1)}, bf16[192,1280]{1,0:T(8,128)(2,1)}, u32[]{:S(2)}, u32[]{:S(2)}) collective-permute-start(bf16[192,1280]{1,0:T(8,128)(2,1)S(1)} %halve.1.refs_0_), channel_id=1, source_target_pairs={{0,6},{1,25},{2,0},{3,27},{4,2},{5,29},{6,4},{7,31},{8,14},{9,1},{... | collective-permute-start | bytes 1474568 | tf_op jit(solution)/shard_map/ppermute | solution.py:153
  15.9 1.9 %collective-permute-start.2 = (bf16[192,1280]{1,0:T(8,128)(2,1)S(1)}, bf16[192,1280]{1,0:T(8,128)(2,1)}, u32[]{:S(2)}, u32[]{:S(2)}) collective-permute-start(bf16[192,1280]{1,0:T(8,128)(2,1)S(1)} %halve.1.refs_0_), channel_id=1, source_target_pairs={{0,4},{1,17},{2,6},{3,19},{4,0},{5,21},{6,2},{7,23},{8,12},{9,25},... | collective-permute-start | bytes 1474568 | tf_op jit(solution)/shard_map/ppermute | solution.py:153
  17.8 0.0 copy-done.3
  17.8 0.0 copy-start
  17.8 0.0 copy-start.2
  17.8 3.1 %all-gather = bf16[128,3072]{1,0:T(8,128)(2,1)S(1)} all-gather(bf16[64,3072]{1,0:T(8,128)(2,1)S(1)} %bitcast.16), channel_id=2, replica_groups={{0,1},{2,3},{4,5},{6,7},{8,9},{10,11},{12,13},{14,15},{16,17},{18,19},{..., dimensions={0}, use_global_device_ids=true | all-gather | bytes 1179648 | tf_op jit(solution)/shard_map/all_gather | solution.py:159
  20.9 1.1 %pack.1 = bf16[4,128,768]{2,1,0:T(8,128)(2,1)} custom-call(bf16[2,64,3072]{2,1,0:T(8,128)(2,1)S(1)} %bitcast.10), custom_call_target="tpu_custom_call" | custom-call | tf_op jit(solution)/shard_map/pack/pallas_call | solution.py:182
  22.0 4.5 %all-to-all-start = ((bf16[4,128,768]{2,1,0:T(8,128)(2,1)}), bf16[4,128,768]{2,1,0:T(8,128)(2,1)S(1)}, u32[]{:S(2)}, u32[]{:S(2)}) async-start(bf16[4,128,768]{2,1,0:T(8,128)(2,1)} %pack.1), calls=%async_computation | async-start | bytes 1572864 | tf_op jit(solution)/shard_map/all_to_all | solution.py:156
  26.5 0.0 copy-done
  26.5 0.0 copy-done.2
  26.5 2.0 %prepare.1 = (s32[16]{0:T(128)S(1)}, s32[4]{0:T(128)S(1)}, bf16[4,128,128]{2,1,0:T(8,128)(2,1)S(1)}) custom-call(s32[16,4,16]{2,1,0:T(4,128)S(1)} %bitcast.14, bf16[16,1,4,128,128]{4,3,2,1,0:T(8,128)(2,1)S(1)} %copy-done), custom_call_target="tpu_custom_call" | custom-call | tf_op jit(solution)/shard_map/prepare/pallas_call | solution.py:193
  28.6 0.0 collective-permute-done.refs_1_
  28.6 0.0 collective-permute-done.1.refs_2_
  28.6 0.0 collective-permute-done.2.refs_3_
  28.6 1.5 %assemble.1.gath = bf16[768,1280]{1,0:T(8,128)(2,1)S(1)} custom-call(bf16[192,1280]{1,0:T(8,128)(2,1)S(1)} %halve.1.refs_0_, bf16[192,1280]{1,0:T(8,128)(2,1)} %collective-permute-done.refs_1_, bf16[192,1280]{1,0:T(8,128)(2,1)} %collective-permute-done.1.refs_2_, bf16[192,1280]{1,0:T(8,128)(2,1)} %collective-permute-done.2.refs_3_), custom_call_target="tpu_custom_call" | custom-call | flops 20000000000 | bytes 10000000 | tf_op jit(solution)/shard_map/assemble/pallas_call | solution.py:172
  30.1 5.0 %all-to-all-done.wall = bf16[4,128,768]{2,1,0:T(8,128)(2,1)S(1)} async-done(((bf16[4,128,768]{2,1,0:T(8,128)(2,1)}), bf16[4,128,768]{2,1,0:T(8,128)(2,1)S(1)}, u32[]{:S(2)}, u32[]{:S(2)}) %all-to-all-start) | async-done | bytes 786464 | tf_op jit(solution)/shard_map/all_to_all | solution.py:156
  35.1 1.2 %project.1 = bf16[4,128,1280]{2,1,0:T(8,128)(2,1)S(1)} custom-call(s32[16]{0:T(128)S(1)} %get-tuple-element.11.idx.idx_from, bf16[4,128,768]{2,1,0:T(8,128)(2,1)S(1)} %all-to-all-done.wall, bf16[768,1280]{1,0:T(8,128)(2,1)S(1)} %assemble.1.gath), custom_call_target="tpu_custom_call" | custom-call | tf_op jit(solution)/shard_map/project/pallas_call | solution.py:207
  36.2 13.9 %all_to_all.20.part = bf16[4,128,1280]{2,1,0:T(8,128)(2,1)S(1)} all-to-all(bf16[4,128,1280]{2,1,0:T(8,128)(2,1)S(1)} %project.1), channel_id=1, replica_groups={{0,8,16,24},{2,10,18,26},{4,12,20,28},{6,14,22,30},{1,3,5,7},{9,11,13,1..., dimensions={0} | all-to-all | bytes 2621440 | tf_op jit(solution)/shard_map/all_to_all | solution.py:156
  50.1 0.7 fold.1
  50.9 3.1 %all-gather.2 = bf16[32,64,128]{2,1,0:T(8,128)(2,1)S(1)} all-gather(bf16[16,64,128]{2,1,0:T(8,128)(2,1)S(1)} %get-tuple-element.13), channel_id=4, replica_groups={{0,1},{2,3},{4,5},{6,7},{8,9},{10,11},{12,13},{14,15},{16,17},{18,19},{..., dimensions={0}, use_global_device_ids=true | all-gather | bytes 786432 | tf_op jit(solution)/shard_map/all_gather | solution.py:159
  53.9 0.0 copy-start.1
  53.9 0.1 merge.1
  54.0 26.0 %all_to_all.21.got = bf16[16,64,128]{2,1,0:T(8,128)(2,1)S(1)} all-to-all(bf16[16,64,128]{2,1,0:T(8,128)(2,1)S(1)} %merge.1), channel_id=1, replica_groups=mesh['frame'=16,'chan'=32] {'frame'}, dimensions={0} | all-to-all | bytes 524288 | tf_op jit(solution)/shard_map/all_to_all | solution.py:238
  80.0 0.8 attend.1
  80.8 10.4 %all_to_all.22 = bf16[16,64,128]{2,1,0:T(8,128)(2,1)S(1)} all-to-all(bf16[16,64,128]{2,1,0:T(8,128)(2,1)S(1)} %attend.1), channel_id=1, replica_groups={{0,2,4,6,8,10,12,14,16,18,20,22,24,26,28,30},{1,3,5,7,9,11,13,15,17,19,..., dimensions={0} | all-to-all | bytes 524288 | tf_op jit(solution)/shard_map/all_to_all | solution.py:156
  91.1 8.4 %all-gather.3 = bf16[32,64,128]{2,1,0:T(8,128)(2,1)S(1)} all-gather(bf16[16,64,128]{2,1,0:T(8,128)(2,1)S(1)} %all_to_all.22), channel_id=5, replica_groups={{0,1},{2,3},{4,5},{6,7},{8,9},{10,11},{12,13},{14,15},{16,17},{18,19},{..., dimensions={0}, use_global_device_ids=true | all-gather | bytes 786432 | tf_op jit(solution)/shard_map/all_gather | solution.py:159
  99.5 0.0 copy-done.1
  99.5 0.9 output.1
  (1 shorter events, 0.0 us)
Async XLA Ops:
  0.0 17.8 %copy-start.3 = (bf16[3072,64]{0,1:T(8,128)(2,1)S(1)}, bf16[3072,64]{0,1:T(8,128)(2,1)}, u32[]{:S(2)}) copy-start(bf16[3072,64]{0,1:T(8,128)(2,1)} %param.6) | copy-start | bytes 1179652
  9.3 19.2 %collective-permute-start = (bf16[192,1280]{1,0:T(8,128)(2,1)S(1)}, bf16[192,1280]{1,0:T(8,128)(2,1)}, u32[]{:S(2)}, u32[]{:S(2)}) collective-permute-start(bf16[192,1280]{1,0:T(8,128)(2,1)S(1)} %halve.1.refs_0_), channel_id=1, source_target_pairs={{0,2},{1,9},{2,4},{3,11},{4,6},{5,13},{6,0},{7,15},{8,10},{9,17},{... | collective-permute-start | bytes 1474568 | tf_op jit(solution)/shard_map/ppermute | solution.py:153
  11.3 17.3 %collective-permute-start.1 = (bf16[192,1280]{1,0:T(8,128)(2,1)S(1)}, bf16[192,1280]{1,0:T(8,128)(2,1)}, u32[]{:S(2)}, u32[]{:S(2)}) collective-permute-start(bf16[192,1280]{1,0:T(8,128)(2,1)S(1)} %halve.1.refs_0_), channel_id=1, source_target_pairs={{0,6},{1,25},{2,0},{3,27},{4,2},{5,29},{6,4},{7,31},{8,14},{9,1},{... | collective-permute-start | bytes 1474568 | tf_op jit(solution)/shard_map/ppermute | solution.py:153
  15.9 12.7 %collective-permute-start.2 = (bf16[192,1280]{1,0:T(8,128)(2,1)S(1)}, bf16[192,1280]{1,0:T(8,128)(2,1)}, u32[]{:S(2)}, u32[]{:S(2)}) collective-permute-start(bf16[192,1280]{1,0:T(8,128)(2,1)S(1)} %halve.1.refs_0_), channel_id=1, source_target_pairs={{0,4},{1,17},{2,6},{3,19},{4,0},{5,21},{6,2},{7,23},{8,12},{9,25},... | collective-permute-start | bytes 1474568 | tf_op jit(solution)/shard_map/ppermute | solution.py:153
  17.8 8.7 %copy-start = (bf16[16,1,4,128,128]{4,3,2,1,0:T(8,128)(2,1)S(1)}, bf16[16,1,4,128,128]{4,3,2,1,0:T(8,128)(2,1)}, u32[]{:S(2)}) copy-start(bf16[16,1,4,128,128]{4,3,2,1,0:T(8,128)(2,1)} %maps.1) | copy-start | bytes 6291460
  17.8 8.7 %copy-start.2 = (s32[16,16,4]{1,2,0:T(4,128)S(1)}, s32[16,16,4]{1,2,0:T(4,128)}, u32[]{:S(2)}) copy-start(s32[16,16,4]{1,2,0:T(4,128)} %param.9) | copy-start | bytes 12292
  22.0 13.0 %all-to-all-start = ((bf16[4,128,768]{2,1,0:T(8,128)(2,1)}), bf16[4,128,768]{2,1,0:T(8,128)(2,1)S(1)}, u32[]{:S(2)}, u32[]{:S(2)}) async-start(bf16[4,128,768]{2,1,0:T(8,128)(2,1)} %pack.1), calls=%async_computation | async-start | bytes 1572864 | tf_op jit(solution)/shard_map/all_to_all | solution.py:156
  53.9 45.6 %copy-start.1 = (bf16[2048,96]{0,1:T(8,128)(2,1)S(1)}, bf16[2048,96]{0,1:T(8,128)(2,1)}, u32[]{:S(2)}) copy-start(bf16[2048,96]{0,1:T(8,128)(2,1)} %param.7) | copy-start | bytes 1179652

commit v10 on v9

--- a/solution.py
+++ b/solution.py
@@ -13,7 +13,7 @@
 BF = jnp.bfloat16
 F32 = jnp.float32
 R4 = range(SIDE)
-STEPS = (0, 1, 3, 2)
+STEPS = (0, 2, 3, 1)
 
 
 def at(x, y, core):
@@ -36,44 +36,33 @@
     return core, jnp.where(core == 0, lax.rem(head, SIDE), lax.div(head, SIDE)), head
 
 
-def halve(both, out):
-    size = out.shape[1]
+def pack(w, out):
+    feat = w.shape[2] // (SIDE * SIDE * CORES)
+    cols = jnp.concatenate([w[0], w[1]], axis=0)
     core = here_at()[0]
     for c in range(CORES):
 
         @pl.when(core == c)
-        def _(start=c * (both.shape[2] - size)):
-            out[...] = jnp.concatenate([both[i, :, start : start + size] for i in range(CORES)], axis=0)
-
-
-def pack(w, out):
-    span = w.shape[2] // SIDE
-    piece = span // SIDE
-    cols = jnp.concatenate([w[0], w[1]], axis=0)
-    core = here_at()[0]
-
-    @pl.when(core == 0)
-    def _():
-        for a in R4:
-            out[a] = cols[:, a * span : (a + 1) * span]
-
-    @pl.when(core == 1)
-    def _():
-        for a in R4:
-            starts = [(b * SIDE + a) * piece for b in R4]
-            out[a] = jnp.concatenate([cols[:, s : s + piece] for s in starts], axis=1)
+        def _(c=c):
+            for a in R4:
+                chips = [a * SIDE + b if c == 0 else b * SIDE + a for b in R4]
+                starts = [(chip * CORES + c) * feat for chip in chips]
+                out[a] = jnp.concatenate([cols[:, s : s + feat] for s in starts], axis=1)
 
 
 def prepare(blocks_dev, lists, maps, idx, src, mine, sem):
-    head, frame = here_at()[2], lax.axis_index("frame")
+    core, b, head = here_at()
+    frame = lax.axis_index("frame")
     copy = pltpu.make_async_copy(maps.at[head, 0], mine, sem)
     copy.start()
-    for q in range(idx.shape[0]):
-        place = jnp.int32(0)
-        for s in range(lists.shape[1]):
-            local = lists[head, s, q] - frame * blocks_dev
-            place = jnp.where((local >= 0) & (local < blocks_dev), local, place)
-        idx[q] = place
+    for a in R4:
+        partner = jnp.where(core == 0, a * SIDE + b, b * SIDE + a)
+        for q in range(idx.shape[1]):
+            place = jnp.int32(0)
+            for s in range(lists.shape[1]):
+                local = lists[partner, s, q] - frame * blocks_dev
+                place = jnp.where((local >= 0) & (local < blocks_dev), local, place)
+            idx[a, q] = place
     for s in range(lists.shape[1]):
         src[s] = lax.div(lists[head, s, frame], jnp.int32(blocks_dev))
     copy.wait()
@@ -88,34 +77,35 @@
         gath[pl.ds(start, rows), :] = chunk[...]
 
 
-def project(idx, wall, gath, out):
-    w = wall[...].reshape(-1, wall.shape[2])
-    out[...] = jnp.dot(w, gath[...], preferred_element_type=F32).astype(BF).reshape(out.shape)
-
-
-def fold(blocks_dev, idx_from, part, own, oth, vals, idx, sem):
+def project(idx_from, wall, gath, out, vals, idx, sem):
     fetch = pltpu.make_async_copy(idx_from, idx, sem)
     fetch.start()
-    total = part[0].astype(F32)
-    for a in R4[1:]:
-        total += part[a].astype(F32)
-    vals[...] = total.astype(BF)
+    vals[...] = jnp.dot(wall[...].reshape(-1, wall.shape[2]), gath[...], preferred_element_type=F32).astype(BF)
     fetch.wait()
+    rows = out.shape[2]
+    for a in R4:
+        for q in range(out.shape[1]):
+            start = pl.multiple_of(idx[a, q] * BLK, BLK)
+            out[a, q] = vals[a * rows : (a + 1) * rows, pl.ds(start, BLK)]
+
+
+def fold(part, own, oth):
+    width = own.shape[1]
     core = here_at()[0]
-    width = own.shape[1]
-    half = vals.shape[1] // BLK
-    mine = pl.ds(pl.multiple_of(core * width, width), width)
-    theirs = pl.ds(pl.multiple_of((1 - core) * width, width), width)
-    for q in range(own.shape[0]):
-        here = (idx[q] < half) == (core == 0)
-        block = jnp.clip(idx[q] - core * (blocks_dev - half), 0, half - 1)
-        at_q = pl.ds(pl.multiple_of(block * BLK, BLK), BLK)
-        own[q] = jnp.where(here, vals[mine, at_q], jnp.zeros((), BF))
-        oth[q] = jnp.where(here, vals[theirs, at_q], jnp.zeros((), BF))
+    for c in range(CORES):
+
+        @pl.when(core == c)
+        def _(c=c):
+            for q in range(own.shape[0]):
+                total = part[0, q].astype(F32)
+                for a in R4[1:]:
+                    total += part[a, q].astype(F32)
+                own[q] = total[c * width : (c + 1) * width]
+                oth[q] = total[(1 - c) * width : (2 - c) * width].astype(BF)
 
 
 def merge(own, pair, out):
-    out[...] = own[...] + pair[1 - here_at()[0]]
+    out[...] = (own[...] + pair[1 - here_at()[0]].astype(F32)).astype(BF)
 
 
 def attend(src, got, maps, out):
@@ -159,19 +149,11 @@
         return lax.all_gather(v, "chan", axis_index_groups=PAIRS)
 
     blocks_dev = kv_rows // BLK
-    half = (blocks_dev + 1) // CORES
-    both = pl.pallas_call(
-        halve,
-        out_shape=jax.ShapeDtypeStruct((CORES * feat, half * BLK), BF),
-        in_specs=vmem(1),
-        out_specs=vmem(1)[0],
-        compiler_params=limit(4),
-        name="halve",
-    )(pair(features.T))
-    chunks = [both] + [send(both, along(k)) for k in STEPS[1:]]
+    ft = features.T
+    chunks = [ft] + [send(ft, along(k)) for k in STEPS[1:]]
     gath = pl.pallas_call(
         assemble,
-        out_shape=jax.ShapeDtypeStruct((SIDE * CORES * feat, half * BLK), BF),
+        out_shape=jax.ShapeDtypeStruct((SIDE * feat, kv_rows), BF),
         in_specs=vmem(SIDE),
         out_specs=vmem(1)[0],
         cost_estimate=pl.CostEstimate(flops=2 * 10**10, bytes_accessed=10**7, transcendentals=0),
@@ -181,7 +163,7 @@
 
     wall = pl.pallas_call(
         pack,
-        out_shape=jax.ShapeDtypeStruct((SIDE, CORES * width, SIDE * CORES * feat), BF),
+        out_shape=jax.ShapeDtypeStruct((SIDE, CORES * width, SIDE * feat), BF),
         in_specs=vmem(1),
         out_specs=vmem(1)[0],
         compiler_params=limit(4),
@@ -193,7 +175,7 @@
     idx, src, my_maps = pl.pallas_call(
         functools.partial(prepare, blocks_dev),
         out_shape=(
-            jax.ShapeDtypeStruct((queries,), jnp.int32),
+            jax.ShapeDtypeStruct((SIDE, queries), jnp.int32),
             jax.ShapeDtypeStruct((slots,), jnp.int32),
             jax.ShapeDtypeStruct((slots, BLK, BLK), BF),
         ),
@@ -206,27 +188,27 @@
 
     part = pl.pallas_call(
         project,
-        out_shape=jax.ShapeDtypeStruct((SIDE, CORES * width, half * BLK), BF),
+        out_shape=jax.ShapeDtypeStruct((SIDE, queries, CORES * width, BLK), BF),
         in_specs=[pl.BlockSpec(memory_space=pl.ANY)] + vmem(2),
         out_specs=vmem(1)[0],
-        compiler_params=limit(16),
+        scratch_shapes=[
+            pltpu.VMEM((SIDE * CORES * width, kv_rows), BF),
+            pltpu.SMEM((SIDE, queries), jnp.int32),
+            pltpu.SemaphoreType.DMA,
+        ],
+        compiler_params=limit(20),
         name="project",
     )(idx, wall, gath)
     part = trade(part, CROSS)
     side = jax.ShapeDtypeStruct((queries, width, BLK), BF)
     own, oth = pl.pallas_call(
-        functools.partial(fold, blocks_dev),
-        out_shape=(side, side),
-        in_specs=[pl.BlockSpec(memory_space=pl.ANY)] + vmem(1),
+        fold,
+        out_shape=(jax.ShapeDtypeStruct(side.shape, F32), side),
+        in_specs=vmem(1),
         out_specs=vmem(2),
-        scratch_shapes=[
-            pltpu.VMEM((CORES * width, half * BLK), BF),
-            pltpu.SMEM((queries,), jnp.int32),
-            pltpu.SemaphoreType.DMA,
-        ],
         compiler_params=limit(8),
         name="fold",
-    )(idx, part)
+    )(part)
     blocks = pl.pallas_call(
         merge,
         out_shape=side,

time: 101 us -> 101 us (level)
  waiting for transfers between devices: 4.99 us -> 2.39 us
  starting transfers between devices: 12.9 us -> 15.4 us
    all_gather x4 -> x3, blocking collectives: 23.8 us -> 18.7 us  [pair(): return lax.all_gather(v, 'chan', axis_index_groups=PAIRS)]
    all_to_all x2, blocking collectives: 24.2 us -> 28.5 us  [trade(): return lax.all_to_all(v, 'chan', 0, 0, axis_index_groups=groups, tiled=True)]
    all_to_all x1, waiting for transfers between devices: 4.99 us -> 2.38 us  [trade(): return lax.all_to_all(v, 'chan', 0, 0, axis_index_groups=groups, tiled=True)]
    ppermute x3, starting transfers between devices: 8.42 us -> 10.9 us  [send(): return lax.ppermute(v, 'chan', perm)]
    pallas_call x4 -> x3, Pallas kernels: 3.43 us -> 3.63 us  [the longest x1 1.92 us: body(): pl.pallas_call(project, out_shape=jax.ShapeDtypeStruct((SIDE, queries, CO...]
where the time goes in v10:
time: 101 us; the launch traced here: 100 us
  blocking collectives  73.6 us (73%)
  starting transfers between devices  15.4 us (15%)
  Pallas kernels  8.72 us (9%)
  waiting for transfers between devices  2.39 us (2%)
    all_to_all x2, blocking collectives, trade(): return lax.all_to_all(v, 'chan', 0, 0, axis_index_groups=groups, tiled=True)  28.5 us
    all_to_all x1, blocking collectives, body(): got = lax.all_to_all(blocks, 'frame', 0, 0, tiled=True)  26.3 us
    all_gather x3, blocking collectives, pair(): return lax.all_gather(v, 'chan', axis_index_groups=PAIRS)  18.7 us
    ppermute x3, starting transfers between devices, send(): return lax.ppermute(v, 'chan', perm)  10.9 us
    all_to_all x1, starting transfers between devices, trade(): return lax.all_to_all(v, 'chan', 0, 0, axis_index_groups=groups, tiled=True)  4.51 us
    pallas_call x1, Pallas kernels, body(): pl.pallas_call(functools.partial(prepare, blocks_dev), out_shape=(jax.Sha...  2.4 us
    all_to_all x1, waiting for transfers between devices, trade(): return lax.all_to_all(v, 'chan', 0, 0, axis_index_groups=groups, tiled=True)  2.38 us
  transfers between devices with their start and end apart: 4, of which 1 were waited for; matrix products, arithmetic and copies ran while one was open for 0% of the time, Pallas kernels for 5%

profile of v10, /device:TPU:1, one launch (start us, length us, event | category | flops | bytes accessed | tf_op | source)
XLA Modules:
  0.0 100.2 jit_solution(10905607482617077776)
XLA Ops:
  0.0 0.0 copy-start.2
  0.0 0.0 copy-start
  0.0 4.1 %collective-permute-start.2 = (bf16[96,2432]{1,0:T(8,128)(2,1)}, bf16[96,2432]{1,0:T(8,128)(2,1)}, u32[]{:S(2)}, u32[]{:S(2)}) collective-permute-start(bf16[96,2432]{1,0:T(8,128)(2,1)} %bitcast.13), channel_id=1, source_target_pairs={{0,2},{1,9},{2,4},{3,11},{4,6},{5,13},{6,0},{7,15},{8,10},{9,17},{... | collective-permute-start | bytes 1400840 | tf_op jit(solution)/shard_map/ppermute | solution.py:143
  4.1 3.2 %collective-permute-start.1 = (bf16[96,2432]{1,0:T(8,128)(2,1)}, bf16[96,2432]{1,0:T(8,128)(2,1)}, u32[]{:S(2)}, u32[]{:S(2)}) collective-permute-start(bf16[96,2432]{1,0:T(8,128)(2,1)} %bitcast.14), channel_id=1, source_target_pairs={{0,6},{1,25},{2,0},{3,27},{4,2},{5,29},{6,4},{7,31},{8,14},{9,1},{... | collective-permute-start | bytes 1400840 | tf_op jit(solution)/shard_map/ppermute | solution.py:143
  7.3 3.6 %collective-permute-start = (bf16[96,2432]{1,0:T(8,128)(2,1)}, bf16[96,2432]{1,0:T(8,128)(2,1)}, u32[]{:S(2)}, u32[]{:S(2)}) collective-permute-start(bf16[96,2432]{1,0:T(8,128)(2,1)} %bitcast.15), channel_id=1, source_target_pairs={{0,4},{1,17},{2,6},{3,19},{4,0},{5,21},{6,2},{7,23},{8,12},{9,25},... | collective-permute-start | bytes 1400840 | tf_op jit(solution)/shard_map/ppermute | solution.py:143
  10.9 7.3 %all-gather = bf16[128,3072]{1,0:T(8,128)(2,1)S(1)} all-gather(bf16[64,3072]{1,0:T(8,128)(2,1)} %bitcast.17), channel_id=2, replica_groups={{0,1},{2,3},{4,5},{6,7},{8,9},{10,11},{12,13},{14,15},{16,17},{18,19},{..., dimensions={0}, use_global_device_ids=true | all-gather | bytes 1179648 | tf_op jit(solution)/shard_map/all_gather | solution.py:149
  18.2 0.0 copy-start.3
  18.2 1.0 %pack.1 = bf16[4,128,384]{2,1,0:T(8,128)(2,1)} custom-call(bf16[2,64,3072]{2,1,0:T(8,128)(2,1)S(1)} %bitcast.8), custom_call_target="tpu_custom_call" | custom-call | tf_op jit(solution)/shard_map/pack/pallas_call | solution.py:164
  19.2 4.5 %all-to-all-start = ((bf16[4,128,384]{2,1,0:T(8,128)(2,1)}), bf16[4,128,384]{2,1,0:T(8,128)(2,1)S(1)}, u32[]{:S(2)}, u32[]{:S(2)}) async-start(bf16[4,128,384]{2,1,0:T(8,128)(2,1)} %pack.1), calls=%async_computation | async-start | bytes 786432 | tf_op jit(solution)/shard_map/all_to_all | solution.py:146
  23.7 0.0 copy-done.2
  23.7 0.0 copy-done
  23.8 2.4 %prepare.1 = (s32[4,16]{1,0:T(4,128)S(1)}, s32[4]{0:T(128)S(1)}, bf16[4,128,128]{2,1,0:T(8,128)(2,1)S(1)}) custom-call(s32[16,4,16]{2,1,0:T(4,128)S(1)} %bitcast.12, bf16[16,1,4,128,128]{4,3,2,1,0:T(8,128)(2,1)S(1)} %copy-done), custom_call_target="tpu_custom_call" | custom-call | tf_op jit(solution)/shard_map/prepare/pallas_call | solution.py:175
  26.2 0.0 collective-permute-done.2.refs_3_
  26.2 0.0 collective-permute-done.1.refs_2_
  26.2 0.0 collective-permute-done.refs_1_
  26.2 0.0 copy-done.3
  26.2 1.5 %assemble.1.gath = bf16[384,2432]{1,0:T(8,128)(2,1)S(1)} custom-call(bf16[96,2432]{1,0:T(8,128)(2,1)S(1)} %bitcast.16, bf16[96,2432]{1,0:T(8,128)(2,1)} %collective-permute-done.refs_1_, bf16[96,2432]{1,0:T(8,128)(2,1)} %collective-permute-done.1.refs_2_, bf16[96,2432]{1,0:T(8,128)(2,1)} %collective-permute-done.2.refs_3_), custom_call_target="tpu_custom_call" | custom-call | flops 20000000000 | bytes 10000000 | tf_op jit(solution)/shard_map/assemble/pallas_call | solution.py:154
  27.7 2.4 %all-to-all-done.wall = bf16[4,128,384]{2,1,0:T(8,128)(2,1)S(1)} async-done(((bf16[4,128,384]{2,1,0:T(8,128)(2,1)}), bf16[4,128,384]{2,1,0:T(8,128)(2,1)S(1)}, u32[]{:S(2)}, u32[]{:S(2)}) %all-to-all-start) | async-done | bytes 393248 | tf_op jit(solution)/shard_map/all_to_all | solution.py:146
  30.0 1.9 %project.1 = bf16[4,16,128,128]{3,2,1,0:T(8,128)(2,1)S(1)} custom-call(s32[4,16]{1,0:T(4,128)S(1)} %get-tuple-element.11.idx_from, bf16[4,128,384]{2,1,0:T(8,128)(2,1)S(1)} %all-to-all-done.wall, bf16[384,2432]{1,0:T(8,128)(2,1)S(1)} %assemble.1.gath), custom_call_target="tpu_custom_call" | custom-call | tf_op jit(solution)/shard_map/project/pallas_call | solution.py:189
  32.0 18.1 %all_to_all.20.part = bf16[4,16,128,128]{3,2,1,0:T(8,128)(2,1)S(1)} all-to-all(bf16[4,16,128,128]{3,2,1,0:T(8,128)(2,1)S(1)} %project.1), channel_id=1, replica_groups={{0,8,16,24},{2,10,18,26},{4,12,20,28},{6,14,22,30},{1,3,5,7},{9,11,13,1..., dimensions={0} | all-to-all | bytes 4194304 | tf_op jit(solution)/shard_map/all_to_all | solution.py:146
  50.1 0.2 fold.1
  50.4 3.1 %all-gather.1 = bf16[32,64,128]{2,1,0:T(8,128)(2,1)S(1)} all-gather(bf16[16,64,128]{2,1,0:T(8,128)(2,1)S(1)} %get-tuple-element.13), channel_id=3, replica_groups={{0,1},{2,3},{4,5},{6,7},{8,9},{10,11},{12,13},{14,15},{16,17},{18,19},{..., dimensions={0}, use_global_device_ids=true | all-gather | bytes 786432 | tf_op jit(solution)/shard_map/all_gather | solution.py:149
  53.4 0.0 copy-start.1
  53.5 26.3 %all_to_all.21.got = bf16[16,64,128]{2,1,0:T(8,128)(2,1)S(1)} all-to-all(bf16[16,64,128]{2,1,0:T(8,128)(2,1)S(1)} %merge.1), channel_id=1, replica_groups=mesh['frame'=16,'chan'=32] {'frame'}, dimensions={0} | all-to-all | bytes 524288 | tf_op jit(solution)/shard_map/all_to_all | solution.py:220
  79.8 0.8 attend.1
  80.5 10.4 %all_to_all.22 = bf16[16,64,128]{2,1,0:T(8,128)(2,1)S(1)} all-to-all(bf16[16,64,128]{2,1,0:T(8,128)(2,1)S(1)} %attend.1), channel_id=1, replica_groups={{0,2,4,6,8,10,12,14,16,18,20,22,24,26,28,30},{1,3,5,7,9,11,13,15,17,19,..., dimensions={0} | all-to-all | bytes 524288 | tf_op jit(solution)/shard_map/all_to_all | solution.py:146
  90.9 8.4 %all-gather.2 = bf16[32,64,128]{2,1,0:T(8,128)(2,1)S(1)} all-gather(bf16[16,64,128]{2,1,0:T(8,128)(2,1)S(1)} %all_to_all.22), channel_id=4, replica_groups={{0,1},{2,3},{4,5},{6,7},{8,9},{10,11},{12,13},{14,15},{16,17},{18,19},{..., dimensions={0}, use_global_device_ids=true | all-gather | bytes 786432 | tf_op jit(solution)/shard_map/all_gather | solution.py:149
  99.3 0.0 copy-done.1
  99.3 0.9 output.1
  (1 shorter events, 0.0 us)
Async XLA Ops:
  0.0 23.7 %copy-start.2 = (s32[16,16,4]{1,2,0:T(4,128)S(1)}, s32[16,16,4]{1,2,0:T(4,128)}, u32[]{:S(2)}) copy-start(s32[16,16,4]{1,2,0:T(4,128)} %param.9) | copy-start | bytes 12292
  0.0 23.7 %copy-start = (bf16[16,1,4,128,128]{4,3,2,1,0:T(8,128)(2,1)S(1)}, bf16[16,1,4,128,128]{4,3,2,1,0:T(8,128)(2,1)}, u32[]{:S(2)}) copy-start(bf16[16,1,4,128,128]{4,3,2,1,0:T(8,128)(2,1)} %maps.1) | copy-start | bytes 6291460
  0.0 26.2 %collective-permute-start.2 = (bf16[96,2432]{1,0:T(8,128)(2,1)}, bf16[96,2432]{1,0:T(8,128)(2,1)}, u32[]{:S(2)}, u32[]{:S(2)}) collective-permute-start(bf16[96,2432]{1,0:T(8,128)(2,1)} %bitcast.13), channel_id=1, source_target_pairs={{0,2},{1,9},{2,4},{3,11},{4,6},{5,13},{6,0},{7,15},{8,10},{9,17},{... | collective-permute-start | bytes 1400840 | tf_op jit(solution)/shard_map/ppermute | solution.py:143
  4.1 22.1 %collective-permute-start.1 = (bf16[96,2432]{1,0:T(8,128)(2,1)}, bf16[96,2432]{1,0:T(8,128)(2,1)}, u32[]{:S(2)}, u32[]{:S(2)}) collective-permute-start(bf16[96,2432]{1,0:T(8,128)(2,1)} %bitcast.14), channel_id=1, source_target_pairs={{0,6},{1,25},{2,0},{3,27},{4,2},{5,29},{6,4},{7,31},{8,14},{9,1},{... | collective-permute-start | bytes 1400840 | tf_op jit(solution)/shard_map/ppermute | solution.py:143
  7.3 18.9 %collective-permute-start = (bf16[96,2432]{1,0:T(8,128)(2,1)}, bf16[96,2432]{1,0:T(8,128)(2,1)}, u32[]{:S(2)}, u32[]{:S(2)}) collective-permute-start(bf16[96,2432]{1,0:T(8,128)(2,1)} %bitcast.15), channel_id=1, source_target_pairs={{0,4},{1,17},{2,6},{3,19},{4,0},{5,21},{6,2},{7,23},{8,12},{9,25},... | collective-permute-start | bytes 1400840 | tf_op jit(solution)/shard_map/ppermute | solution.py:143
  18.2 8.0 %copy-start.3 = (bf16[2432,96]{0,1:T(8,128)(2,1)S(1)}, bf16[2432,96]{0,1:T(8,128)(2,1)}, u32[]{:S(2)}) copy-start(bf16[2432,96]{0,1:T(8,128)(2,1)} %param.5) | copy-start | bytes 1400836
  19.2 10.8 %all-to-all-start = ((bf16[4,128,384]{2,1,0:T(8,128)(2,1)}), bf16[4,128,384]{2,1,0:T(8,128)(2,1)S(1)}, u32[]{:S(2)}, u32[]{:S(2)}) async-start(bf16[4,128,384]{2,1,0:T(8,128)(2,1)} %pack.1), calls=%async_computation | async-start | bytes 786432 | tf_op jit(solution)/shard_map/all_to_all | solution.py:146
  53.4 45.9 %copy-start.1 = (bf16[2048,96]{0,1:T(8,128)(2,1)S(1)}, bf16[2048,96]{0,1:T(8,128)(2,1)}, u32[]{:S(2)}) copy-start(bf16[2048,96]{0,1:T(8,128)(2,1)} %param.7) | copy-start | bytes 1179652

commit v11 on v10

--- a/solution.py
+++ b/solution.py
@@ -13,7 +13,7 @@
 BF = jnp.bfloat16
 F32 = jnp.float32
 R4 = range(SIDE)
-STEPS = (0, 2, 3, 1)
+STEPS = (0, 3, 2, 1)
 
 
 def at(x, y, core):

time: 101 us -> 100 us (0.990)
  no operation moved by 1% of the time
where the time goes in v11:
time: 100 us
  blocking collectives  73.2 us (73%)
  starting transfers between devices  15.4 us (15%)
  Pallas kernels  8.72 us (9%)
  waiting for transfers between devices  2.62 us (3%)
    all_to_all x2, blocking collectives, trade(): return lax.all_to_all(v, 'chan', 0, 0, axis_index_groups=groups, tiled=True)  27.9 us
    all_to_all x1, blocking collectives, body(): got = lax.all_to_all(blocks, 'frame', 0, 0, tiled=True)  26.9 us
    all_gather x3, blocking collectives, pair(): return lax.all_gather(v, 'chan', axis_index_groups=PAIRS)  18.4 us
    ppermute x3, starting transfers between devices, send(): return lax.ppermute(v, 'chan', perm)  11.5 us
    all_to_all x1, starting transfers between devices, trade(): return lax.all_to_all(v, 'chan', 0, 0, axis_index_groups=groups, tiled=True)  3.9 us
    all_to_all x1, waiting for transfers between devices, trade(): return lax.all_to_all(v, 'chan', 0, 0, axis_index_groups=groups, tiled=True)  2.61 us
    pallas_call x1, Pallas kernels, body(): pl.pallas_call(functools.partial(prepare, blocks_dev), out_shape=(jax.Sha...  2.4 us
  transfers between devices with their start and end apart: 4, of which 1 were waited for; matrix products, arithmetic and copies ran while one was open for 0% of the time, Pallas kernels for 5%

profile of v11, /device:TPU:1, one launch (start us, length us, event | category | flops | bytes accessed | tf_op | source)
XLA Modules:
  0.0 100.1 jit_solution(1927920138117891836)
XLA Ops:
  0.0 0.0 copy-start.2
  0.0 0.0 copy-start
  0.0 4.1 %collective-permute-start.2 = (bf16[96,2432]{1,0:T(8,128)(2,1)}, bf16[96,2432]{1,0:T(8,128)(2,1)}, u32[]{:S(2)}, u32[]{:S(2)}) collective-permute-start(bf16[96,2432]{1,0:T(8,128)(2,1)} %bitcast.13), channel_id=1, source_target_pairs={{0,2},{1,9},{2,4},{3,11},{4,6},{5,13},{6,0},{7,15},{8,10},{9,17},{... | collective-permute-start | bytes 1400840 | tf_op jit(solution)/shard_map/ppermute | solution.py:143
  4.1 4.4 %collective-permute-start.1 = (bf16[96,2432]{1,0:T(8,128)(2,1)}, bf16[96,2432]{1,0:T(8,128)(2,1)}, u32[]{:S(2)}, u32[]{:S(2)}) collective-permute-start(bf16[96,2432]{1,0:T(8,128)(2,1)} %bitcast.14), channel_id=1, source_target_pairs={{0,4},{1,17},{2,6},{3,19},{4,0},{5,21},{6,2},{7,23},{8,12},{9,25},... | collective-permute-start | bytes 1400840 | tf_op jit(solution)/shard_map/ppermute | solution.py:143
  8.5 3.1 %collective-permute-start = (bf16[96,2432]{1,0:T(8,128)(2,1)}, bf16[96,2432]{1,0:T(8,128)(2,1)}, u32[]{:S(2)}, u32[]{:S(2)}) collective-permute-start(bf16[96,2432]{1,0:T(8,128)(2,1)} %bitcast.15), channel_id=1, source_target_pairs={{0,6},{1,25},{2,0},{3,27},{4,2},{5,29},{6,4},{7,31},{8,14},{9,1},{... | collective-permute-start | bytes 1400840 | tf_op jit(solution)/shard_map/ppermute | solution.py:143
  11.5 6.7 %all-gather = bf16[128,3072]{1,0:T(8,128)(2,1)S(1)} all-gather(bf16[64,3072]{1,0:T(8,128)(2,1)} %bitcast.17), channel_id=2, replica_groups={{0,1},{2,3},{4,5},{6,7},{8,9},{10,11},{12,13},{14,15},{16,17},{18,19},{..., dimensions={0}, use_global_device_ids=true | all-gather | bytes 1179648 | tf_op jit(solution)/shard_map/all_gather | solution.py:149
  18.2 0.0 copy-start.3
  18.2 1.0 %pack.1 = bf16[4,128,384]{2,1,0:T(8,128)(2,1)} custom-call(bf16[2,64,3072]{2,1,0:T(8,128)(2,1)S(1)} %bitcast.8), custom_call_target="tpu_custom_call" | custom-call | tf_op jit(solution)/shard_map/pack/pallas_call | solution.py:164
  19.2 3.9 %all-to-all-start = ((bf16[4,128,384]{2,1,0:T(8,128)(2,1)}), bf16[4,128,384]{2,1,0:T(8,128)(2,1)S(1)}, u32[]{:S(2)}, u32[]{:S(2)}) async-start(bf16[4,128,384]{2,1,0:T(8,128)(2,1)} %pack.1), calls=%async_computation | async-start | bytes 786432 | tf_op jit(solution)/shard_map/all_to_all | solution.py:146
  23.1 0.0 copy-done.2
  23.1 0.0 copy-done
  23.1 2.4 %prepare.1 = (s32[4,16]{1,0:T(4,128)S(1)}, s32[4]{0:T(128)S(1)}, bf16[4,128,128]{2,1,0:T(8,128)(2,1)S(1)}) custom-call(s32[16,4,16]{2,1,0:T(4,128)S(1)} %bitcast.12, bf16[16,1,4,128,128]{4,3,2,1,0:T(8,128)(2,1)S(1)} %copy-done), custom_call_target="tpu_custom_call" | custom-call | tf_op jit(solution)/shard_map/prepare/pallas_call | solution.py:175
  25.6 0.0 collective-permute-done.2.refs_3_
  25.6 0.0 collective-permute-done.1.refs_2_
  25.6 0.0 collective-permute-done.refs_1_
  25.6 0.0 copy-done.3
  25.6 1.5 %assemble.1.gath = bf16[384,2432]{1,0:T(8,128)(2,1)S(1)} custom-call(bf16[96,2432]{1,0:T(8,128)(2,1)S(1)} %bitcast.16, bf16[96,2432]{1,0:T(8,128)(2,1)} %collective-permute-done.refs_1_, bf16[96,2432]{1,0:T(8,128)(2,1)} %collective-permute-done.1.refs_2_, bf16[96,2432]{1,0:T(8,128)(2,1)} %collective-permute-done.2.refs_3_), custom_call_target="tpu_custom_call" | custom-call | flops 20000000000 | bytes 10000000 | tf_op jit(solution)/shard_map/assemble/pallas_call | solution.py:154
  27.1 2.6 %all-to-all-done.wall = bf16[4,128,384]{2,1,0:T(8,128)(2,1)S(1)} async-done(((bf16[4,128,384]{2,1,0:T(8,128)(2,1)}), bf16[4,128,384]{2,1,0:T(8,128)(2,1)S(1)}, u32[]{:S(2)}, u32[]{:S(2)}) %all-to-all-start) | async-done | bytes 393248 | tf_op jit(solution)/shard_map/all_to_all | solution.py:146
  29.7 1.9 %project.1 = bf16[4,16,128,128]{3,2,1,0:T(8,128)(2,1)S(1)} custom-call(s32[4,16]{1,0:T(4,128)S(1)} %get-tuple-element.11.idx_from, bf16[4,128,384]{2,1,0:T(8,128)(2,1)S(1)} %all-to-all-done.wall, bf16[384,2432]{1,0:T(8,128)(2,1)S(1)} %assemble.1.gath), custom_call_target="tpu_custom_call" | custom-call | tf_op jit(solution)/shard_map/project/pallas_call | solution.py:189
  31.6 18.0 %all_to_all.20.part = bf16[4,16,128,128]{3,2,1,0:T(8,128)(2,1)S(1)} all-to-all(bf16[4,16,128,128]{3,2,1,0:T(8,128)(2,1)S(1)} %project.1), channel_id=1, replica_groups={{0,8,16,24},{2,10,18,26},{4,12,20,28},{6,14,22,30},{1,3,5,7},{9,11,13,1..., dimensions={0} | all-to-all | bytes 4194304 | tf_op jit(solution)/shard_map/all_to_all | solution.py:146
  49.6 0.2 fold.1
  49.8 3.6 %all-gather.1 = bf16[32,64,128]{2,1,0:T(8,128)(2,1)S(1)} all-gather(bf16[16,64,128]{2,1,0:T(8,128)(2,1)S(1)} %get-tuple-element.13), channel_id=3, replica_groups={{0,1},{2,3},{4,5},{6,7},{8,9},{10,11},{12,13},{14,15},{16,17},{18,19},{..., dimensions={0}, use_global_device_ids=true | all-gather | bytes 786432 | tf_op jit(solution)/shard_map/all_gather | solution.py:149
  53.4 0.0 copy-start.1
  53.5 26.9 %all_to_all.21.got = bf16[16,64,128]{2,1,0:T(8,128)(2,1)S(1)} all-to-all(bf16[16,64,128]{2,1,0:T(8,128)(2,1)S(1)} %merge.1), channel_id=1, replica_groups=mesh['frame'=16,'chan'=32] {'frame'}, dimensions={0} | all-to-all | bytes 524288 | tf_op jit(solution)/shard_map/all_to_all | solution.py:220
  80.4 0.8 attend.1
  81.2 9.9 %all_to_all.22 = bf16[16,64,128]{2,1,0:T(8,128)(2,1)S(1)} all-to-all(bf16[16,64,128]{2,1,0:T(8,128)(2,1)S(1)} %attend.1), channel_id=1, replica_groups={{0,2,4,6,8,10,12,14,16,18,20,22,24,26,28,30},{1,3,5,7,9,11,13,15,17,19,..., dimensions={0} | all-to-all | bytes 524288 | tf_op jit(solution)/shard_map/all_to_all | solution.py:146
  91.1 8.1 %all-gather.2 = bf16[32,64,128]{2,1,0:T(8,128)(2,1)S(1)} all-gather(bf16[16,64,128]{2,1,0:T(8,128)(2,1)S(1)} %all_to_all.22), channel_id=4, replica_groups={{0,1},{2,3},{4,5},{6,7},{8,9},{10,11},{12,13},{14,15},{16,17},{18,19},{..., dimensions={0}, use_global_device_ids=true | all-gather | bytes 786432 | tf_op jit(solution)/shard_map/all_gather | solution.py:149
  99.2 0.0 copy-done.1
  99.2 0.9 output.1
  (1 shorter events, 0.0 us)
Async XLA Ops:
  0.0 23.1 %copy-start.2 = (s32[16,16,4]{1,2,0:T(4,128)S(1)}, s32[16,16,4]{1,2,0:T(4,128)}, u32[]{:S(2)}) copy-start(s32[16,16,4]{1,2,0:T(4,128)} %param.9) | copy-start | bytes 12292
  0.0 23.1 %copy-start = (bf16[16,1,4,128,128]{4,3,2,1,0:T(8,128)(2,1)S(1)}, bf16[16,1,4,128,128]{4,3,2,1,0:T(8,128)(2,1)}, u32[]{:S(2)}) copy-start(bf16[16,1,4,128,128]{4,3,2,1,0:T(8,128)(2,1)} %maps.1) | copy-start | bytes 6291460
  0.0 25.6 %collective-permute-start.2 = (bf16[96,2432]{1,0:T(8,128)(2,1)}, bf16[96,2432]{1,0:T(8,128)(2,1)}, u32[]{:S(2)}, u32[]{:S(2)}) collective-permute-start(bf16[96,2432]{1,0:T(8,128)(2,1)} %bitcast.13), channel_id=1, source_target_pairs={{0,2},{1,9},{2,4},{3,11},{4,6},{5,13},{6,0},{7,15},{8,10},{9,17},{... | collective-permute-start | bytes 1400840 | tf_op jit(solution)/shard_map/ppermute | solution.py:143
  4.1 21.5 %collective-permute-start.1 = (bf16[96,2432]{1,0:T(8,128)(2,1)}, bf16[96,2432]{1,0:T(8,128)(2,1)}, u32[]{:S(2)}, u32[]{:S(2)}) collective-permute-start(bf16[96,2432]{1,0:T(8,128)(2,1)} %bitcast.14), channel_id=1, source_target_pairs={{0,4},{1,17},{2,6},{3,19},{4,0},{5,21},{6,2},{7,23},{8,12},{9,25},... | collective-permute-start | bytes 1400840 | tf_op jit(solution)/shard_map/ppermute | solution.py:143
  8.5 17.1 %collective-permute-start = (bf16[96,2432]{1,0:T(8,128)(2,1)}, bf16[96,2432]{1,0:T(8,128)(2,1)}, u32[]{:S(2)}, u32[]{:S(2)}) collective-permute-start(bf16[96,2432]{1,0:T(8,128)(2,1)} %bitcast.15), channel_id=1, source_target_pairs={{0,6},{1,25},{2,0},{3,27},{4,2},{5,29},{6,4},{7,31},{8,14},{9,1},{... | collective-permute-start | bytes 1400840 | tf_op jit(solution)/shard_map/ppermute | solution.py:143
  18.2 7.4 %copy-start.3 = (bf16[2432,96]{0,1:T(8,128)(2,1)S(1)}, bf16[2432,96]{0,1:T(8,128)(2,1)}, u32[]{:S(2)}) copy-start(bf16[2432,96]{0,1:T(8,128)(2,1)} %param.5) | copy-start | bytes 1400836
  19.2 10.4 %all-to-all-start = ((bf16[4,128,384]{2,1,0:T(8,128)(2,1)}), bf16[4,128,384]{2,1,0:T(8,128)(2,1)S(1)}, u32[]{:S(2)}, u32[]{:S(2)}) async-start(bf16[4,128,384]{2,1,0:T(8,128)(2,1)} %pack.1), calls=%async_computation | async-start | bytes 786432 | tf_op jit(solution)/shard_map/all_to_all | solution.py:146
  53.4 45.8 %copy-start.1 = (bf16[2048,96]{0,1:T(8,128)(2,1)S(1)}, bf16[2048,96]{0,1:T(8,128)(2,1)}, u32[]{:S(2)}) copy-start(bf16[2048,96]{0,1:T(8,128)(2,1)} %param.7) | copy-start | bytes 1179652
